TPU v7x, 32 devices: a whole 2x2x4 slice. The times are simulated.
32 devices in a mesh: dp: 2 (over y), ctx: 4 (over z), tensor: 4 (over x, core).
Axes of the slice: x: 2, y: 2, z: 4, core: 2. Of those that a mesh axis runs over, the one named last changes fastest.
Arguments:
- activations: bfloat16 [2, 512, 2048], P('dp', 'ctx'), may hold values from -6 to 6
- cotangent: bfloat16 [2, 512, 2048], P('dp', 'ctx'), may hold values from -6 to 6
- doc_ids: int32 [2, 512], P('dp'), may hold values from 0 to 3, as said below
- attn_gain: bfloat16 [2048], replicated, may hold values from 0.25 to 1.75
- query_weight: bfloat16 [2048, 2048], P(None, 'tensor'), may hold values from -0.125 to 0.125
- key_weight: bfloat16 [2048, 2048], P(None, 'tensor'), may hold values from -0.125 to 0.125
- value_weight: bfloat16 [2048, 2048], P(None, 'tensor'), may hold values from -0.125 to 0.125
- out_weight: bfloat16 [2048, 2048], P('tensor'), may hold values from -1.5 to 1.5
- mlp_gain: bfloat16 [2048], replicated, may hold values from 0.25 to 1.75
- gate_weight: bfloat16 [2048, 8192], P(None, 'tensor'), may hold values from -0.125 to 0.125
- up_weight: bfloat16 [2048, 8192], P(None, 'tensor'), may hold values from -0.125 to 0.125
- down_weight: bfloat16 [8192, 2048], P('tensor'), may hold values from -0.0625 to 0.0625
Outputs:
- layer_out: bfloat16 [2, 512, 2048], P('dp', 'ctx')
- input_grad: bfloat16 [2, 512, 2048], P('dp', 'ctx')
- attn_gain_grad: float32 [2048], P(('dp', 'ctx'))
- query_grad: float32 [2048, 2048], P(('dp', 'ctx'), 'tensor')
- key_grad: float32 [2048, 2048], P(('dp', 'ctx'), 'tensor')
- value_grad: float32 [2048, 2048], P(('dp', 'ctx'), 'tensor')
- out_grad: float32 [2048, 2048], P('tensor', ('dp', 'ctx'))
- mlp_gain_grad: float32 [2048], P(('dp', 'ctx'))
- gate_grad: float32 [2048, 8192], P(('dp', 'ctx'), 'tensor')
- up_grad: float32 [2048, 8192], P(('dp', 'ctx'), 'tensor')
- down_grad: float32 [8192, 2048], P('tensor', ('dp', 'ctx'))
- attn_mass: float32 [2, 512, 16], P('dp', 'ctx', 'tensor')
Inputs may be any that keep to these rules, and one draw needn't show every extreme that they name: `doc_ids`: in each sequence the numbers start at 0, never fall and rise by one at each of three places; document 1 begins within the first 128 tokens and ends within the last 128.
All inputs are finite; a program needn't handle non-finite values.
Results may differ from a plain program's by a relative error of at most 0.014.
Values may be sent and summed in bfloat16 or wider, within the bound.
No kernel may reach another device: no remote copies, remote signals or barrier semaphores. Data moves between devices by JAX's collectives and lax.ppermute only.
A program may use at most 256 MiB of HBM per device.

v0:
```python
import math

import jax
import jax.numpy as jnp
from jax import lax
from jax.sharding import PartitionSpec as P

HD = 128


epsilon = 1e-05


def rotate(values):
    half_width = values.shape[-1] // 2
    return jnp.concatenate([-values[..., half_width:], values[..., :half_width]], axis=-1)


def rotary(values, cosine_table, sine_table):
    return values * cosine_table + rotate(values) * sine_table


def rotary_back(grads_in, cosine_table, sine_table):
    return grads_in * cosine_table - rotate(grads_in * sine_table)


def rope_tables(first_row, row_count, head_width):
    half_width = head_width // 2
    frequency = 10000.0 ** (-jnp.arange(half_width, dtype=jnp.float32) * 2.0 / head_width)
    positions = (first_row + jnp.arange(row_count, dtype=jnp.int32)).astype(jnp.float32)
    angles = positions[:, None] * frequency[None, :]
    cosine_table = jnp.concatenate([jnp.cos(angles), jnp.cos(angles)], axis=1)
    sine_table = jnp.concatenate([jnp.sin(angles), jnp.sin(angles)], axis=1)
    return (cosine_table[:, None, :], sine_table[:, None, :])


def norm_forward(inputs, gain_vec):
    inv_root = lax.rsqrt(jnp.mean(inputs * inputs, axis=-1, keepdims=True) + epsilon)
    return (inputs * inv_root * gain_vec, inv_root)


def norm_back(upstream, inputs, inv_root, gain_vec):
    scaled = inputs * inv_root
    gain_grad = jnp.sum(upstream * scaled, axis=0)
    inner = upstream * gain_vec
    return (
        inv_root * (inner - scaled * jnp.mean(inner * scaled, axis=-1, keepdims=True)),
        gain_grad,
    )


def block_scores(query_block, key_head, spot_block, doc_block, doc_row, score_scale, bias_shift):
    scores = (
        jnp.einsum("qd,kd->qk", query_block, key_head, preferred_element_type=jnp.float32)
        * score_scale
        + bias_shift
    )
    key_spots = jnp.arange(doc_row.shape[0], dtype=jnp.int32)
    allowed = (
        (key_spots[None, :] <= spot_block[:, None]) & (doc_row[None, :] == doc_block[:, None])
    ).astype(jnp.float32)
    return (scores, allowed)


def attend_forward(
    query_head,
    key_head,
    value_head,
    spots,
    query_docs,
    doc_row,
    block_rows,
    score_scale,
    bias_shift,
):
    block_count = query_head.shape[0] // block_rows

    def step(unused_state, block_index):
        scores, allowed = block_scores(
            query_head, key_head, spots, query_docs, doc_row, score_scale, bias_shift
        )
        weights = jax.nn.sigmoid(scores) * allowed
        mixed_rows = jnp.dot(
            weights.astype(jnp.bfloat16), value_head, preferred_element_type=jnp.float32
        )
        return (unused_state, (mixed_rows, jnp.sum(weights, axis=-1)))

    unused_state, (mixed_rows, mass_rows) = lax.scan(
        step, None, jnp.arange(block_count, dtype=jnp.int32)
    )
    return (mixed_rows.reshape(-1, value_head.shape[1]), mass_rows.reshape(-1))


def attend_backward(
    query_head,
    key_head,
    value_head,
    grad_head,
    spots,
    query_docs,
    doc_row,
    block_rows,
    score_scale,
    bias_shift,
):
    block_count = query_head.shape[0] // block_rows

    def step(totals, block_index):
        key_total, value_total = totals
        scores, allowed = block_scores(
            query_head, key_head, spots, query_docs, doc_row, score_scale, bias_shift
        )
        sigmoid_rows = jax.nn.sigmoid(scores)
        weights = sigmoid_rows * allowed
        weight_back = jnp.einsum(
            "qd,kd->qk", grad_head, value_head, preferred_element_type=jnp.float32
        )
        score_back = (weight_back * sigmoid_rows * (1.0 - sigmoid_rows) * allowed).astype(
            jnp.bfloat16
        )
        query_back = jnp.dot(score_back, key_head, preferred_element_type=jnp.float32) * score_scale
        key_total = (
            key_total
            + jnp.einsum("qk,qd->kd", score_back, query_head, preferred_element_type=jnp.float32)
            * score_scale
        )
        value_total = value_total + jnp.einsum(
            "qk,qd->kd", weights.astype(jnp.bfloat16), grad_head, preferred_element_type=jnp.float32
        )
        return ((key_total, value_total), query_back)

    zero_rows = jnp.zeros((key_head.shape[0], key_head.shape[1]), jnp.float32)
    (key_total, value_total), query_back = lax.scan(
        step, (zero_rows, zero_rows), jnp.arange(block_count, dtype=jnp.int32)
    )
    return (query_back.reshape(-1, key_head.shape[1]), key_total, value_total)


def per_device(
    activations,
    cotangent,
    doc_ids,
    attn_gain,
    query_weight,
    key_weight,
    value_weight,
    out_weight,
    mlp_gain,
    gate_weight,
    up_weight,
    down_weight,
):
    row_count = activations.shape[1]
    heads_here = query_weight.shape[1] // HD
    full_length = row_count * lax.axis_size("ctx")
    first_row = lax.axis_index("ctx") * row_count
    block_rows = min(512, row_count)
    score_scale = HD ** (-0.5)
    bias_shift = -math.log(full_length)
    inputs = activations[0].astype(jnp.float32)
    cot_rows = cotangent[0]
    doc_row = doc_ids[0]
    spots = first_row + jnp.arange(row_count, dtype=jnp.int32)
    query_docs = lax.dynamic_slice_in_dim(doc_row, first_row, row_count, 0)
    cosine_table, sine_table = rope_tables(first_row, row_count, HD)
    gain_first = attn_gain.astype(jnp.float32)
    gain_second = mlp_gain.astype(jnp.float32)
    normed_first, root_first = norm_forward(inputs, gain_first)
    normed_first = normed_first.astype(jnp.bfloat16)
    query_proj = jnp.dot(normed_first, query_weight, preferred_element_type=jnp.float32)
    key_proj = jnp.dot(normed_first, key_weight, preferred_element_type=jnp.float32)
    value_proj = jnp.dot(normed_first, value_weight, preferred_element_type=jnp.float32)
    queries = rotary(
        query_proj.reshape(row_count, heads_here, HD), cosine_table, sine_table
    ).astype(jnp.bfloat16)
    key_rows = (
        rotary(key_proj.reshape(row_count, heads_here, HD), cosine_table, sine_table)
        .astype(jnp.bfloat16)
        .reshape(row_count, heads_here * HD)
    )
    value_rows = value_proj.astype(jnp.bfloat16)
    key_all, value_all = (
        lax.all_gather(key_rows, "ctx", axis=0, tiled=True),
        lax.all_gather(value_rows, "ctx", axis=0, tiled=True),
    )
    mixed_parts = []
    mass_parts = []
    for head in range(heads_here):
        mixed_rows, mass_rows = attend_forward(
            queries[:, head, :],
            key_all[:, head * HD : (head + 1) * HD],
            value_all[:, head * HD : (head + 1) * HD],
            spots,
            query_docs,
            doc_row,
            block_rows,
            score_scale,
            bias_shift,
        )
        mixed_parts.append(mixed_rows)
        mass_parts.append(mass_rows)
    attended = jnp.concatenate(mixed_parts, axis=1).astype(jnp.bfloat16)
    attn_mass = jnp.stack(mass_parts, axis=1)
    partial_branch = jnp.dot(attended, out_weight, preferred_element_type=jnp.float32)
    branch = lax.psum(partial_branch, "tensor")
    middle_share = inputs + branch
    normed_second, root_second = norm_forward(middle_share, gain_second)
    normed_second = normed_second.astype(jnp.bfloat16)
    gate_proj = jnp.dot(normed_second, gate_weight, preferred_element_type=jnp.float32)
    up_proj = jnp.dot(normed_second, up_weight, preferred_element_type=jnp.float32)
    gate_sig = jax.nn.sigmoid(gate_proj)
    activated = gate_proj * gate_sig
    hidden = (activated * up_proj).astype(jnp.bfloat16)
    mlp_out = lax.psum(jnp.dot(hidden, down_weight, preferred_element_type=jnp.float32), "tensor")
    down_wgrad = jnp.einsum("tf,td->fd", hidden, cot_rows, preferred_element_type=jnp.float32)
    hidden_back = jnp.einsum("td,fd->tf", cot_rows, down_weight, preferred_element_type=jnp.float32)
    gate_back = (hidden_back * up_proj * gate_sig * (1.0 + gate_proj * (1.0 - gate_sig))).astype(
        jnp.bfloat16
    )
    up_back = (hidden_back * activated).astype(jnp.bfloat16)
    gate_wgrad = jnp.einsum(
        "td,tf->df", normed_second, gate_back, preferred_element_type=jnp.float32
    )
    up_wgrad = jnp.einsum("td,tf->df", normed_second, up_back, preferred_element_type=jnp.float32)
    second_part = jnp.einsum(
        "tf,df->td", gate_back, gate_weight, preferred_element_type=jnp.float32
    ) + jnp.einsum("tf,df->td", up_back, up_weight, preferred_element_type=jnp.float32)
    second_back = lax.psum(second_part, "tensor")
    middle_part, gain_second_grad = norm_back(second_back, middle_share, root_second, gain_second)
    middle_back = cot_rows.astype(jnp.float32) + middle_part
    layer_out = (middle_share + mlp_out).astype(jnp.bfloat16)
    branch_back = middle_back.astype(jnp.bfloat16)
    out_wgrad = jnp.einsum("tc,td->cd", attended, branch_back, preferred_element_type=jnp.float32)
    attended_back = jnp.einsum(
        "td,cd->tc", branch_back, out_weight, preferred_element_type=jnp.float32
    ).astype(jnp.bfloat16)
    query_parts = []
    key_parts = []
    value_parts = []
    for head in range(heads_here):
        query_back, key_total, value_total = attend_backward(
            queries[:, head, :],
            key_all[:, head * HD : (head + 1) * HD],
            value_all[:, head * HD : (head + 1) * HD],
            attended_back[:, head * HD : (head + 1) * HD],
            spots,
            query_docs,
            doc_row,
            block_rows,
            score_scale,
            bias_shift,
        )
        query_parts.append(query_back)
        key_parts.append(key_total)
        value_parts.append(value_total)
    query_back_rows = (
        rotary_back(jnp.stack(query_parts, axis=1), cosine_table, sine_table)
        .reshape(row_count, heads_here * HD)
        .astype(jnp.bfloat16)
    )
    key_mine, value_mine = (
        lax.psum_scatter(
            jnp.concatenate(key_parts, axis=1), "ctx", scatter_dimension=0, tiled=True
        ),
        lax.psum_scatter(
            jnp.concatenate(value_parts, axis=1), "ctx", scatter_dimension=0, tiled=True
        ),
    )
    key_back_rows = (
        rotary_back(key_mine.reshape(row_count, heads_here, HD), cosine_table, sine_table)
        .reshape(row_count, heads_here * HD)
        .astype(jnp.bfloat16)
    )
    value_back_rows = value_mine.astype(jnp.bfloat16)
    query_wgrad = jnp.einsum(
        "td,tc->dc", normed_first, query_back_rows, preferred_element_type=jnp.float32
    )
    key_wgrad = jnp.einsum(
        "td,tc->dc", normed_first, key_back_rows, preferred_element_type=jnp.float32
    )
    value_wgrad = jnp.einsum(
        "td,tc->dc", normed_first, value_back_rows, preferred_element_type=jnp.float32
    )
    first_part = jnp.einsum(
        "tc,dc->td", query_back_rows, query_weight, preferred_element_type=jnp.float32
    )
    first_part = first_part + jnp.einsum(
        "tc,dc->td", key_back_rows, key_weight, preferred_element_type=jnp.float32
    )
    first_part = first_part + jnp.einsum(
        "tc,dc->td", value_back_rows, value_weight, preferred_element_type=jnp.float32
    )
    first_back = lax.psum(first_part, "tensor")
    input_part, gain_first_grad = norm_back(first_back, inputs, root_first, gain_first)
    input_grad = (middle_back + input_part).astype(jnp.bfloat16)
    summed = (
        lax.psum_scatter(gain_first_grad, ("dp", "ctx"), scatter_dimension=0, tiled=True),
        lax.psum_scatter(query_wgrad, ("dp", "ctx"), scatter_dimension=0, tiled=True),
        lax.psum_scatter(key_wgrad, ("dp", "ctx"), scatter_dimension=0, tiled=True),
        lax.psum_scatter(value_wgrad, ("dp", "ctx"), scatter_dimension=0, tiled=True),
        lax.psum_scatter(out_wgrad, ("dp", "ctx"), scatter_dimension=1, tiled=True),
        lax.psum_scatter(gain_second_grad, ("dp", "ctx"), scatter_dimension=0, tiled=True),
        lax.psum_scatter(gate_wgrad, ("dp", "ctx"), scatter_dimension=0, tiled=True),
        lax.psum_scatter(up_wgrad, ("dp", "ctx"), scatter_dimension=0, tiled=True),
        lax.psum_scatter(down_wgrad, ("dp", "ctx"), scatter_dimension=1, tiled=True),
    )
    return (
        layer_out[None],
        input_grad[None],
        summed[0],
        summed[1],
        summed[2],
        summed[3],
        summed[4],
        summed[5],
        summed[6],
        summed[7],
        summed[8],
        attn_mass[None],
    )


def solution(mesh):
    return jax.shard_map(
        per_device,
        mesh=mesh,
        in_specs=(
            P("dp", "ctx", None),
            P("dp", "ctx", None),
            P("dp", None),
            P(),
            P(None, "tensor"),
            P(None, "tensor"),
            P(None, "tensor"),
            P("tensor", None),
            P(),
            P(None, "tensor"),
            P(None, "tensor"),
            P("tensor", None),
        ),
        out_specs=(
            P("dp", "ctx", None),
            P("dp", "ctx", None),
            P(("dp", "ctx")),
            P(("dp", "ctx"), "tensor"),
            P(("dp", "ctx"), "tensor"),
            P(("dp", "ctx"), "tensor"),
            P("tensor", ("dp", "ctx")),
            P(("dp", "ctx")),
            P(("dp", "ctx"), "tensor"),
            P(("dp", "ctx"), "tensor"),
            P("tensor", ("dp", "ctx")),
            P("dp", "ctx", "tensor"),
        ),
        check_vma=False,
    )
```

profile of v0, /device:TPU:0, one launch (start us, length us, event | category | flops | bytes accessed | tf_op | source)
XLA Modules:
  0.0 1523.2 jit_solution(5354512274264811788)
XLA Ops:
  10.0 4.0 copy.29
  14.0 3.9 copy.28
  22.8 16.8 %all_gather.6 = bf16[512,512]{0,1:T(8,128)(2,1)S(1)} all-gather(bf16[128,512]{0,1:T(8,128)(2,1)S(1)} %bitcast.164), channel_id=1, replica_groups=mesh['dp'=2,'ctx'=4,'tensor'=4] {'ctx'}, dimensions={0}, use_global_device_ids=true | all-gather | bytes 655360 | tf_op jit(solution)/shard_map/all_gather | solution.py:183
  44.6 16.5 %all_gather.7 = bf16[512,512]{1,0:T(8,128)(2,1)} all-gather(bf16[128,512]{1,0:T(8,128)(2,1)S(1)} %convolution_convert_fusion.1), channel_id=1, replica_groups=mesh['dp'=2,'ctx'=4,'tensor'=4] {'ctx'}, dimensions={0}, use_global_device_ids=true | all-gather | bytes 655360 | tf_op jit(solution)/shard_map/all_gather | solution.py:184
  71.4 36.0 %all-reduce.8.cloned.1.call-done = f32[128,2048]{1,0:T(8,128)} async-done(((f32[128,2048]{1,0:T(8,128)}), f32[128,2048]{1,0:T(8,128)}) %all-reduce.8.cloned.1.call-update) | async-done | bytes 1048592 | tf_op jit(solution)/shard_map/psum | solution.py:205
  110.1 4.8 fusion.138
  117.1 7.4 multiply_convert_fusion
  124.5 2.9 fusion.140
  127.4 3.9 convolution_add_fusion.2
  131.4 36.6 %all-reduce.10.cloned.1.call-done = f32[128,2048]{1,0:T(8,128)} async-done(((f32[128,2048]{1,0:T(8,128)}), f32[128,2048]{1,0:T(8,128)}) %all-reduce.10.cloned.1.call-update) | async-done | bytes 1048592 | tf_op jit(solution)/shard_map/psum | solution.py:228
  167.9 2.5 multiply_reduce_fusion
  179.1 5.7 fusion.139
  191.8 14.6 reduce-scatter.10.cloned.1.call-done
  211.1 23.9 %reduce-scatter.12.cloned.1.call-done = f32[128,512]{0,1:T(8,128)} async-done(((f32[512,512]{0,1:T(8,128)}), f32[128,512]{0,1:T(8,128)}) %reduce-scatter.12.cloned.1.call-update) | async-done | bytes 262160 | tf_op jit(solution)/shard_map/reduce_scatter | solution.py:265
  235.1 3.5 convolution_add_fusion
  238.7 2.7 fusion.74
  241.5 2.8 fusion.94
  244.4 2.8 fusion.125
  247.3 2.8 fusion.64
  250.2 8.1 fusion.56
  259.4 8.1 fusion.143
  268.6 8.1 fusion.142
  279.3 9.7 all-reduce.12.cloned.1.call-done
  290.6 38.8 %all-reduce.2 = (f32[2048]{0:T(1024)S(1)}, f32[2048]{0:T(1024)S(1)}) all-reduce(f32[2048]{0:T(1024)S(1)} %get-tuple-element.188, f32[2048]{0:T(1024)S(1)} %copy-done.44), channel_id=4, replica_groups=mesh['dp'=2,'ctx'=4,'tensor'=4] {'dp','ctx'}, use_global_device_ids=true, to_apply=%region_11.12.clone | all-reduce | flops 4096 | bytes 32768
  333.2 2.7 fusion.55
  335.9 47.0 %reduce-scatter.20.cloned.1.call-done = f32[512,256]{1,0:T(8,128)} async-done(((f32[512,2048]{1,0:T(8,128)}), f32[512,256]{1,0:T(8,128)}) %reduce-scatter.20.cloned.1.call-update) | async-done | bytes 524304 | tf_op jit(solution)/shard_map/reduce_scatter | solution.py:301
  382.8 91.9 %reduce-scatter.18.cloned.1.call-done = f32[256,512]{1,0:T(8,128)} async-done(((f32[2048,512]{1,0:T(8,128)}), f32[256,512]{1,0:T(8,128)}) %reduce-scatter.18.cloned.1.call-update) | async-done | bytes 524304 | tf_op jit(solution)/shard_map/reduce_scatter | solution.py:300
  474.7 92.3 %reduce-scatter.16.cloned.1.call-done = f32[256,512]{1,0:T(8,128)} async-done(((f32[2048,512]{1,0:T(8,128)}), f32[256,512]{1,0:T(8,128)}) %reduce-scatter.16.cloned.1.call-update) | async-done | bytes 524304 | tf_op jit(solution)/shard_map/reduce_scatter | solution.py:299
  567.0 91.9 %reduce-scatter.14.cloned.1.call-done = f32[256,512]{1,0:T(8,128)} async-done(((f32[2048,512]{1,0:T(8,128)}), f32[256,512]{1,0:T(8,128)}) %reduce-scatter.14.cloned.1.call-update) | async-done | bytes 524304 | tf_op jit(solution)/shard_map/reduce_scatter | solution.py:298
  658.9 286.5 %reduce-scatter.26.cloned.1.call-done = f32[2048,256]{1,0:T(8,128)} async-done(((f32[2048,2048]{1,0:T(8,128)}), f32[2048,256]{1,0:T(8,128)}) %reduce-scatter.26.cloned.1.call-update) | async-done | bytes 2097168 | tf_op jit(solution)/shard_map/reduce_scatter | solution.py:305
  945.4 285.3 %reduce-scatter.24.cloned.1.call-done = f32[256,2048]{1,0:T(8,128)} async-done(((f32[2048,2048]{1,0:T(8,128)}), f32[256,2048]{1,0:T(8,128)}) %reduce-scatter.24.cloned.1.call-update) | async-done | bytes 2097168 | tf_op jit(solution)/shard_map/reduce_scatter | solution.py:304
  1230.7 285.7 %reduce-scatter.22.cloned.1.call-done = f32[256,2048]{1,0:T(8,128)} async-done(((f32[2048,2048]{1,0:T(8,128)}), f32[256,2048]{1,0:T(8,128)}) %reduce-scatter.22.cloned.1.call-update) | async-done | bytes 2097168 | tf_op jit(solution)/shard_map/reduce_scatter | solution.py:303
  (213 shorter events, 57.0 us)
Async XLA Ops:
  7.2 61.9 %copy-start = (bf16[512,2048]{1,0:T(8,128)(2,1)S(1)}, bf16[512,2048]{1,0:T(8,128)(2,1)}, u32[]{:S(2)}) copy-start(bf16[512,2048]{1,0:T(8,128)(2,1)} %param.19) | copy-start | bytes 6291460
  7.2 100.2 %all-reduce.8.cloned.1.call-start = ((), (), s32[]{:S(2)}) async-start(), calls=%async_computation.9 | async-start | bytes 2097152 | tf_op jit(solution)/shard_map/psum | solution.py:205
  22.8 42.2 %copy-start.25 = (bf16[128,4,128]{0,2,1:T(8,128)(2,1)}, bf16[128,4,128]{0,2,1:T(8,128)(2,1)S(1)}, u32[]{:S(2)}) copy-start(bf16[128,4,128]{0,2,1:T(8,128)(2,1)S(1)} %get-tuple-element.236) | copy-start | bytes 393220
  22.8 38.3 %copy-start.43 = (s32[1,512]{1,0:T(1,128)S(1)}, s32[1,512]{1,0:T(1,128)}, u32[]{:S(2)}) copy-start(s32[1,512]{1,0:T(1,128)} %param.14) | copy-start | bytes 6148
  39.6 25.4 %copy-start.12 = (bf16[512,512]{0,1:T(8,128)(2,1)}, bf16[512,512]{0,1:T(8,128)(2,1)S(1)}, u32[]{:S(2)}) copy-start(bf16[512,512]{0,1:T(8,128)(2,1)S(1)} %all_gather.6) | copy-start | bytes 1572868
  62.4 46.5 %copy-start.35 = (bf16[128,128]{0,1:T(8,128)(2,1)}, bf16[128,128]{0,1:T(8,128)(2,1)S(1)}, u32[]{:S(2)}) copy-start(bf16[128,128]{0,1:T(8,128)(2,1)S(1)} %convolution_convert_fusion.2) | copy-start | bytes 98308
  63.7 45.2 %copy-start.37 = (bf16[128,128]{0,1:T(8,128)(2,1)}, bf16[128,128]{0,1:T(8,128)(2,1)S(1)}, u32[]{:S(2)}) copy-start(bf16[128,128]{0,1:T(8,128)(2,1)S(1)} %convolution_convert_fusion.3) | copy-start | bytes 98308
  65.0 43.9 %copy-start.39 = (bf16[128,128]{0,1:T(8,128)(2,1)}, bf16[128,128]{0,1:T(8,128)(2,1)S(1)}, u32[]{:S(2)}) copy-start(bf16[128,128]{0,1:T(8,128)(2,1)S(1)} %convolution_convert_fusion.4) | copy-start | bytes 98308
  69.0 41.0 %copy-start.41 = (bf16[128,128]{0,1:T(8,128)(2,1)}, bf16[128,128]{0,1:T(8,128)(2,1)S(1)}, u32[]{:S(2)}) copy-start(bf16[128,128]{0,1:T(8,128)(2,1)S(1)} %convolution_convert_fusion.5) | copy-start | bytes 98308
  70.5 97.4 %all-reduce.10.cloned.1.call-start = ((), (), s32[]{:S(2)}) async-start(), calls=%async_computation.10 | async-start | bytes 2097152 | tf_op jit(solution)/shard_map/psum | solution.py:228
  115.8 11.6 slice-start.2
  117.1 10.3 slice-start.3
  131.3 43.1 %copy-start.45 = (s32[128]{0:T(128)S(1)}, s32[128]{0:T(128)}, u32[]{:S(2)}) copy-start(s32[128]{0:T(128)} %iota_add_fusion) | copy-start | bytes 1540
  131.3 43.1 %copy-start.49 = (s32[128]{0:T(128)S(1)}, s32[128]{0:T(128)}, u32[]{:S(2)}) copy-start(s32[128]{0:T(128)} %copy-done.48) | copy-start | bytes 1540
  131.3 75.1 %reduce-scatter.10.cloned.1.call-start = ((), (), s32[]{:S(2)}) async-start(), calls=%async_computation.11 | async-start | bytes 1310720 | tf_op jit(solution)/shard_map/reduce_scatter | solution.py:262
  178.7 56.3 %reduce-scatter.12.cloned.1.call-start = ((), (), s32[]{:S(2)}) async-start(), calls=%async_computation.12 | async-start | bytes 1310720 | tf_op jit(solution)/shard_map/reduce_scatter | solution.py:265
  187.0 22.4 %copy-start.6 = (bf16[2048,512]{1,0:T(8,128)(2,1)S(1)}, bf16[2048,512]{1,0:T(8,128)(2,1)}, u32[]{:S(2)}) copy-start(bf16[2048,512]{1,0:T(8,128)(2,1)} %param.16) | copy-start | bytes 6291460
  187.0 102.0 %all-reduce.12.cloned.1.call-start = ((), (), s32[]{:S(2)}) async-start(), calls=%async_computation.20 | async-start | bytes 4194304 | tf_op jit(solution)/shard_map/psum | solution.py:214
  211.1 27.6 %copy-start.5 = (f32[128,2048]{1,0:T(8,128)S(1)}, f32[128,2048]{1,0:T(8,128)}, u32[]{:S(2)}) copy-start(f32[128,2048]{1,0:T(8,128)} %copy-done.4) | copy-start | bytes 3145732
  211.1 27.6 %copy-start.36 = (bf16[128,128]{0,1:T(8,128)(2,1)S(1)}, bf16[128,128]{0,1:T(8,128)(2,1)}, u32[]{:S(2)}) copy-start(bf16[128,128]{0,1:T(8,128)(2,1)} %copy-done.35) | copy-start | bytes 98308
  211.1 27.6 %copy-start.38 = (bf16[128,128]{0,1:T(8,128)(2,1)S(1)}, bf16[128,128]{0,1:T(8,128)(2,1)}, u32[]{:S(2)}) copy-start(bf16[128,128]{0,1:T(8,128)(2,1)} %copy-done.37) | copy-start | bytes 98308
  211.1 27.6 %copy-start.40 = (bf16[128,128]{0,1:T(8,128)(2,1)S(1)}, bf16[128,128]{0,1:T(8,128)(2,1)}, u32[]{:S(2)}) copy-start(bf16[128,128]{0,1:T(8,128)(2,1)} %copy-done.39) | copy-start | bytes 98308
  211.1 27.6 %copy-start.42 = (bf16[128,128]{0,1:T(8,128)(2,1)S(1)}, bf16[128,128]{0,1:T(8,128)(2,1)}, u32[]{:S(2)}) copy-start(bf16[128,128]{0,1:T(8,128)(2,1)} %copy-done.41) | copy-start | bytes 98308
  238.6 144.2 %reduce-scatter.20.cloned.1.call-start = ((), (), s32[]{:S(2)}) async-start(), calls=%async_computation.16 | async-start | bytes 4718592 | tf_op jit(solution)/shard_map/reduce_scatter | solution.py:301
  241.5 233.2 %reduce-scatter.18.cloned.1.call-start = ((), (), s32[]{:S(2)}) async-start(), calls=%async_computation.15 | async-start | bytes 4718592 | tf_op jit(solution)/shard_map/reduce_scatter | solution.py:300
  244.4 322.7 %reduce-scatter.16.cloned.1.call-start = ((), (), s32[]{:S(2)}) async-start(), calls=%async_computation.14 | async-start | bytes 4718592 | tf_op jit(solution)/shard_map/reduce_scatter | solution.py:299
  247.2 411.7 %reduce-scatter.14.cloned.1.call-start = ((), (), s32[]{:S(2)}) async-start(), calls=%async_computation.13 | async-start | bytes 4718592 | tf_op jit(solution)/shard_map/reduce_scatter | solution.py:298
  250.2 695.2 %reduce-scatter.26.cloned.1.call-start = ((), (), s32[]{:S(2)}) async-start(), calls=%async_computation.19 | async-start | bytes 18874368 | tf_op jit(solution)/shard_map/reduce_scatter | solution.py:305
  258.4 972.3 %reduce-scatter.24.cloned.1.call-start = ((), (), s32[]{:S(2)}) async-start(), calls=%async_computation.18 | async-start | bytes 18874368 | tf_op jit(solution)/shard_map/reduce_scatter | solution.py:304
  267.6 1248.8 %reduce-scatter.22.cloned.1.call-start = ((), (), s32[]{:S(2)}) async-start(), calls=%async_computation.17 | async-start | bytes 18874368 | tf_op jit(solution)/shard_map/reduce_scatter | solution.py:303
  276.8 13.8 copy-start.44
  276.8 1239.6 %copy-start.1 = (bf16[512,2048]{1,0:T(8,128)(2,1)S(1)}, bf16[512,2048]{1,0:T(8,128)(2,1)}, u32[]{:S(2)}) copy-start(bf16[512,2048]{1,0:T(8,128)(2,1)} %param.19) | copy-start | bytes 6291460
  (41 other events, 163.8 us)
Sparse Core Ops, SparseCore 0:
  70.6 36.7 all-reduce.7
  131.4 36.4 all-reduce.9
  178.8 27.5 reduce-scatter.9
  209.2 25.7 reduce-scatter.11
  238.7 50.2 all-reduce.11
  293.5 89.2 reduce-scatter.19
  387.0 87.6 reduce-scatter.17
  479.3 87.6 reduce-scatter.15
  571.2 87.6 reduce-scatter.13
  663.6 281.7 reduce-scatter.25
  949.7 280.9 reduce-scatter.23
  1235.4 280.9 reduce-scatter.21
where the time goes:
time: 1520 us
  waiting for transfers between devices  1300 us (86%)
  matrix products  94.1 us (6%)
  blocking collectives  72.2 us (5%)
  other arithmetic  22.1 us (1%)
  local copies, waits for them, and re-layouts  16.3 us (1%)
  between operations  15.9 us (1%)
    reduce_scatter x1, waiting for transfers between devices, per_device(): lax.psum_scatter(down_wgrad, ('dp', 'ctx'), scatter_dimension=1, tiled=True)  286 us
    reduce_scatter x1, waiting for transfers between devices, per_device(): lax.psum_scatter(gate_wgrad, ('dp', 'ctx'), scatter_dimension=0, tiled=True)  286 us
    reduce_scatter x1, waiting for transfers between devices, per_device(): lax.psum_scatter(up_wgrad, ('dp', 'ctx'), scatter_dimension=0, tiled=True)  285 us
    reduce_scatter x1, waiting for transfers between devices, per_device(): lax.psum_scatter(key_wgrad, ('dp', 'ctx'), scatter_dimension=0, tiled=True)  92.3 us
    reduce_scatter x1, waiting for transfers between devices, per_device(): lax.psum_scatter(query_wgrad, ('dp', 'ctx'), scatter_dimension=0, tiled=T...  91.9 us
    reduce_scatter x1, waiting for transfers between devices, per_device(): lax.psum_scatter(value_wgrad, ('dp', 'ctx'), scatter_dimension=0, tiled=T...  91.9 us
    reduce_scatter x1, waiting for transfers between devices, per_device(): lax.psum_scatter(out_wgrad, ('dp', 'ctx'), scatter_dimension=1, tiled=True)  47 us
    unnamed x1, blocking collectives  38.8 us
  transfers between devices with their start and end apart: 12, of which 12 were waited for; matrix products, arithmetic and copies ran while one was open for 4% of the time, Pallas kernels for 0%

commit v1 on v0

v1 whole, which is shorter than its diff:
```python
import functools
import math

import jax
import jax.numpy as jnp
from jax import lax
from jax.experimental import pallas as pl
from jax.experimental.pallas import tpu as pltpu
from jax.sharding import PartitionSpec as P

HD = 128
EPS = 1e-05
BF = jnp.bfloat16
F32 = jnp.float32
VMEM_LIMIT = 56 * 1024 * 1024


def swap(values, axis, distance):
    count = lax.axis_size(axis)
    return lax.ppermute(values, axis, [(i, i ^ distance) for i in range(count)])


def turn(values, axis, shift):
    count = lax.axis_size(axis)
    return lax.ppermute(values, axis, [(i, (i + shift) % count) for i in range(count)])


def bits_of(count):
    return [1 << i for i in range(count.bit_length() - 1)]


def slot_order(count):
    order = [0]
    for bit in reversed(bits_of(count)):
        order = order + [slot ^ bit for slot in order]
    return order


def gather_tensor(rows):
    for bit in reversed(bits_of(lax.axis_size("tensor"))):
        rows = jnp.concatenate([rows, swap(rows, "tensor", bit)], axis=0)
    return rows


def scatter_tensor(rows):
    for bit in bits_of(lax.axis_size("tensor")):
        half = rows.shape[0] // 2
        got = swap(rows[half:].astype(BF), "tensor", bit)
        rows = rows[:half].astype(F32) + got.astype(F32)
    return rows


def gather_tokens(rows):
    return jnp.concatenate(
        [rows] + [turn(rows, "ctx", k) for k in range(1, lax.axis_size("ctx"))], axis=0
    )


def gather_dp(rows):
    return jnp.concatenate(
        [rows] + [turn(rows, "dp", k) for k in range(1, lax.axis_size("dp"))], axis=0
    )


def from_slots(blocks, slots, place):
    size = blocks.shape[0] // len(slots)
    out = jnp.zeros_like(blocks)
    for index, slot in enumerate(slots):
        out = lax.dynamic_update_slice_in_dim(
            out, blocks[index * size : (index + 1) * size], (place ^ slot) * size, 0
        )
    return out


def rope_rows(u, cos, sin):
    return u * cos + pltpu.roll(u, HD // 2, 1) * sin


def rope_back_rows(u, cos, sin):
    return u * cos - pltpu.roll(u, HD // 2, 1) * sin


def dot(a, b):
    return lax.dot_general(a, b, (((1,), (0,)), ((), ())), preferred_element_type=F32)


def dot_nt(a, b):
    return lax.dot_general(a, b, (((1,), (1,)), ((), ())), preferred_element_type=F32)


def dot_tn(a, b):
    return lax.dot_general(a, b, (((0,), (0,)), ((), ())), preferred_element_type=F32)


def own_rows(values, chunk, ring):
    step = chunk * ring
    return jnp.concatenate(
        [values[i * step : i * step + chunk] for i in range(values.shape[0] // step)], axis=0
    )


def attend_kernel(
    chunk, ring, scale, shift,
    x_ref, wq_ref, wk_ref, wv_ref, cos_ref, sin_ref, ok_ref,
    q_ref, k_ref, v_ref, att_ref, mass_ref,
):
    rows = x_ref[...]
    cos, sin, ok = cos_ref[...], sin_ref[...], ok_ref[...]
    q_all = dot(rows, wq_ref[...])
    k_all = dot(rows, wk_ref[...])
    v_all = dot(rows, wv_ref[...]).astype(BF)
    v_ref[...] = v_all
    for j in range(q_all.shape[1] // HD):
        cols = slice(j * HD, (j + 1) * HD)
        q = rope_rows(q_all[:, cols], cos, sin).astype(BF)
        k = rope_rows(k_all[:, cols], cos, sin).astype(BF)
        q_ref[:, cols] = q
        k_ref[:, cols] = k
        scores = dot_nt(own_rows(q, chunk, ring), k) * scale + shift
        weights = jax.nn.sigmoid(scores) * ok
        mass_ref[j] = jnp.sum(weights, axis=-1, keepdims=True)
        att_ref[:, cols] = dot(weights.astype(BF), v_all[:, cols]).astype(BF)


def attend(x_seq, wq, wk, wv, cos, sin, ok_own, chunk, ring, scale, shift):
    seq, width = x_seq.shape
    cols = wq.shape[1]
    heads = cols // HD
    step = min(2, heads)
    own = ok_own.shape[0]
    whole = lambda *shape: pl.BlockSpec(shape, lambda i: (0,) * len(shape))
    wspec = pl.BlockSpec((width, step * HD), lambda i: (0, i))
    sspec = pl.BlockSpec((seq, step * HD), lambda i: (0, i))
    return pl.pallas_call(
        functools.partial(attend_kernel, chunk, ring, scale, shift),
        grid=(heads // step,),
        in_specs=[whole(seq, width), wspec, wspec, wspec, whole(seq, HD), whole(seq, HD),
                  whole(own, seq)],
        out_specs=[sspec, sspec, sspec,
                   pl.BlockSpec((own, step * HD), lambda i: (0, i)),
                   pl.BlockSpec((step, own, 1), lambda i: (i, 0, 0))],
        out_shape=[jax.ShapeDtypeStruct((seq, cols), BF)] * 3
        + [jax.ShapeDtypeStruct((own, cols), BF), jax.ShapeDtypeStruct((heads, own, 1), F32)],
        compiler_params=pltpu.CompilerParams(vmem_limit_bytes=VMEM_LIMIT),
        cost_estimate=pl.CostEstimate(
            flops=2 * seq * width * cols * 3, bytes_accessed=6 * width * cols, transcendentals=0
        ),
    )(x_seq, wq, wk, wv, cos, sin, ok_own)


def attend_back_kernel(
    chunk, ring, scale, shift,
    bb_ref, wo_ref, q_ref, k_ref, v_ref, cos_ref, sin_ref, ok_ref,
    qb_ref, kb_ref, vb_ref, att_ref, qo_ref, ko_ref, vo_ref,
):
    cos, sin, ok = cos_ref[...], sin_ref[...], ok_ref[...]
    ab_all = dot_nt(bb_ref[...], wo_ref[...]).astype(BF)
    for j in range(ab_all.shape[1] // HD):
        cols = slice(j * HD, (j + 1) * HD)
        q, k, v, ab = q_ref[:, cols], k_ref[:, cols], v_ref[:, cols], ab_all[:, cols]
        sig = jax.nn.sigmoid(dot_nt(q, k) * scale + shift)
        weights = (sig * ok).astype(BF)
        att_ref[:, cols] = dot(weights, v).astype(BF)
        back = (dot_nt(ab, v) * sig * (1.0 - sig) * ok).astype(BF)
        qb = rope_back_rows(dot(back, k) * scale, cos, sin).astype(BF)
        kb = rope_back_rows(dot_tn(back, q) * scale, cos, sin).astype(BF)
        vb = dot_tn(weights, ab).astype(BF)
        qb_ref[:, cols] = qb
        kb_ref[:, cols] = kb
        vb_ref[:, cols] = vb
        qo_ref[:, cols] = own_rows(qb, chunk, ring)
        ko_ref[:, cols] = own_rows(kb, chunk, ring)
        vo_ref[:, cols] = own_rows(vb, chunk, ring)


def attend_back(bb_seq, wo, q, k, v, cos, sin, ok, chunk, ring, scale, shift):
    seq, width = bb_seq.shape
    cols = wo.shape[0]
    heads = cols // HD
    step = min(2, heads)
    own = seq // ring
    whole = lambda *shape: pl.BlockSpec(shape, lambda i: (0,) * len(shape))
    sspec = pl.BlockSpec((seq, step * HD), lambda i: (0, i))
    ospec = pl.BlockSpec((own, step * HD), lambda i: (0, i))
    return pl.pallas_call(
        functools.partial(attend_back_kernel, chunk, ring, scale, shift),
        grid=(heads // step,),
        in_specs=[whole(seq, width), pl.BlockSpec((step * HD, width), lambda i: (i, 0)),
                  sspec, sspec, sspec, whole(seq, HD), whole(seq, HD), whole(seq, seq)],
        out_specs=[sspec] * 4 + [ospec] * 3,
        out_shape=[jax.ShapeDtypeStruct((seq, cols), BF)] * 4
        + [jax.ShapeDtypeStruct((own, cols), BF)] * 3,
        compiler_params=pltpu.CompilerParams(vmem_limit_bytes=VMEM_LIMIT),
        cost_estimate=pl.CostEstimate(
            flops=2 * seq * width * cols + 14 * seq * seq * cols,
            bytes_accessed=2 * (seq + cols) * width + 20 * seq * cols,
            transcendentals=seq * seq * heads,
        ),
    )(bb_seq, wo, q, k, v, cos, sin, ok)


def gate_math(gate, up, hidden_back):
    sig = jax.nn.sigmoid(gate)
    act = gate * sig
    hidden = (act * up).astype(BF)
    gate_back = (hidden_back * up * sig * (1.0 + gate * (1.0 - sig))).astype(BF)
    up_back = (hidden_back * act).astype(BF)
    return hidden, gate_back, up_back


def mlp_kernel(x_ref, cot_ref, wg_ref, wu_ref, wd_ref, back_ref, out_ref, back_acc, out_acc):
    step = pl.program_id(0)
    x, cot = x_ref[...], cot_ref[...]
    wg, wu, wd = wg_ref[...], wu_ref[...], wd_ref[...]
    hidden, gate_back, up_back = gate_math(dot(x, wg), dot(x, wu), dot_nt(cot, wd))
    back = dot_nt(gate_back, wg) + dot_nt(up_back, wu)
    out = dot(hidden, wd)

    @pl.when(step == 0)
    def _():
        back_acc[...] = back
        out_acc[...] = out

    @pl.when(step > 0)
    def _():
        back_acc[...] += back
        out_acc[...] += out

    @pl.when(step == pl.num_programs(0) - 1)
    def _():
        back_ref[...] = back_acc[...].astype(BF)
        out_ref[...] = out_acc[...].astype(BF)


def mlp(x, cot, wg, wu, wd):
    rows, width = x.shape
    units = wg.shape[1]
    block = min(512, units)
    whole = pl.BlockSpec((rows, width), lambda i: (0, 0))
    wspec = pl.BlockSpec((width, block), lambda i: (0, i))
    return pl.pallas_call(
        mlp_kernel,
        grid=(units // block,),
        in_specs=[whole, whole, wspec, wspec, pl.BlockSpec((block, width), lambda i: (i, 0))],
        out_specs=[whole, whole],
        out_shape=[jax.ShapeDtypeStruct((rows, width), BF)] * 2,
        scratch_shapes=[pltpu.VMEM((rows, width), F32)] * 2,
        compiler_params=pltpu.CompilerParams(vmem_limit_bytes=VMEM_LIMIT),
        cost_estimate=pl.CostEstimate(
            flops=12 * rows * width * units, bytes_accessed=6 * width * units, transcendentals=0
        ),
    )(x, cot, wg, wu, wd)


def mlp_grad_kernel(
    tile, x_ref, cot_ref, xb_ref, cb_ref, wg_ref, wu_ref, wd_ref, *rest
):
    gg_ref, ug_ref, dg_ref, hid, gbk, ubk = rest[-6:]
    wg, wu, wd = wg_ref[...], wu_ref[...], wd_ref[...]

    def part(i, _):
        at = pl.ds(pl.multiple_of(i * tile, tile), tile)
        x, cot = x_ref[at, :], cot_ref[at, :]
        hid[at, :], gbk[at, :], ubk[at, :] = gate_math(dot(x, wg), dot(x, wu), dot_nt(cot, wd))
        return 0

    lax.fori_loop(0, x_ref.shape[0] // tile, part, 0)
    xb = xb_ref[...]
    gg_ref[...] = dot_tn(xb, gbk[...])
    ug_ref[...] = dot_tn(xb, ubk[...])
    dg_ref[...] = dot_tn(hid[...], cb_ref[...])


def mlp_grad(x, cot, xb, cb, wg, wu, wd, first, count, before):
    rows, width = x.shape
    units = wg.shape[1]
    block = 256
    out = xb.shape[1]
    whole = lambda a: pl.BlockSpec(a.shape, lambda i: (0, 0))
    wspec = pl.BlockSpec((width, block), lambda i: (0, i + first))
    dspec = pl.BlockSpec((block, width), lambda i: (i + first, 0))
    any_spec = pl.BlockSpec(memory_space=pl.ANY)
    return pl.pallas_call(
        functools.partial(mlp_grad_kernel, min(512, rows)),
        grid=(count,),
        in_specs=[whole(x), whole(cot), whole(xb), whole(cb), wspec, wspec, dspec]
        + [any_spec] * len(before),
        out_specs=[pl.BlockSpec((out, block), lambda i: (0, i + first))] * 2
        + [pl.BlockSpec((block, out), lambda i: (i + first, 0))],
        out_shape=[jax.ShapeDtypeStruct((out, units), F32)] * 2
        + [jax.ShapeDtypeStruct((units, out), F32)],
        scratch_shapes=[pltpu.VMEM((rows, block), BF)] * 3,
        input_output_aliases={7 + i: i for i in range(len(before))},
        compiler_params=pltpu.CompilerParams(vmem_limit_bytes=VMEM_LIMIT),
        cost_estimate=pl.CostEstimate(
            flops=6 * rows * block * count * (width + out),
            bytes_accessed=6 * width * block * count + 8 * rows * width,
            transcendentals=0,
        ),
    )(x, cot, xb, cb, wg, wu, wd, *before)


def row_mean(values):
    return jnp.mean(values, axis=-1, keepdims=True)


def norm_parts(values):
    root = lax.rsqrt(row_mean(values * values) + EPS)
    return values * root, root


def norm_back(upstream, scaled, root, gain):
    inner = upstream * gain
    return root * (inner - scaled * row_mean(inner * scaled))


def per_device(
    activations, cotangent, doc_ids, attn_gain, query_weight, key_weight, value_weight,
    out_weight, mlp_gain, gate_weight, up_weight, down_weight,
):
    rows, width = activations.shape[1:]
    n_dp, n_ctx, n_t = lax.axis_size("dp"), lax.axis_size("ctx"), lax.axis_size("tensor")
    dp, ctx, place = lax.axis_index("dp"), lax.axis_index("ctx"), lax.axis_index("tensor")
    chunk = rows // n_t
    length = rows * n_ctx
    slots = slot_order(n_t)
    scale, shift = HD ** (-0.5), -math.log(length)
    gain_first, gain_second = attn_gain.astype(F32), mlp_gain.astype(F32)

    def slotted(values):
        return jnp.concatenate(
            [lax.dynamic_slice_in_dim(values, (place ^ s) * chunk, chunk, 0) for s in slots], axis=0
        )

    inputs = slotted(activations[0])
    cot = slotted(cotangent[0])
    inputs32 = inputs.astype(F32)
    scaled_first, root_first = norm_parts(inputs32)
    normed_first = (scaled_first * gain_first).astype(BF)

    half = rows // 2 if n_t > 1 else rows
    mine = normed_first[:half]
    rings = [mine] + [turn(mine, "ctx", k) for k in range(1, n_ctx)]
    part = jnp.concatenate(
        [r[i * chunk : (i + 1) * chunk] for i in range(half // chunk) for r in rings], axis=0
    )
    x_seq = jnp.concatenate([part, swap(part, "tensor", 1)], axis=0) if n_t > 1 else part

    ring_at = ((ctx - jnp.arange(n_ctx, dtype=jnp.int32)) % n_ctx) * rows
    slot_at = (place ^ jnp.array(slots, jnp.int32)) * chunk
    spots = (
        slot_at[:, None, None] + ring_at[None, :, None]
        + jnp.arange(chunk, dtype=jnp.int32)[None, None, :]
    ).reshape(-1)
    cuts = [jnp.sum((doc_ids[0] < j).astype(jnp.int32)) for j in range(1, 4)]
    docs = sum((spots >= cut).astype(jnp.int32) for cut in cuts)
    allowed = (
        (spots[None, :] <= spots[:, None]) & (docs[None, :] == docs[:, None])
    ).astype(F32)
    allowed_own = allowed.reshape(n_t, n_ctx, chunk, length)[:, 0].reshape(rows, length)
    frequency = 10000.0 ** (-jnp.arange(HD // 2, dtype=F32) * 2.0 / HD)
    angles = spots.astype(F32)[:, None] * frequency[None, :]
    cos, sin = jnp.cos(angles), jnp.sin(angles)
    cos = jnp.concatenate([cos, cos], axis=1)
    sin = jnp.concatenate([-sin, sin], axis=1)

    cot_all = gather_tensor(gather_dp(gather_tokens(cot[:chunk])))

    q, k, v, attended, mass = attend(
        x_seq, query_weight, key_weight, value_weight, cos, sin, allowed_own,
        chunk, n_ctx, scale, shift,
    )
    attn_mass = from_slots(mass[:, :, 0].T, slots, place)

    branch = scatter_tensor(jnp.dot(attended, out_weight, preferred_element_type=F32).astype(BF))
    middle = inputs32[:chunk] + branch
    scaled_second, root_second = norm_parts(middle)
    normed_chunk = (scaled_second * gain_second).astype(BF)
    normed_second = gather_tensor(normed_chunk)
    second_part, mlp_part = mlp(normed_second, cot, gate_weight, up_weight, down_weight)
    x_all = gather_tensor(gather_dp(gather_tokens(normed_chunk)))

    second_back = scatter_tensor(second_part)
    mlp_gain_part = jnp.sum(second_back * scaled_second, axis=0)
    middle_back = cot[:chunk].astype(F32) + norm_back(
        second_back, scaled_second, root_second, gain_second
    )
    branch_back = gather_tensor(gather_tokens(middle_back.astype(BF)))

    layer_out = (middle + scatter_tensor(mlp_part)).astype(BF)
    layer_out = from_slots(gather_tensor(layer_out), slots, place)

    qb, kb, vb, attended_all, q_own, k_own, v_own = attend_back(
        branch_back, out_weight, q, k, v, cos, sin, allowed, chunk, n_ctx, scale, shift
    )
    first_part = (
        jnp.einsum("tc,dc->td", q_own, query_weight, preferred_element_type=F32)
        + jnp.einsum("tc,dc->td", k_own, key_weight, preferred_element_type=F32)
        + jnp.einsum("tc,dc->td", v_own, value_weight, preferred_element_type=F32)
    )
    first_back = scatter_tensor(first_part.astype(BF))
    scaled_chunk, root_chunk = scaled_first[:chunk], root_first[:chunk]
    attn_gain_part = jnp.sum(first_back * scaled_chunk, axis=0)
    input_grad = (
        middle_back + norm_back(first_back, scaled_chunk, root_chunk, gain_first)
    ).astype(BF)
    input_grad = from_slots(gather_tensor(input_grad), slots, place)

    out_cols = width // (n_dp * n_ctx)

    def block_of(values, step):
        owner = ((dp + step) % n_dp) * n_ctx + ctx
        return lax.dynamic_slice_in_dim(values, owner * out_cols, out_cols, 1)

    def summed(make):
        total = make(0)
        for step in range(1, n_dp):
            total = total + turn(make(step).astype(BF), "dp", step).astype(F32)
        return total

    grads = jnp.concatenate([qb, kb, vb], axis=1)
    qkv_grad = summed(
        lambda step: jnp.einsum(
            "td,tc->dc", block_of(x_seq, step), grads, preferred_element_type=F32
        )
    )
    query_grad, key_grad, value_grad = jnp.split(qkv_grad, 3, axis=1)
    out_grad = summed(
        lambda step: jnp.einsum(
            "tc,td->cd", attended_all, block_of(branch_back, step), preferred_element_type=F32
        )
    )
    blocks = gate_weight.shape[1] // 256
    calls = min(4, blocks)
    mlp_grads = ()
    for call in range(calls):
        mlp_grads = mlp_grad(
            x_all, cot_all, block_of(x_all, 0), block_of(cot_all, 0),
            gate_weight, up_weight, down_weight,
            call * blocks // calls, blocks // calls, mlp_grads,
        )
    gate_grad, up_grad, down_grad = mlp_grads

    gains = jnp.stack([attn_gain_part, mlp_gain_part])
    for bit in bits_of(n_t):
        gains = gains + swap(gains, "tensor", bit)
    gains = gains.reshape(2, n_dp * n_ctx, out_cols)

    def gain_block(step_dp, step_ctx):
        owner = ((dp + step_dp) % n_dp) * n_ctx + (ctx + step_ctx) % n_ctx
        return lax.dynamic_index_in_dim(gains, owner, 1, False)

    total = []
    for step_ctx in range(n_ctx):
        piece = gain_block(0, step_ctx)
        for step_dp in range(1, n_dp):
            piece = piece + turn(gain_block(step_dp, step_ctx), "dp", step_dp)
        total.append(turn(piece, "ctx", step_ctx) if step_ctx else piece)
    gain_grads = sum(total)

    return (
        layer_out[None], input_grad[None], gain_grads[0], query_grad, key_grad, value_grad,
        out_grad, gain_grads[1], gate_grad, up_grad, down_grad, attn_mass[None],
    )


def solution(mesh):
    return jax.shard_map(
        per_device,
        mesh=mesh,
        in_specs=(
            P("dp", "ctx", None),
            P("dp", "ctx", None),
            P("dp", None),
            P(),
            P(None, "tensor"),
            P(None, "tensor"),
            P(None, "tensor"),
            P("tensor", None),
            P(),
            P(None, "tensor"),
            P(None, "tensor"),
            P("tensor", None),
        ),
        out_specs=(
            P("dp", "ctx", None),
            P("dp", "ctx", None),
            P(("dp", "ctx")),
            P(("dp", "ctx"), "tensor"),
            P(("dp", "ctx"), "tensor"),
            P(("dp", "ctx"), "tensor"),
            P("tensor", ("dp", "ctx")),
            P(("dp", "ctx")),
            P(("dp", "ctx"), "tensor"),
            P(("dp", "ctx"), "tensor"),
            P("tensor", ("dp", "ctx")),
            P("dp", "ctx", "tensor"),
        ),
        check_vma=False,
    )
```

time: 1520 us -> 316 us (0.21)
  waiting for transfers between devices: 1300 us -> 91.5 us
  Pallas kernels: 0 us -> 95.8 us
  matrix products: 94.1 us -> 11.4 us
  blocking collectives: 72.2 us -> 0 us
  starting transfers between devices: 1.16 us -> 56.4 us
  local copies, waits for them, and re-layouts: 16.3 us -> 39.3 us
    reduce_scatter x9 -> x0, waiting for transfers between devices: 1220 us -> none  [the longest x1 286 us: per_device(): lax.psum_scatter(down_wgrad, ('dp', 'ctx'), scatter_dimension=1, tiled=True)]
    pallas_call x0 -> x7, Pallas kernels: none -> 95.8 us  [the longest x4 59.3 us: mlp_grad(): pl.pallas_call(functools.partial(mlp_grad_kernel, min(512, rows)), grid=(...]
    ppermute x0 -> x46, waiting for transfers between devices: none -> 91.5 us  [the longest x23 61 us: swap(): return lax.ppermute(values, axis, [(i, i ^ distance) for i in range(count)])]
    dot_general x45 -> x8, matrix products: 94.1 us -> 11.4 us  [the longest x2 3.53 us: per_device(): jnp.einsum('tc,td->cd', attended_all, block_of(branch_back, step), prefer...]
    psum x3 -> x0, waiting for transfers between devices: 82.3 us -> none  [the longest x1 36.6 us: per_device(): second_back = lax.psum(second_part, 'tensor')]
    ppermute x0 -> x46, starting transfers between devices: none -> 56.4 us  [the longest x23 40.6 us: turn(): lax.ppermute(values, axis, [(i, (i + shift) % count) for i in range(count)])]
    unnamed x1 -> x0, blocking collectives: 38.8 us -> none
    all_gather x2 -> x0, blocking collectives: 33.3 us -> none  [the longest x1 16.8 us: per_device(): lax.all_gather(key_rows, 'ctx', axis=0, tiled=True)]
  transfers between devices with their start and end apart: 12 -> 46, of which waited for: 12 -> 16; matrix products, arithmetic and copies ran while one was open for 4% -> 18% of each run, Pallas kernels for 0% -> 12%
where the time goes in v1:
time: 316 us; the launch traced here: 315 us
  Pallas kernels  95.8 us (30%)
  waiting for transfers between devices  91.5 us (29%)
  starting transfers between devices  56.4 us (18%)
  local copies, waits for them, and re-layouts  39.3 us (12%)
  other arithmetic  18.6 us (6%)
  matrix products  11.4 us (4%)
    ppermute x23, waiting for transfers between devices, swap(): return lax.ppermute(values, axis, [(i, i ^ distance) for i in range(count)])  61 us
    pallas_call x4, Pallas kernels, mlp_grad(): pl.pallas_call(functools.partial(mlp_grad_kernel, min(512, rows)), grid=(...  59.3 us
    ppermute x23, starting transfers between devices, turn(): lax.ppermute(values, axis, [(i, (i + shift) % count) for i in range(count)])  40.6 us
    ppermute x23, waiting for transfers between devices, turn(): lax.ppermute(values, axis, [(i, (i + shift) % count) for i in range(count)])  30.6 us
    unnamed x104, local copies, waits for them, and re-layouts  19.1 us
    pallas_call x1, Pallas kernels, mlp(): pl.pallas_call(mlp_kernel, grid=(units // block,), in_specs=[whole, whole...  18 us
    ppermute x23, starting transfers between devices, swap(): return lax.ppermute(values, axis, [(i, i ^ distance) for i in range(count)])  15.8 us
    pallas_call x1, Pallas kernels, attend_back(): pl.pallas_call(functools.partial(attend_back_kernel, chunk, ring, scale,...  9.94 us
  transfers between devices with their start and end apart: 46, of which 16 were waited for; matrix products, arithmetic and copies ran while one was open for 18% of the time, Pallas kernels for 12%

profile of v1, /device:TPU:0, one launch (start us, length us, event | category | flops | bytes accessed | tf_op | source)
XLA Modules:
  0.0 314.8 jit_solution(6153720297355146337)
XLA Ops:
  0.7 2.0 dynamic-slice_bitcast_fusion.2
  3.8 3.0 collective-permute-start
  6.8 2.6 collective-permute-start.1
  16.5 2.6 convert_add_fusion.4
  19.2 2.0 convert_add_fusion.5
  26.8 5.1 %collective-permute-start.40 = (bf16[32,2048]{1,0:T(8,128)(2,1)S(1)}, bf16[32,2048]{1,0:T(8,128)(2,1)}, u32[]{:S(2)}, u32[]{:S(2)}) collective-permute-start(bf16[32,2048]{1,0:T(8,128)(2,1)S(1)} %get-tuple-element.72), channel_id=1, source_target_pairs={{0,4},{4,8},{8,12},{12,0},{1,5},{5,9},{9,13},{13,1},{2,6},{6,10},{... | collective-permute-start | bytes 393224 | tf_op jit(solution)/shard_map/ppermute | solution.py:25
  32.2 2.6 collective-permute-done.3
  36.2 8.6 %shard_map.220 = (bf16[512,512]{1,0:T(8,128)(2,1)}, bf16[512,512]{1,0:T(8,128)(2,1)}, bf16[512,512]{1,0:T(8,128)(2,1)}, bf16[128,512]{1,0:T(8,128)(2,1)}, f32[4,128,1]{2,1,0:T(8,128)}) custom-call(bf16[512,2048]{1,0:T(8,128)(2,1)} %copy-done.18, bf16[2048,512]{1,0:T(8,128)(2,1)} %wq_ref.1, bf16[2048,512]{1,0:T(8,128)(2,1)} %wk_ref.1, ...), custom_call_target="tpu_custom_call" | custom-call | flops 3221225472 | bytes 6291456 | tf_op jit(solution)/shard_map/pallas_call | solution.py:134
  53.2 2.2 fusion.5
  60.9 8.9 %collective-permute-start.36 = (bf16[32,2048]{1,0:T(8,128)(2,1)S(1)}, bf16[32,2048]{1,0:T(8,128)(2,1)S(1)}, u32[]{:S(2)}, u32[]{:S(2)}) collective-permute-start(bf16[32,2048]{1,0:T(8,128)(2,1)S(1)} %get-tuple-element.74), channel_id=1, source_target_pairs={{0,12},{4,0},{8,4},{12,8},{1,13},{5,1},{9,5},{13,9},{2,14},{6,2},{... | collective-permute-start | bytes 393224 | tf_op jit(solution)/shard_map/ppermute | solution.py:25
  71.2 7.1 %collective-permute-done.34 = bf16[32,2048]{1,0:T(8,128)(2,1)S(1)} collective-permute-done((bf16[32,2048]{1,0:T(8,128)(2,1)S(1)}, bf16[32,2048]{1,0:T(8,128)(2,1)S(1)}, u32[]{:S(2)}, u32[]{:S(2)}) %collective-permute-start.34) | collective-permute-done | bytes 131104 | tf_op jit(solution)/shard_map/ppermute | solution.py:25
  81.3 18.0 %shard_map.221 = (bf16[128,2048]{1,0:T(8,128)(2,1)}, bf16[128,2048]{1,0:T(8,128)(2,1)}) custom-call(bf16[128,2048]{1,0:T(8,128)(2,1)} %get-tuple-element.144.x_ref, bf16[128,2048]{1,0:T(8,128)(2,1)} %get-tuple-element.131.cot_ref, bf16[2048,2048]{1,0:T(8,128)(2,1)} %wg_ref.9, bf16[2048,2048]{1,0:T(8,128)(2,1)} %wu_ref.9, bf16[2048,2048]{1,0:T(8,128)(2,1)} %wd_ref.9), custom_call_target="tpu_custom_call" | custom-call | flops 6442450944 | bytes 25165824 | tf_op jit(solution)/shard_map/pallas_call | solution.py:241
  107.5 4.2 %collective-permute-done.13 = bf16[32,2048]{1,0:T(8,128)(2,1)S(1)} collective-permute-done((bf16[32,2048]{1,0:T(8,128)(2,1)S(1)}, bf16[32,2048]{1,0:T(8,128)(2,1)S(1)}, u32[]{:S(2)}, u32[]{:S(2)}) %collective-permute-start.13) | collective-permute-done | bytes 131104 | tf_op jit(solution)/shard_map/ppermute | solution.py:20
  113.7 2.0 collective-permute-start.15
  121.2 2.2 constant_dynamic-update-slice_fusion.55
  123.4 2.9 collective-permute-start.16
  132.0 31.6 %collective-permute-done.17 = bf16[128,2048]{1,0:T(8,128)(2,1)S(1)} collective-permute-done((bf16[128,2048]{1,0:T(8,128)(2,1)S(1)}, bf16[128,2048]{1,0:T(8,128)(2,1)S(1)}, u32[]{:S(2)}, u32[]{:S(2)}) %collective-permute-start.17) | collective-permute-done | bytes 524320 | tf_op jit(solution)/shard_map/ppermute | solution.py:20
  165.6 16.1 %collective-permute-done.38 = bf16[256,2048]{1,0:T(8,128)(2,1)S(1)} collective-permute-done((bf16[256,2048]{1,0:T(8,128)(2,1)S(1)}, bf16[256,2048]{1,0:T(8,128)(2,1)S(1)}, u32[]{:S(2)}, u32[]{:S(2)}) %collective-permute-start.38) | collective-permute-done | bytes 1048608 | tf_op jit(solution)/shard_map/ppermute | solution.py:20
  184.8 9.9 %shard_map.222 = (bf16[512,512]{1,0:T(8,128)(2,1)}, bf16[512,512]{1,0:T(8,128)(2,1)}, bf16[512,512]{1,0:T(8,128)(2,1)}, bf16[512,512]{1,0:T(8,128)(2,1)}, bf16[1...) custom-call(bf16[512,2048]{1,0:T(8,128)(2,1)} %copy-done.21, bf16[512,2048]{1,0:T(8,128)(2,1)} %wo_ref.1, ...), custom_call_target="tpu_custom_call" | custom-call | flops 2952790016 | bytes 9437184 | tf_op jit(solution)/shard_map/pallas_call | solution.py:185
  194.8 1.9 fusion.42
  203.9 2.5 collective-permute-done.20
  210.3 6.6 %collective-permute-done.33 = bf16[512,256]{1,0:T(8,128)(2,1)S(1)} collective-permute-done((bf16[512,256]{1,0:T(8,128)(2,1)S(1)}, bf16[512,256]{1,0:T(8,128)(2,1)S(1)}, u32[]{:S(2)}, u32[]{:S(2)}) %collective-permute-start.33) | collective-permute-done | bytes 262176 | tf_op jit(solution)/shard_map/ppermute | solution.py:25
  216.9 2.1 convolution_add_fusion.2
  231.1 2.9 collective-permute-done.21
  234.1 11.7 %collective-permute-done.32 = bf16[256,1536]{1,0:T(8,128)(2,1)S(1)} collective-permute-done((bf16[256,1536]{1,0:T(8,128)(2,1)S(1)}, bf16[256,1536]{1,0:T(8,128)(2,1)S(1)}, u32[]{:S(2)}, u32[]{:S(2)}) %collective-permute-start.32) | collective-permute-done | bytes 786464 | tf_op jit(solution)/shard_map/ppermute | solution.py:25
  248.6 2.0 constant_dynamic-update-slice_fusion.60.cot_ref
  251.6 2.0 constant_dynamic-update-slice_fusion.42.x_ref
  253.6 1.9 constant_dynamic-slice_fusion.1.xb_ref
  255.5 14.8 %shard_map.223 = (f32[256,2048]{1,0:T(8,128)}, f32[256,2048]{1,0:T(8,128)}, f32[2048,256]{1,0:T(8,128)}) custom-call(bf16[1024,2048]{1,0:T(8,128)(2,1)} %constant_dynamic-update-slice_fusion.42.x_ref, bf16[1024,2048]{1,0:T(8,128)(2,1)} %copy-done, bf16[1024,256]{1,0:T(8,128)(2,1)} %constant_dynamic-slice_fusion.1.xb_ref, ...), custom_call_target="tpu_custom_call" | custom-call | flops 7247757312 | bytes 23068672 | tf_op jit(solution)/shard_map/pallas_call | solution.py:283
  270.2 14.9 %shard_map.224 = (f32[256,2048]{1,0:T(8,128)}, f32[256,2048]{1,0:T(8,128)}, f32[2048,256]{1,0:T(8,128)}) custom-call(bf16[1024,2048]{1,0:T(8,128)(2,1)} %constant_dynamic-update-slice_fusion.42.x_ref, bf16[1024,2048]{1,0:T(8,128)(2,1)} %copy-done, ...), custom_call_target="tpu_custom_call", output_to_operand_aliasing={{0}: (7, {}), {1}: (8, {}), {2}: (9, {})} | custom-call | flops 7247757312 | bytes 23068672 | tf_op jit(solution)/shard_map/pallas_call | solution.py:283
  285.1 14.9 %shard_map.225 = (f32[256,2048]{1,0:T(8,128)}, f32[256,2048]{1,0:T(8,128)}, f32[2048,256]{1,0:T(8,128)}) custom-call(bf16[1024,2048]{1,0:T(8,128)(2,1)} %constant_dynamic-update-slice_fusion.42.x_ref, bf16[1024,2048]{1,0:T(8,128)(2,1)} %copy-done, ...), custom_call_target="tpu_custom_call", output_to_operand_aliasing={{0}: (7, {}), {1}: (8, {}), {2}: (9, {})} | custom-call | flops 7247757312 | bytes 23068672 | tf_op jit(solution)/shard_map/pallas_call | solution.py:283
  300.0 14.8 %shard_map.226 = (f32[256,2048]{1,0:T(8,128)}, f32[256,2048]{1,0:T(8,128)}, f32[2048,256]{1,0:T(8,128)}) custom-call(bf16[1024,2048]{1,0:T(8,128)(2,1)} %constant_dynamic-update-slice_fusion.42.x_ref, bf16[1024,2048]{1,0:T(8,128)(2,1)} %copy-done, ...), custom_call_target="tpu_custom_call", output_to_operand_aliasing={{0}: (7, {}), {1}: (8, {}), {2}: (9, {})} | custom-call | flops 7247757312 | bytes 23068672 | tf_op jit(solution)/shard_map/pallas_call | solution.py:283
  (265 shorter events, 86.6 us)
Async XLA Ops:
  3.8 22.9 %collective-permute-start = (bf16[64,2048]{1,0:T(8,128)(2,1)}, bf16[64,2048]{1,0:T(8,128)(2,1)S(1)}, u32[]{:S(2)}, u32[]{:S(2)}) collective-permute-start(bf16[64,2048]{1,0:T(8,128)(2,1)} %slice.166), channel_id=1, source_target_pairs={{0,4},{4,8},{8,12},{12,0},{1,5},{5,9},{9,13},{13,1},{2,6},{6,10},{... | collective-permute-start | bytes 786440 | tf_op jit(solution)/shard_map/ppermute | solution.py:25
  6.8 25.0 %collective-permute-start.1 = (bf16[64,2048]{1,0:T(8,128)(2,1)}, bf16[64,2048]{1,0:T(8,128)(2,1)S(1)}, u32[]{:S(2)}, u32[]{:S(2)}) collective-permute-start(bf16[64,2048]{1,0:T(8,128)(2,1)} %slice.166), channel_id=1, source_target_pairs={{0,8},{4,12},{8,0},{12,4},{1,9},{5,13},{9,1},{13,5},{2,10},{6,14},... | collective-permute-start | bytes 786440 | tf_op jit(solution)/shard_map/ppermute | solution.py:25
  9.4 22.5 %collective-permute-start.2 = (bf16[64,2048]{1,0:T(8,128)(2,1)}, bf16[64,2048]{1,0:T(8,128)(2,1)S(1)}, u32[]{:S(2)}, u32[]{:S(2)}) collective-permute-start(bf16[64,2048]{1,0:T(8,128)(2,1)} %slice.166), channel_id=1, source_target_pairs={{0,12},{4,0},{8,4},{12,8},{1,13},{5,1},{9,5},{13,9},{2,14},{6,2},{... | collective-permute-start | bytes 786440 | tf_op jit(solution)/shard_map/ppermute | solution.py:25
  12.4 40.8 %collective-permute-start.42 = (bf16[32,2048]{1,0:T(8,128)(2,1)S(1)}, bf16[32,2048]{1,0:T(8,128)(2,1)}, u32[]{:S(2)}, u32[]{:S(2)}) collective-permute-start(bf16[32,2048]{1,0:T(8,128)(2,1)S(1)} %get-tuple-element.72), channel_id=1, source_target_pairs={{0,12},{4,0},{8,4},{12,8},{1,13},{5,1},{9,5},{13,9},{2,14},{6,2},{... | collective-permute-start | bytes 393224 | tf_op jit(solution)/shard_map/ppermute | solution.py:25
  12.8 40.3 %collective-permute-start.41 = (bf16[32,2048]{1,0:T(8,128)(2,1)S(1)}, bf16[32,2048]{1,0:T(8,128)(2,1)}, u32[]{:S(2)}, u32[]{:S(2)}) collective-permute-start(bf16[32,2048]{1,0:T(8,128)(2,1)S(1)} %get-tuple-element.72), channel_id=1, source_target_pairs={{0,8},{4,12},{8,0},{12,4},{1,9},{5,13},{9,1},{13,5},{2,10},{6,14},... | collective-permute-start | bytes 393224 | tf_op jit(solution)/shard_map/ppermute | solution.py:25
  26.8 26.4 %collective-permute-start.40 = (bf16[32,2048]{1,0:T(8,128)(2,1)S(1)}, bf16[32,2048]{1,0:T(8,128)(2,1)}, u32[]{:S(2)}, u32[]{:S(2)}) collective-permute-start(bf16[32,2048]{1,0:T(8,128)(2,1)S(1)} %get-tuple-element.72), channel_id=1, source_target_pairs={{0,4},{4,8},{8,12},{12,0},{1,5},{5,9},{9,13},{13,1},{2,6},{6,10},{... | collective-permute-start | bytes 393224 | tf_op jit(solution)/shard_map/ppermute | solution.py:25
  51.6 6.0 %collective-permute-start.5 = (bf16[32,2048]{1,0:T(8,128)(2,1)}, bf16[32,2048]{1,0:T(8,128)(2,1)S(1)}, u32[]{:S(2)}, u32[]{:S(2)}) collective-permute-start(bf16[32,2048]{1,0:T(8,128)(2,1)} %slice.264), channel_id=1, source_target_pairs={{0,2},{1,3},{2,0},{3,1},{4,6},{5,7},{6,4},{7,5},{8,10},{9,11},{10,... | collective-permute-start | bytes 393224 | tf_op jit(solution)/shard_map/ppermute | solution.py:20
  55.4 65.8 %collective-permute-start.43 = (bf16[128,2048]{1,0:T(8,128)(2,1)}, bf16[128,2048]{1,0:T(8,128)(2,1)}, u32[]{:S(2)}, u32[]{:S(2)}) collective-permute-start(bf16[128,2048]{1,0:T(8,128)(2,1)} %get-tuple-element.130), channel_id=1, source_target_pairs={{0,16},{16,0},{1,17},{17,1},{2,18},{18,2},{3,19},{19,3},{4,20},{20... | collective-permute-start | bytes 1572872 | tf_op jit(solution)/shard_map/ppermute | solution.py:25
  58.5 11.9 %collective-permute-start.6 = (bf16[32,2048]{1,0:T(8,128)(2,1)S(1)}, bf16[32,2048]{1,0:T(8,128)(2,1)S(1)}, u32[]{:S(2)}, u32[]{:S(2)}) collective-permute-start(bf16[32,2048]{1,0:T(8,128)(2,1)S(1)} %get-tuple-element.74), channel_id=1, source_target_pairs={{0,2},{1,3},{2,0},{3,1},{4,6},{5,7},{6,4},{7,5},{8,10},{9,11},{10,... | collective-permute-start | bytes 393224 | tf_op jit(solution)/shard_map/ppermute | solution.py:20
  60.9 18.2 %collective-permute-start.36 = (bf16[32,2048]{1,0:T(8,128)(2,1)S(1)}, bf16[32,2048]{1,0:T(8,128)(2,1)S(1)}, u32[]{:S(2)}, u32[]{:S(2)}) collective-permute-start(bf16[32,2048]{1,0:T(8,128)(2,1)S(1)} %get-tuple-element.74), channel_id=1, source_target_pairs={{0,12},{4,0},{8,4},{12,8},{1,13},{5,1},{9,5},{13,9},{2,14},{6,2},{... | collective-permute-start | bytes 393224 | tf_op jit(solution)/shard_map/ppermute | solution.py:25
  69.8 10.7 %collective-permute-start.35 = (bf16[32,2048]{1,0:T(8,128)(2,1)S(1)}, bf16[32,2048]{1,0:T(8,128)(2,1)S(1)}, u32[]{:S(2)}, u32[]{:S(2)}) collective-permute-start(bf16[32,2048]{1,0:T(8,128)(2,1)S(1)} %get-tuple-element.74), channel_id=1, source_target_pairs={{0,8},{4,12},{8,0},{12,4},{1,9},{5,13},{9,1},{13,5},{2,10},{6,14},... | collective-permute-start | bytes 393224 | tf_op jit(solution)/shard_map/ppermute | solution.py:25
  69.8 8.6 %collective-permute-start.34 = (bf16[32,2048]{1,0:T(8,128)(2,1)S(1)}, bf16[32,2048]{1,0:T(8,128)(2,1)S(1)}, u32[]{:S(2)}, u32[]{:S(2)}) collective-permute-start(bf16[32,2048]{1,0:T(8,128)(2,1)S(1)} %get-tuple-element.74), channel_id=1, source_target_pairs={{0,4},{4,8},{8,12},{12,0},{1,5},{5,9},{9,13},{13,1},{2,6},{6,10},{... | collective-permute-start | bytes 393224 | tf_op jit(solution)/shard_map/ppermute | solution.py:25
  70.5 10.0 %collective-permute-start.7 = (bf16[64,2048]{1,0:T(8,128)(2,1)S(1)}, bf16[64,2048]{1,0:T(8,128)(2,1)S(1)}, u32[]{:S(2)}, u32[]{:S(2)}) collective-permute-start(bf16[64,2048]{1,0:T(8,128)(2,1)S(1)} %pad_maximum_fusion.7), channel_id=1, source_target_pairs={{0,1},{1,0},{2,3},{3,2},{4,5},{5,4},{6,7},{7,6},{8,9},{9,8},{10,11... | collective-permute-start | bytes 786440 | tf_op jit(solution)/shard_map/ppermute | solution.py:20
  103.7 26.7 %collective-permute-start.37 = (bf16[128,2048]{1,0:T(8,128)(2,1)S(1)}, bf16[128,2048]{1,0:T(8,128)(2,1)S(1)}, u32[]{:S(2)}, u32[]{:S(2)}) collective-permute-start(bf16[128,2048]{1,0:T(8,128)(2,1)S(1)} %get-tuple-element.143), channel_id=1, source_target_pairs={{0,16},{16,0},{1,17},{17,1},{2,18},{18,2},{3,19},{19,3},{4,20},{20... | collective-permute-start | bytes 1572872 | tf_op jit(solution)/shard_map/ppermute | solution.py:25
  105.3 6.5 %collective-permute-start.13 = (bf16[32,2048]{1,0:T(8,128)(2,1)S(1)}, bf16[32,2048]{1,0:T(8,128)(2,1)S(1)}, u32[]{:S(2)}, u32[]{:S(2)}) collective-permute-start(bf16[32,2048]{1,0:T(8,128)(2,1)S(1)} %slice.262), channel_id=1, source_target_pairs={{0,2},{1,3},{2,0},{3,1},{4,6},{5,7},{6,4},{7,5},{8,10},{9,11},{10,... | collective-permute-start | bytes 393224 | tf_op jit(solution)/shard_map/ppermute | solution.py:20
  106.0 9.7 %collective-permute-start.9 = (bf16[32,2048]{1,0:T(8,128)(2,1)S(1)}, bf16[32,2048]{1,0:T(8,128)(2,1)S(1)}, u32[]{:S(2)}, u32[]{:S(2)}) collective-permute-start(bf16[32,2048]{1,0:T(8,128)(2,1)S(1)} %slice.263), channel_id=1, source_target_pairs={{0,2},{1,3},{2,0},{3,1},{4,6},{5,7},{6,4},{7,5},{8,10},{9,11},{10,... | collective-permute-start | bytes 393224 | tf_op jit(solution)/shard_map/ppermute | solution.py:20
  112.1 15.7 %collective-permute-start.14 = (bf16[32,2048]{1,0:T(8,128)(2,1)S(1)}, bf16[32,2048]{1,0:T(8,128)(2,1)S(1)}, u32[]{:S(2)}, u32[]{:S(2)}) collective-permute-start(bf16[32,2048]{1,0:T(8,128)(2,1)S(1)} %get-tuple-element.128), channel_id=1, source_target_pairs={{0,4},{4,8},{8,12},{12,0},{1,5},{5,9},{9,13},{13,1},{2,6},{6,10},{... | collective-permute-start | bytes 393224 | tf_op jit(solution)/shard_map/ppermute | solution.py:25
  113.7 14.2 %collective-permute-start.15 = (bf16[32,2048]{1,0:T(8,128)(2,1)S(1)}, bf16[32,2048]{1,0:T(8,128)(2,1)S(1)}, u32[]{:S(2)}, u32[]{:S(2)}) collective-permute-start(bf16[32,2048]{1,0:T(8,128)(2,1)S(1)} %get-tuple-element.128), channel_id=1, source_target_pairs={{0,8},{4,12},{8,0},{12,4},{1,9},{5,13},{9,1},{13,5},{2,10},{6,14},... | collective-permute-start | bytes 393224 | tf_op jit(solution)/shard_map/ppermute | solution.py:25
  115.8 10.5 %collective-permute-start.10 = (bf16[32,2048]{1,0:T(8,128)(2,1)S(1)}, bf16[32,2048]{1,0:T(8,128)(2,1)S(1)}, u32[]{:S(2)}, u32[]{:S(2)}) collective-permute-start(bf16[32,2048]{1,0:T(8,128)(2,1)S(1)} %get-tuple-element.81), channel_id=1, source_target_pairs={{0,2},{1,3},{2,0},{3,1},{4,6},{5,7},{6,4},{7,5},{8,10},{9,11},{10,... | collective-permute-start | bytes 393224 | tf_op jit(solution)/shard_map/ppermute | solution.py:20
  126.3 37.6 %collective-permute-start.44 = (bf16[256,2048]{1,0:T(8,128)(2,1)S(1)}, bf16[256,2048]{1,0:T(8,128)(2,1)S(1)}, u32[]{:S(2)}, u32[]{:S(2)}) collective-permute-start(bf16[256,2048]{1,0:T(8,128)(2,1)S(1)} %get-tuple-element.95), channel_id=1, source_target_pairs={{0,2},{1,3},{2,0},{3,1},{4,6},{5,7},{6,4},{7,5},{8,10},{9,11},{10,... | collective-permute-start | bytes 3145736 | tf_op jit(solution)/shard_map/ppermute | solution.py:20
  127.8 36.0 %collective-permute-start.11 = (bf16[64,2048]{1,0:T(8,128)(2,1)S(1)}, bf16[64,2048]{1,0:T(8,128)(2,1)S(1)}, u32[]{:S(2)}, u32[]{:S(2)}) collective-permute-start(bf16[64,2048]{1,0:T(8,128)(2,1)S(1)} %pad_maximum_fusion.8), channel_id=1, source_target_pairs={{0,1},{1,0},{2,3},{3,2},{4,5},{5,4},{6,7},{7,6},{8,9},{9,8},{10,11... | collective-permute-start | bytes 786440 | tf_op jit(solution)/shard_map/ppermute | solution.py:20
  128.8 34.8 %collective-permute-start.17 = (bf16[128,2048]{1,0:T(8,128)(2,1)S(1)}, bf16[128,2048]{1,0:T(8,128)(2,1)S(1)}, u32[]{:S(2)}, u32[]{:S(2)}) collective-permute-start(bf16[128,2048]{1,0:T(8,128)(2,1)S(1)} %pad_maximum_fusion.4), channel_id=1, source_target_pairs={{0,2},{1,3},{2,0},{3,1},{4,6},{5,7},{6,4},{7,5},{8,10},{9,11},{10,... | collective-permute-start | bytes 1572872 | tf_op jit(solution)/shard_map/ppermute | solution.py:20
  131.4 50.3 %collective-permute-start.38 = (bf16[256,2048]{1,0:T(8,128)(2,1)S(1)}, bf16[256,2048]{1,0:T(8,128)(2,1)S(1)}, u32[]{:S(2)}, u32[]{:S(2)}) collective-permute-start(bf16[256,2048]{1,0:T(8,128)(2,1)S(1)} %get-tuple-element.98), channel_id=1, source_target_pairs={{0,2},{1,3},{2,0},{3,1},{4,6},{5,7},{6,4},{7,5},{8,10},{9,11},{10,... | collective-permute-start | bytes 3145736 | tf_op jit(solution)/shard_map/ppermute | solution.py:20
  163.7 19.1 %collective-permute-start.18 = (bf16[256,2048]{1,0:T(8,128)(2,1)S(1)}, bf16[256,2048]{1,0:T(8,128)(2,1)S(1)}, u32[]{:S(2)}, u32[]{:S(2)}) collective-permute-start(bf16[256,2048]{1,0:T(8,128)(2,1)S(1)} %get-tuple-element.99), channel_id=1, source_target_pairs={{0,1},{1,0},{2,3},{3,2},{4,5},{5,4},{6,7},{7,6},{8,9},{9,8},{10,11... | collective-permute-start | bytes 3145736 | tf_op jit(solution)/shard_map/ppermute | solution.py:20
  165.1 83.5 %collective-permute-start.45 = (bf16[512,2048]{1,0:T(8,128)(2,1)}, bf16[512,2048]{1,0:T(8,128)(2,1)}, u32[]{:S(2)}, u32[]{:S(2)}) collective-permute-start(bf16[512,2048]{1,0:T(8,128)(2,1)} %get-tuple-element.87), channel_id=1, source_target_pairs={{0,1},{1,0},{2,3},{3,2},{4,5},{5,4},{6,7},{7,6},{8,9},{9,8},{10,11... | collective-permute-start | bytes 6291464 | tf_op jit(solution)/shard_map/ppermute | solution.py:20
  200.8 5.6 %collective-permute-start.20 = (bf16[32,2048]{1,0:T(8,128)(2,1)S(1)}, bf16[32,2048]{1,0:T(8,128)(2,1)S(1)}, u32[]{:S(2)}, u32[]{:S(2)}) collective-permute-start(bf16[32,2048]{1,0:T(8,128)(2,1)S(1)} %slice.261), channel_id=1, source_target_pairs={{0,2},{1,3},{2,0},{3,1},{4,6},{5,7},{6,4},{7,5},{8,10},{9,11},{10,... | collective-permute-start | bytes 393224 | tf_op jit(solution)/shard_map/ppermute | solution.py:20
  208.1 8.8 %collective-permute-start.33 = (bf16[512,256]{1,0:T(8,128)(2,1)S(1)}, bf16[512,256]{1,0:T(8,128)(2,1)S(1)}, u32[]{:S(2)}, u32[]{:S(2)}) collective-permute-start(bf16[512,256]{1,0:T(8,128)(2,1)S(1)} %convolution_convert_fusion.2), channel_id=1, source_target_pairs={{0,16},{16,0},{1,17},{17,1},{2,18},{18,2},{3,19},{19,3},{4,20},{20... | collective-permute-start | bytes 786440 | tf_op jit(solution)/shard_map/ppermute | solution.py:25
  208.7 10.2 %collective-permute-start.24 = (f32[2,2048]{1,0:T(2,128)S(1)}, f32[2,2048]{1,0:T(2,128)S(1)}, u32[]{:S(2)}, u32[]{:S(2)}) collective-permute-start(f32[2,2048]{1,0:T(2,128)S(1)} %fusion.36), channel_id=1, source_target_pairs={{0,2},{1,3},{2,0},{3,1},{4,6},{5,7},{6,4},{7,5},{8,10},{9,11},{10,... | collective-permute-start | bytes 49160 | tf_op jit(solution)/shard_map/ppermute | solution.py:20
  224.7 5.7 %collective-permute-start.27 = (f32[2,256]{1,0:T(2,128)S(1)}, f32[2,256]{1,0:T(2,128)S(1)}, u32[]{:S(2)}, u32[]{:S(2)}) collective-permute-start(f32[2,256]{1,0:T(2,128)S(1)} %bitcast_add_fusion.2), channel_id=1, source_target_pairs={{0,4},{4,8},{8,12},{12,0},{1,5},{5,9},{9,13},{13,1},{2,6},{6,10},{... | collective-permute-start | bytes 6152 | tf_op jit(solution)/shard_map/ppermute | solution.py:25
  225.8 25.8 %collective-permute-start.39 = (bf16[512,2048]{1,0:T(8,128)(2,1)S(1)}, bf16[512,2048]{1,0:T(8,128)(2,1)S(1)}, u32[]{:S(2)}, u32[]{:S(2)}) collective-permute-start(bf16[512,2048]{1,0:T(8,128)(2,1)S(1)} %copy-done.28), channel_id=1, source_target_pairs={{0,1},{1,0},{2,3},{3,2},{4,5},{5,4},{6,7},{7,6},{8,9},{9,8},{10,11... | collective-permute-start | bytes 6291464 | tf_op jit(solution)/shard_map/ppermute | solution.py:20
  226.8 19.0 %collective-permute-start.32 = (bf16[256,1536]{1,0:T(8,128)(2,1)S(1)}, bf16[256,1536]{1,0:T(8,128)(2,1)S(1)}, u32[]{:S(2)}, u32[]{:S(2)}) collective-permute-start(bf16[256,1536]{1,0:T(8,128)(2,1)S(1)} %convolution_convert_fusion), channel_id=1, source_target_pairs={{0,16},{16,0},{1,17},{17,1},{2,18},{18,2},{3,19},{19,3},{4,20},{20... | collective-permute-start | bytes 2359304 | tf_op jit(solution)/shard_map/ppermute | solution.py:25
  234.0 14.6 %collective-permute-start.22 = (bf16[64,2048]{1,0:T(8,128)(2,1)S(1)}, bf16[64,2048]{1,0:T(8,128)(2,1)S(1)}, u32[]{:S(2)}, u32[]{:S(2)}) collective-permute-start(bf16[64,2048]{1,0:T(8,128)(2,1)S(1)} %pad_maximum_fusion.9), channel_id=1, source_target_pairs={{0,1},{1,0},{2,3},{3,2},{4,5},{5,4},{6,7},{7,6},{8,9},{9,8},{10,11... | collective-permute-start | bytes 786440 | tf_op jit(solution)/shard_map/ppermute | solution.py:20
  (49 other events, 311.5 us)

commit v2 on v1

v2 whole, which is shorter than its diff:
```python
import functools
import math

import jax
import jax.numpy as jnp
import numpy as np
from jax import lax
from jax.experimental import pallas as pl
from jax.experimental.pallas import tpu as pltpu
from jax.sharding import PartitionSpec as P

HD = 128
EPS = 1e-05
BF = jnp.bfloat16
F32 = jnp.float32
MIB = 1024 * 1024


def swap(values, axis, distance):
    count = lax.axis_size(axis)
    return lax.ppermute(values, axis, [(i, i ^ distance) for i in range(count)])


def turn(values, axis, shift):
    count = lax.axis_size(axis)
    return lax.ppermute(values, axis, [(i, (i + shift) % count) for i in range(count)])


def after(value, *others):
    return lax.optimization_barrier((value, others))[0]


def in_hbm(values):
    return pltpu.with_memory_space_constraint(values, pltpu.HBM)


def in_vmem(values):
    return pltpu.with_memory_space_constraint(values, pltpu.VMEM)


def bits_of(count):
    return [1 << i for i in range(count.bit_length() - 1)]


def slot_order(count):
    order = [0]
    for bit in reversed(bits_of(count)):
        order = order + [slot ^ bit for slot in order]
    return order


def gather_tensor(rows):
    for bit in reversed(bits_of(lax.axis_size("tensor"))):
        rows = jnp.concatenate([rows, swap(rows, "tensor", bit)], axis=0)
    return rows


def scatter_tensor(rows, beside=()):
    bits = bits_of(lax.axis_size("tensor"))
    for bit in bits:
        half = rows.shape[0] // 2
        got = swap(rows[half:].astype(BF), "tensor", bit)
        if bit == bits[-1]:
            got = after(got, beside)
        rows = rows[:half].astype(F32) + got.astype(F32)
    return rows


def ring_of(rows):
    return [rows] + [turn(rows, "ctx", k) for k in range(1, lax.axis_size("ctx"))]


def from_slots(blocks, slots, place):
    size = blocks.shape[0] // len(slots)
    out = jnp.zeros_like(blocks)
    for index, slot in enumerate(slots):
        out = lax.dynamic_update_slice_in_dim(
            out, blocks[index * size : (index + 1) * size], (place ^ slot) * size, 0
        )
    return out


def rope_rows(u, cos, sin):
    return u * cos + pltpu.roll(u, HD // 2, 1) * sin


def rope_back_rows(u, cos, sin):
    return u * cos - pltpu.roll(u, HD // 2, 1) * sin


def dot(a, b):
    return lax.dot_general(a, b, (((1,), (0,)), ((), ())), preferred_element_type=F32)


def dot_nt(a, b):
    return lax.dot_general(a, b, (((1,), (1,)), ((), ())), preferred_element_type=F32)


def dot_tn(a, b):
    return lax.dot_general(a, b, (((0,), (0,)), ((), ())), preferred_element_type=F32)


def place_rows(step, pieces, places, rows, sem, start=True, wait=True):
    @pl.when(step == 0)
    def _():
        copies = []
        for i, (piece, place) in enumerate(zip(pieces, places, strict=True)):
            copies.append(pltpu.make_async_copy(piece, rows.at[place], sem.at[i]))
        if start:
            for copy in copies:
                copy.start()
        if wait:
            for copy in copies:
                copy.wait()


def chunk_places(at_ref, first, count, chunk):
    return [
        pl.ds(pl.multiple_of(at_ref[first + i] * chunk, chunk), chunk) for i in range(count)
    ]


NEVER = -1e30


def attend_kernel(chunk, slots, scale, shift, at_ref, *refs):
    count = len(refs) - 17
    pieces = refs[:count]
    (own_spot_ref, own_doc_ref, doc_ref, cos_ref, sin_ref, wq_ref, wk_ref, wv_ref,
     q_ref, k_ref, v_ref, att_ref, mass_ref, seq_hbm, x, sem, out_sem) = refs[count:]
    step, last = pl.program_id(0), pl.num_programs(0) - 1
    place_rows(step, pieces, chunk_places(at_ref, 0, count, chunk), x, sem)
    keep = pltpu.make_async_copy(x, seq_hbm, out_sem)

    @pl.when(step == 0)
    def _():
        keep.start()

    cos, sin = cos_ref[...], sin_ref[...]
    shape = (own_spot_ref.shape[0], doc_ref.shape[1])
    allowed = (lax.broadcasted_iota(jnp.int32, shape, 1) <= own_spot_ref[...]) & (
        own_doc_ref[...] == doc_ref[...]
    )
    bias = jnp.where(allowed, shift, NEVER)
    rows = x[...]
    q_all = dot(rows, wq_ref[...])
    k_all = dot(rows, wk_ref[...])
    v_all = dot(rows, wv_ref[...]).astype(BF)
    v_ref[...] = v_all
    own = chunk_places(at_ref, 0, slots, chunk)
    for j in range(q_all.shape[1] // HD):
        cols = slice(j * HD, (j + 1) * HD)
        q_ref[:, cols] = rope_rows(q_all[:, cols], cos, sin).astype(BF)
        k = rope_rows(k_all[:, cols], cos, sin).astype(BF)
        k_ref[:, cols] = k
        q = jnp.concatenate([q_ref[spot, cols] for spot in own], axis=0)
        weights = jax.nn.sigmoid(dot_nt(q, k) * scale + bias)
        mass_ref[j] = jnp.sum(weights, axis=-1, keepdims=True)
        att_ref[:, cols] = dot(weights.astype(BF), v_all[:, cols]).astype(BF)

    @pl.when(step == last)
    def _():
        keep.wait()


def attend(places, pieces, own_spots, own_docs, docs, cos, sin, wq, wk, wv, slots, scale, shift):
    chunk, width = pieces[0].shape
    seq, rows = chunk * len(pieces), own_spots.shape[0]
    cols = wq.shape[1]
    heads = cols // HD
    step = min(2, heads)
    whole = lambda *shape: pl.BlockSpec(
        shape, lambda i: (0,) * len(shape), pipeline_mode=pl.Buffered(1)
    )
    hbm = pl.BlockSpec(memory_space=pl.ANY)
    wspec = pl.BlockSpec((width, step * HD), lambda i: (0, i))
    sspec = pl.BlockSpec((seq, step * HD), lambda i: (0, i))
    return pl.pallas_call(
        functools.partial(attend_kernel, chunk, slots, scale, shift),
        grid=(heads // step,),
        in_specs=[pl.BlockSpec(memory_space=pltpu.SMEM)] + [hbm] * len(pieces)
        + [whole(rows, 1), whole(rows, 1), whole(1, seq), whole(seq, HD), whole(seq, HD)]
        + [wspec] * 3,
        out_specs=[sspec, sspec, sspec,
                   pl.BlockSpec((rows, step * HD), lambda i: (0, i)),
                   pl.BlockSpec((step, rows, 1), lambda i: (i, 0, 0)),
                   pl.BlockSpec(memory_space=pltpu.HBM)],
        out_shape=[jax.ShapeDtypeStruct((seq, cols), BF)] * 3
        + [jax.ShapeDtypeStruct((rows, cols), BF), jax.ShapeDtypeStruct((heads, rows, 1), F32),
           jax.ShapeDtypeStruct((seq, width), BF)],
        scratch_shapes=[pltpu.VMEM((seq, width), BF),
                        pltpu.SemaphoreType.DMA((len(pieces),)), pltpu.SemaphoreType.DMA],
        compiler_params=pltpu.CompilerParams(vmem_limit_bytes=56 * MIB),
        cost_estimate=pl.CostEstimate(
            flops=2 * seq * width * cols * 3, bytes_accessed=6 * width * cols, transcendentals=0
        ),
    )(places, *pieces, own_spots, own_docs, docs, cos, sin,
      wq, wk, wv)


def attend_back_kernel(chunk, slots, scale, shift, at_ref, starts_ref, *refs):
    count = len(refs) - 23
    pieces = refs[:count]
    (wo_ref, q_ref, k_ref, v_ref, cos_ref, sin_ref, doc_row_ref, doc_ref,
     x_hbm, wq_hbm, wk_hbm, wv_hbm, mine_ref, theirs_ref, first_ref,
     bb, x_cols, w_cols, acc, every, bb_sem, x_sem, w_sem) = refs[count:]
    step = pl.program_id(0)
    owners = x_cols.shape[0]
    spots = chunk_places(at_ref, 0, count, chunk)
    place_rows(step, pieces, spots, bb, bb_sem, wait=False)
    seq, size, width = bb.shape[0], x_cols.shape[2], w_cols.shape[2]
    starts = [pl.multiple_of(starts_ref[i], HD) for i in range(owners)]
    at = pl.ds(pl.multiple_of(step * width, HD), width)
    copies = [
        pltpu.make_async_copy(x_hbm.at[:, pl.ds(starts[i], size)], x_cols.at[i], x_sem.at[i])
        for i in range(owners)
    ] + [
        pltpu.make_async_copy(w_hbm.at[:, at], w_cols.at[i], w_sem.at[i])
        for i, w_hbm in enumerate((wq_hbm, wk_hbm, wv_hbm))
    ]
    for copy in copies:
        copy.start()

    block = min(256, seq)
    parts = [slice(i * block, (i + 1) * block) for i in range(seq // block)]
    heads = [slice(j * HD, (j + 1) * HD) for j in range(width // HD)]
    weights, attended = {}, []
    for i, part in enumerate(parts):
        shape = (block, part.stop)
        allowed = (
            lax.broadcasted_iota(jnp.int32, shape, 1)
            <= lax.broadcasted_iota(jnp.int32, shape, 0) + part.start
        ) & (doc_ref[part, :] == doc_row_ref[:, : part.stop])
        bias = jnp.where(allowed, shift, NEVER)
        row = []
        for j, cols in enumerate(heads):
            scores = dot_nt(q_ref[part, cols], k_ref[: part.stop, cols]) * scale + bias
            weights[i, j] = jax.nn.sigmoid(scores)
            row.append(dot(weights[i, j].astype(BF), v_ref[: part.stop, cols]).astype(BF))
        attended.append(jnp.concatenate(row, axis=1))
    attended = jnp.concatenate(attended, axis=0)

    place_rows(step, pieces, spots, bb, bb_sem, start=False)
    ab_all = dot_nt(bb[...], wo_ref[...]).astype(BF)
    for j, cols in enumerate(heads):
        key_sums, value_sums = [None] * len(parts), [None] * len(parts)
        for i, part in enumerate(parts):
            ab, weight = ab_all[part, cols], weights[i, j]
            slope = weight - weight * weight
            back = (dot_nt(ab, v_ref[: part.stop, cols]) * slope).astype(BF)
            weight = weight.astype(BF)
            query_back = dot(back, k_ref[: part.stop, cols]) * scale
            every[part, cols] = rope_back_rows(
                query_back, cos_ref[part, :], sin_ref[part, :]
            ).astype(BF)
            for n in range(i + 1):
                key_part = dot_tn(back[:, parts[n]], q_ref[part, cols])
                value_part = dot_tn(weight[:, parts[n]], ab)
                key_sums[n] = key_part if i == n else key_sums[n] + key_part
                value_sums[n] = value_part if i == n else value_sums[n] + value_part
        for n, part in enumerate(parts):
            at_key = slice(width + cols.start, width + cols.stop)
            at_value = slice(2 * width + cols.start, 2 * width + cols.stop)
            every[part, at_key] = rope_back_rows(
                key_sums[n] * scale, cos_ref[part, :], sin_ref[part, :]
            ).astype(BF)
            every[part, at_value] = value_sums[n].astype(BF)

    def give(i, n, part):
        if i == 0:
            mine_ref[n] = part
        else:
            theirs_ref[i - 1, n] = part.astype(BF)

    for i in range(owners):
        give(i, 3, dot_tn(bb[:, pl.ds(starts[i], size)], attended))

    for copy in copies:
        copy.wait()
    for i in range(owners):
        total = dot_tn(x_cols[i], every[...])
        for n in range(3):
            give(i, n, total[:, n * width : (n + 1) * width])
    own = jnp.concatenate([every[spot, :] for spot in spots[:slots]], axis=0)
    first = sum(dot_nt(own[:, n * width : (n + 1) * width], w_cols[n]) for n in range(3))

    @pl.when(step == 0)
    def _():
        acc[...] = first

    @pl.when(step > 0)
    def _():
        acc[...] += first

    @pl.when(step == pl.num_programs(0) - 1)
    def _():
        first_ref[...] = acc[...].astype(BF)


def attend_back(
    places, starts, pieces, wo, q, k, v, cos, sin, docs, doc_column, x_seq, wq, wk, wv,
    size, slots, scale, shift,
):
    seq, width = x_seq.shape
    chunk = pieces[0].shape[0]
    cols = wo.shape[0]
    heads = cols // HD
    step = min(2, heads)
    own = slots * chunk
    owners = starts.shape[0]
    whole = lambda *shape: pl.BlockSpec(
        shape, lambda i: (0,) * len(shape), pipeline_mode=pl.Buffered(1)
    )
    sspec = pl.BlockSpec((seq, step * HD), lambda i: (0, i))
    hbm = pl.BlockSpec(memory_space=pl.ANY)
    return pl.pallas_call(
        functools.partial(attend_back_kernel, chunk, slots, scale, shift),
        grid=(heads // step,),
        in_specs=[pl.BlockSpec(memory_space=pltpu.SMEM)] * 2 + [hbm] * len(pieces)
        + [pl.BlockSpec((step * HD, width), lambda i: (i, 0)),
           sspec, sspec, sspec, whole(seq, HD), whole(seq, HD), whole(1, seq), whole(seq, 1)]
        + [hbm] * 4,
        out_specs=[pl.BlockSpec((4, size, step * HD), lambda i: (0, 0, i)),
                   pl.BlockSpec((owners - 1, 4, size, step * HD), lambda i: (0, 0, 0, i)),
                   whole(own, width)],
        out_shape=[jax.ShapeDtypeStruct((4, size, cols), F32),
                   jax.ShapeDtypeStruct((owners - 1, 4, size, cols), BF),
                   jax.ShapeDtypeStruct((own, width), BF)],
        scratch_shapes=[pltpu.VMEM((seq, width), BF), pltpu.VMEM((owners, seq, size), BF),
                        pltpu.VMEM((3, width, step * HD), BF),
                        pltpu.VMEM((own, width), F32),
                        pltpu.VMEM((seq, 3 * step * HD), BF),
                        pltpu.SemaphoreType.DMA((len(pieces),)),
                        pltpu.SemaphoreType.DMA((owners,)), pltpu.SemaphoreType.DMA((3,))],
        compiler_params=pltpu.CompilerParams(vmem_limit_bytes=56 * MIB),
        cost_estimate=pl.CostEstimate(
            flops=2 * seq * width * cols + 14 * seq * seq * cols,
            bytes_accessed=2 * (seq + cols) * width + 20 * seq * cols,
            transcendentals=seq * seq * heads,
        ),
    )(
        places, starts, *pieces, in_hbm(wo), q, k, v, cos, sin,
        docs, doc_column, in_hbm(x_seq), in_hbm(wq), in_hbm(wk), in_hbm(wv),
    )


def gate_math(gate, up, hidden_back):
    sig = jax.nn.sigmoid(gate)
    act = gate * sig
    hidden = (act * up).astype(BF)
    gate_back = (hidden_back * up * sig * (1.0 + gate * (1.0 - sig))).astype(BF)
    up_back = (hidden_back * act).astype(BF)
    return hidden, gate_back, up_back


def mlp_kernel(x_ref, hb_ref, wg_ref, wu_ref, hidden_ref, back_ref, acc):
    step = pl.program_id(0)
    x, wg, wu = x_ref[...], wg_ref[...], wu_ref[...]
    hidden, gate_back, up_back = gate_math(dot(x, wg), dot(x, wu), hb_ref[...].astype(F32))
    hidden_ref[...] = hidden
    back = dot_nt(gate_back, wg) + dot_nt(up_back, wu)

    @pl.when(step == 0)
    def _():
        acc[...] = back

    @pl.when(step > 0)
    def _():
        acc[...] += back

    @pl.when(step == pl.num_programs(0) - 1)
    def _():
        back_ref[...] = acc[...].astype(BF)


def mlp(x, hidden_back, wg, wu):
    rows, width = x.shape
    units = wg.shape[1]
    block = min(512, units)
    whole = pl.BlockSpec((rows, width), lambda i: (0, 0), pipeline_mode=pl.Buffered(1))
    wspec = pl.BlockSpec((width, block), lambda i: (0, i))
    uspec = pl.BlockSpec((rows, block), lambda i: (0, i))
    return pl.pallas_call(
        mlp_kernel,
        grid=(units // block,),
        in_specs=[whole, uspec, wspec, wspec],
        out_specs=[uspec, whole],
        out_shape=[
            jax.ShapeDtypeStruct((rows, units), BF), jax.ShapeDtypeStruct((rows, width), BF)
        ],
        scratch_shapes=[pltpu.VMEM((rows, width), F32)],
        compiler_params=pltpu.CompilerParams(vmem_limit_bytes=56 * MIB),
        cost_estimate=pl.CostEstimate(
            flops=8 * rows * width * units, bytes_accessed=4 * width * units, transcendentals=0
        ),
    )(x, hidden_back, in_hbm(wg), in_hbm(wu))


def hidden_back_kernel(tile, cot_hbm, wd_ref, out_ref, cot, sem):
    tiles = [pl.ds(i * tile, tile) for i in range(cot.shape[0] // tile)]
    copies = [
        pltpu.make_async_copy(cot_hbm.at[at], cot.at[at], sem.at[i]) for i, at in enumerate(tiles)
    ]

    def every_tile(waits):
        wd = wd_ref[...]
        for copy, at in zip(copies, tiles, strict=True):
            if waits:
                copy.wait()
            out_ref[at, :] = dot_nt(cot[at, :], wd).astype(BF)

    @pl.when(pl.program_id(0) == 0)
    def _():
        for copy in copies:
            copy.start()
        every_tile(True)

    @pl.when(pl.program_id(0) > 0)
    def _():
        every_tile(False)


def hidden_back_of(cot, wd):
    rows, width = cot.shape
    units = wd.shape[0]
    block, tile = min(512, units), 256
    return pl.pallas_call(
        functools.partial(hidden_back_kernel, tile),
        grid=(units // block,),
        in_specs=[pl.BlockSpec(memory_space=pl.ANY),
                  pl.BlockSpec((block, width), lambda i: (i, 0))],
        out_specs=pl.BlockSpec((rows, block), lambda i: (0, i)),
        out_shape=jax.ShapeDtypeStruct((rows, units), BF),
        scratch_shapes=[pltpu.VMEM((rows, width), BF), pltpu.SemaphoreType.DMA((rows // tile,))],
        compiler_params=pltpu.CompilerParams(vmem_limit_bytes=56 * MIB),
        cost_estimate=pl.CostEstimate(
            flops=2 * rows * width * units, bytes_accessed=2 * width * (rows + units),
            transcendentals=0,
        ),
    )(cot, in_hbm(wd))


def mlp_grad_kernel(count, chunk, at_ref, *refs):
    pieces = refs[:count]
    hb_ref, cb_ref, wg_ref, wu_ref = refs[count : count + 4]
    gg_ref, ug_ref, dg_ref, gain_ref, x_all, hid, gbk, ubk, sem = refs[-9:]
    size = cb_ref.shape[1]
    per = pieces[0].shape[0] // chunk
    own = pl.ds(pl.multiple_of(at_ref[0] * size, size), size)

    @pl.when(pl.program_id(0) == 0)
    def _():
        copies = []
        for i in range(count * per):
            spot = pl.ds(pl.multiple_of(at_ref[1 + i] * chunk, chunk), chunk)
            part = pieces[i // per].at[pl.ds(i % per * chunk, chunk)]
            copies.append(pltpu.make_async_copy(part, x_all.at[spot], sem.at[i]))
        for copy in copies:
            copy.start()
        for copy in copies:
            copy.wait()

    wg, wu = wg_ref[...], wu_ref[...]
    for i in range(x_all.shape[0] // 128):
        at = pl.ds(i * 128, 128)
        x = x_all[at, :]
        hid[at, :], gbk[at, :], ubk[at, :] = gate_math(
            dot(x, wg), dot(x, wu), hb_ref[at, :].astype(F32)
        )
    xb = x_all[:, own]
    gate_grad = dot_tn(xb, gbk[...])
    up_grad = dot_tn(xb, ubk[...])
    gg_ref[...] = gate_grad
    ug_ref[...] = up_grad
    dg_ref[...] = dot_tn(hid[...], cb_ref[...])
    gain = jnp.sum(
        wg_ref[own, :].astype(F32) * gate_grad + wu_ref[own, :].astype(F32) * up_grad,
        axis=1, keepdims=True,
    )

    @pl.when(pl.program_id(0) == 0)
    def _():
        gain_ref[...] = gain

    @pl.when(pl.program_id(0) > 0)
    def _():
        gain_ref[...] += gain


def mlp_grad(places, chunk, pieces, cot, hb, wg, wu, size, first, count, before):
    tile, width = pieces[0].shape
    rows, units = hb.shape
    block = min(256, count)
    skip = first // block
    wspec = pl.BlockSpec((width, block), lambda i, at: (0, i + skip))
    hbm = pl.BlockSpec(memory_space=pl.ANY)
    grid_spec = pltpu.PrefetchScalarGridSpec(
        num_scalar_prefetch=1,
        grid=(count // block,),
        in_specs=[hbm] * len(pieces)
        + [pl.BlockSpec((rows, block), lambda i, at: (0, i + skip)),
           pl.BlockSpec((rows, size), lambda i, at: (0, at[0]), pipeline_mode=pl.Buffered(1)),
           wspec, wspec]
        + [hbm] * len(before),
        out_specs=[pl.BlockSpec((size, block), lambda i, at: (0, i + skip))] * 2
        + [pl.BlockSpec((block, size), lambda i, at: (i + skip, 0)),
           pl.BlockSpec((size, 1), lambda i, at: (0, 0))],
        scratch_shapes=[pltpu.VMEM((rows, width), BF)]
        + [pltpu.VMEM((rows, block), BF)] * 3
        + [pltpu.SemaphoreType.DMA((rows // chunk,))],
    )
    return pl.pallas_call(
        functools.partial(mlp_grad_kernel, len(pieces), chunk),
        grid_spec=grid_spec,
        out_shape=[jax.ShapeDtypeStruct((size, units), F32)] * 2
        + [jax.ShapeDtypeStruct((units, size), F32), jax.ShapeDtypeStruct((size, 1), F32)],
        input_output_aliases={len(pieces) + 5 + i: i for i in range(len(before))},
        compiler_params=pltpu.CompilerParams(vmem_limit_bytes=56 * MIB),
        cost_estimate=pl.CostEstimate(
            flops=2 * rows * count * (2 * width + 3 * size),
            bytes_accessed=4 * width * count + 4 * rows * width,
            transcendentals=0,
        ),
    )(places, *pieces, hb, cot, in_hbm(wg), in_hbm(wu), *before)


def row_mean(values):
    return jnp.mean(values, axis=-1, keepdims=True)


def norm_parts(values):
    root = lax.rsqrt(row_mean(values * values) + EPS)
    return values * root, root


def norm_back(upstream, scaled, root, gain):
    inner = upstream * gain
    return root * (inner - scaled * row_mean(inner * scaled))


def per_device(
    activations, cotangent, doc_ids, attn_gain, query_weight, key_weight, value_weight,
    out_weight, mlp_gain, gate_weight, up_weight, down_weight,
):
    rows, width = activations.shape[1:]
    n_dp, n_ctx, n_t = lax.axis_size("dp"), lax.axis_size("ctx"), lax.axis_size("tensor")
    dp, ctx, place = lax.axis_index("dp"), lax.axis_index("ctx"), lax.axis_index("tensor")
    chunk = rows // n_t
    length = rows * n_ctx
    slots = slot_order(n_t)
    scale, shift = HD ** (-0.5), -math.log(length)
    gain_first, gain_second = attn_gain.astype(F32), mlp_gain.astype(F32)

    def slotted(values):
        return jnp.concatenate(
            [lax.dynamic_slice_in_dim(values, (place ^ s) * chunk, chunk, 0) for s in slots], axis=0
        )

    inputs32 = slotted(activations[0]).astype(F32)
    scaled_first, root_first = norm_parts(inputs32)
    normed_first = (scaled_first * gain_first).astype(BF)

    bits = list(reversed(bits_of(n_t)))

    def spread(rings, beside=()):
        lists = [[ring] for ring in rings]
        for bit in bits:
            lists = [items + [swap(item, "tensor", bit) for item in items] for items in lists]
            if bit == bits[0]:
                lists = after(lists, beside)
        return lists

    mine, *rings = ring_of(normed_first[:chunk])
    cot_all = lax.all_gather(
        lax.dynamic_slice_in_dim(after(cotangent[0], normed_first), place * chunk, chunk, 0),
        ("dp", "ctx", "tensor"), axis=0, tiled=True,
    )

    ring_at = (ctx - jnp.arange(n_ctx, dtype=jnp.int32) + n_ctx) % n_ctx
    seq_places = jnp.concatenate([
        ring_at[k : k + 1] * n_t + (place ^ slot) for k in range(n_ctx) for slot in slots
    ])
    docs = doc_ids
    doc_column = doc_ids.reshape(length, 1)
    out_cols = width // (n_dp * n_ctx)
    owners = jnp.stack([((dp + step) % n_dp) * n_ctx + ctx for step in range(n_dp)])
    starts = owners * out_cols
    owner = owners[0]
    places = [owner[None]]
    for flip in (0, 1):
        for step in range(n_dp):
            for slot in slots[: n_t // 2]:
                group = ((dp - step + n_dp) % n_dp) * n_ctx + ring_at
                places.append(group * n_t + (place ^ slot ^ flip))
    places = jnp.concatenate(places)
    own_spots = slotted(ctx * rows + jnp.arange(rows, dtype=jnp.int32)[:, None])
    own_docs = slotted(
        lax.dynamic_slice_in_dim(doc_ids.reshape(length, 1), ctx * rows, rows, 0)
    )
    frequency = np.float32(10000.0) ** (
        -np.arange(HD // 2, dtype=np.float32) * np.float32(2.0) / np.float32(HD)
    )
    angles = np.arange(length, dtype=np.float32)[:, None] * frequency[None, :]
    cos = jnp.asarray(np.concatenate([np.cos(angles), np.cos(angles)], axis=1))
    sin = jnp.asarray(np.concatenate([-np.sin(angles), np.sin(angles)], axis=1))
    cot = slotted(cotangent[0])
    rings = after(rings, seq_places, own_spots, own_docs, cot, starts, places, doc_column)
    hidden_back = lax.dot_general(
        after(cot, rings), down_weight, (((1,), (1,)), ((), ())), preferred_element_type=F32
    ).astype(BF)
    seq_pieces = spread(rings, hidden_back)
    own_pieces = [normed_first[i * chunk : (i + 1) * chunk] for i in range(n_t)]
    q, k, v, attended, mass, x_seq = attend(
        seq_places, own_pieces + sum(seq_pieces, []), own_spots, own_docs, docs, cos, sin,
        query_weight, key_weight, value_weight, n_t, scale, shift,
    )
    attn_mass = from_slots(mass[:, :, 0].T, slots, place)

    def over_dp(items):
        return [turn(item, "dp", step) for step in range(1, n_dp) for item in items]

    def over_tensor(items, bits):
        for bit in bits:
            items = items + [swap(item, "tensor", bit) for item in items]
        return items

    branch = scatter_tensor(
        jnp.dot(attended, out_weight, preferred_element_type=F32).astype(BF), attn_mass
    )
    middle = inputs32[:chunk] + branch
    scaled_second, root_second = norm_parts(middle)
    normed_chunk = (scaled_second * gain_second).astype(BF)
    normed_second = gather_tensor(normed_chunk)
    chunk_rings = ring_of(normed_chunk)
    hidden, second_part = mlp(normed_second, hidden_back, gate_weight, up_weight)
    second_part, chunk_rings = lax.optimization_barrier((second_part, chunk_rings))
    x_near = [jnp.concatenate(chunk_rings, axis=0)]
    x_far = over_dp(x_near)
    x_near_more = over_tensor(x_near, bits[:-1])[1:]
    second_back = scatter_tensor(second_part)
    middle_back = cot[:chunk].astype(F32) + norm_back(
        second_back, scaled_second, root_second, gain_second
    )
    branch_back = middle_back.astype(BF)
    bb_rings = ring_of(branch_back)
    hidden_back_all = hidden_back_of(after(cot_all, branch_back), down_weight)
    bb_rings, x_far, x_near_more = after((bb_rings, x_far, x_near_more), hidden_back_all)
    mlp_part = jnp.dot(
        after(hidden, bb_rings), down_weight, preferred_element_type=F32
    ).astype(BF)
    bb_pieces = spread(bb_rings, mlp_part)
    x_far_more = over_tensor(x_far, bits[:-1])[len(x_far) :]

    mine_grads, theirs_grads, first_part = attend_back(
        seq_places, starts, sum(bb_pieces, []), out_weight, q, k, v, cos, sin, docs, doc_column,
        x_seq, query_weight, key_weight, value_weight, out_cols, n_t, scale, shift,
    )

    theirs = [turn(theirs_grads[step - 1], "dp", step) for step in range(1, n_dp)]

    x_pieces = over_tensor(x_near + x_near_more + x_far + x_far_more, bits[-1:])

    gate_grad, up_grad, down_grad, mlp_gain_sum = mlp_grad(
        after(places, first_part), chunk, x_pieces, cot_all, hidden_back_all,
        gate_weight, up_weight, out_cols, 0, gate_weight.shape[1], (),
    )
    mlp_gain_sum = mlp_gain_sum[:, 0]
    theirs = after(theirs, gate_grad)
    both = scatter_tensor(jnp.concatenate([first_part, mlp_part], axis=1), gate_grad)
    first_back, mlp_out = both[:, :width], both[:, width:]
    scaled_chunk, root_chunk = scaled_first[:chunk], root_first[:chunk]
    input_grad = (
        middle_back + norm_back(first_back, scaled_chunk, root_chunk, gain_first)
    ).astype(BF)
    layer_out = (middle + mlp_out).astype(BF)
    results = gather_tensor(jnp.concatenate([layer_out, input_grad], axis=1))
    results = from_slots(results, slots, place)
    layer_out, input_grad = results[:, :width], results[:, width:]
    attn_grads = mine_grads + sum(part.astype(F32) for part in theirs)
    query_grad, key_grad, value_grad = attn_grads[0], attn_grads[1], attn_grads[2]
    out_grad = attn_grads[3].T

    def rows_of(weight):
        return lax.dynamic_slice_in_dim(weight, owner * out_cols, out_cols, 0).astype(F32)

    attn_gain_sum = jnp.sum(
        rows_of(query_weight) * query_grad + rows_of(key_weight) * key_grad
        + rows_of(value_weight) * value_grad, axis=1,
    )
    gains = jnp.stack([attn_gain_sum, mlp_gain_sum])
    for bit in bits_of(n_t):
        gains = gains + swap(gains, "tensor", bit)
    gain_grads = gains / lax.dynamic_slice_in_dim(
        jnp.stack([gain_first, gain_second]), owner * out_cols, out_cols, 1
    )

    return (
        layer_out[None], input_grad[None], gain_grads[0], query_grad, key_grad, value_grad,
        out_grad, gain_grads[1], gate_grad, up_grad, down_grad, attn_mass[None],
    )


def solution(mesh):
    return jax.shard_map(
        per_device,
        mesh=mesh,
        in_specs=(
            P("dp", "ctx", None),
            P("dp", "ctx", None),
            P("dp", None),
            P(),
            P(None, "tensor"),
            P(None, "tensor"),
            P(None, "tensor"),
            P("tensor", None),
            P(),
            P(None, "tensor"),
            P(None, "tensor"),
            P("tensor", None),
        ),
        out_specs=(
            P("dp", "ctx", None),
            P("dp", "ctx", None),
            P(("dp", "ctx")),
            P(("dp", "ctx"), "tensor"),
            P(("dp", "ctx"), "tensor"),
            P(("dp", "ctx"), "tensor"),
            P("tensor", ("dp", "ctx")),
            P(("dp", "ctx")),
            P(("dp", "ctx"), "tensor"),
            P(("dp", "ctx"), "tensor"),
            P("tensor", ("dp", "ctx")),
            P("dp", "ctx", "tensor"),
        ),
        check_vma=False,
    )
```

time: 316 us -> 213 us (0.67)
  waiting for transfers between devices: 91.5 us -> 27 us
  local copies, waits for them, and re-layouts: 39.3 us -> 17.1 us
  between operations: 1.65 us -> 17.6 us
  starting transfers between devices: 56.4 us -> 41.5 us
  Pallas kernels: 95.8 us -> 83.5 us
  other arithmetic: 18.6 us -> 12.9 us
    ppermute x23 -> x39, waiting for transfers between devices: 61 us -> 26.6 us  [swap(): return lax.ppermute(values, axis, [(i, i ^ distance) for i in range(count)])]
    ppermute x23 -> x11, waiting for transfers between devices: 30.6 us -> 0.43 us  [turn(): lax.ppermute(values, axis, [(i, (i + shift) % count) for i in range(count)])]
    ppermute x23 -> x11, starting transfers between devices: 40.6 us -> 20.5 us  [turn(): lax.ppermute(values, axis, [(i, (i + shift) % count) for i in range(count)])]
    unnamed x104 -> x94, local copies, waits for them, and re-layouts: 19.1 us -> 5.7 us
    pallas_call x7 -> x5, Pallas kernels: 95.8 us -> 83.5 us  [the longest x1 30.5 us: mlp_grad(): pl.pallas_call(functools.partial(mlp_grad_kernel, len(pieces), chunk), gr...]
    ppermute x23 -> x39, starting transfers between devices: 15.8 us -> 21 us  [swap(): return lax.ppermute(values, axis, [(i, i ^ distance) for i in range(count)])]
    add x7 -> x6, other arithmetic: 4.73 us -> 0.4 us  [the longest x1 0.36 us: per_device(): attn_grads = mine_grads + sum((part.astype(F32) for part in theirs))]
    concatenate x9 -> x5, local copies, waits for them, and re-layouts: 6.69 us -> 2.68 us  [the longest x2 1.45 us: slotted(): jnp.concatenate([lax.dynamic_slice_in_dim(values, (place ^ s) * chunk, ch...]
  transfers between devices with their start and end apart: 46 -> 51, of which waited for: 16 -> 15; matrix products, arithmetic and copies ran while one was open for 18% -> 16% of each run, Pallas kernels for 12% -> 39%
where the time goes in v2:
time: 213 us
  Pallas kernels  83.5 us (39%)
  starting transfers between devices  41.5 us (19%)
  waiting for transfers between devices  27 us (13%)
  between operations  17.6 us (8%)
  local copies, waits for them, and re-layouts  17.1 us (8%)
  matrix products  13.1 us (6%)
  other arithmetic  12.9 us (6%)
    pallas_call x1, Pallas kernels, mlp_grad(): pl.pallas_call(functools.partial(mlp_grad_kernel, len(pieces), chunk), gr...  30.5 us
    ppermute x39, waiting for transfers between devices, swap(): return lax.ppermute(values, axis, [(i, i ^ distance) for i in range(count)])  26.6 us
    ppermute x39, starting transfers between devices, swap(): return lax.ppermute(values, axis, [(i, i ^ distance) for i in range(count)])  21 us
    ppermute x11, starting transfers between devices, turn(): lax.ppermute(values, axis, [(i, (i + shift) % count) for i in range(count)])  20.5 us
    pallas_call x1, Pallas kernels, attend_back(): pl.pallas_call(functools.partial(attend_back_kernel, chunk, slots, scale,...  15.8 us
    pallas_call x1, Pallas kernels, hidden_back_of(): pl.pallas_call(functools.partial(hidden_back_kernel, tile), grid=(units /...  14.2 us
    pallas_call x1, Pallas kernels, mlp(): pl.pallas_call(mlp_kernel, grid=(units // block,), in_specs=[whole, uspec...  12.8 us
    pallas_call x1, Pallas kernels, attend(): pl.pallas_call(functools.partial(attend_kernel, chunk, slots, scale, shif...  10.1 us
  transfers between devices with their start and end apart: 51, of which 15 were waited for; matrix products, arithmetic and copies ran while one was open for 16% of the time, Pallas kernels for 39%

profile of v2, /device:TPU:0, one launch (start us, length us, event | category | flops | bytes accessed | tf_op | source)
XLA Modules:
  0.0 212.6 jit_solution(3096826807816259869)
XLA Ops:
  10.3 3.0 %collective-permute-start = (bf16[32,2048]{1,0:T(8,128)(2,1)S(1)}, bf16[32,2048]{1,0:T(8,128)(2,1)S(1)}, u32[]{:S(2)}, u32[]{:S(2)}) collective-permute-start(bf16[32,2048]{1,0:T(8,128)(2,1)S(1)} %get-tuple-element.175.refs_0_), channel_id=1, source_target_pairs={{0,4},{4,8},{8,12},{12,0},{1,5},{5,9},{9,13},{13,1},{2,6},{6,10},{... | collective-permute-start | bytes 393224 | tf_op jit(solution)/shard_map/ppermute | solution.py:26
  13.3 2.6 %collective-permute-start.1 = (bf16[32,2048]{1,0:T(8,128)(2,1)S(1)}, bf16[32,2048]{1,0:T(8,128)(2,1)S(1)}, u32[]{:S(2)}, u32[]{:S(2)}) collective-permute-start(bf16[32,2048]{1,0:T(8,128)(2,1)S(1)} %get-tuple-element.175.refs_0_), channel_id=1, source_target_pairs={{0,8},{4,12},{8,0},{12,4},{1,9},{5,13},{9,1},{13,5},{2,10},{6,14},... | collective-permute-start | bytes 393224 | tf_op jit(solution)/shard_map/ppermute | solution.py:26
  15.9 1.3 collective-permute-start.2
  24.5 1.6 collective-permute-start.3
  26.6 1.5 collective-permute-start.5
  28.1 7.1 %convolution_convert_fusion.1.hb_ref = bf16[128,2048]{1,0:T(8,128)(2,1)} fusion(bf16[128,2048]{1,0:T(8,128)(2,1)S(1)} %pad_maximum_fusion.1, bf16[2048,2048]{1,0:T(8,128)(2,1)} %wd_ref.1), kind=kOutput, calls=%fused_computation.1 | convolution fusion | flops 1074003968 | bytes 9437184 | tf_op jit(solution)/shard_map/dot_general | solution.py:608
  40.4 10.1 %shard_map.229 = (bf16[512,512]{1,0:T(8,128)(2,1)}, bf16[512,512]{1,0:T(8,128)(2,1)}, bf16[512,512]{1,0:T(8,128)(2,1)}, bf16[128,512]{1,0:T(8,128)(2,1)}, f32[4,...) custom-call(s32[16]{0:T(128)} %concatenate.38.at_ref, bf16[32,2048]{1,0:T(8,128)(2,1)} %copy-done.22, ...), custom_call_target="tpu_custom_call" | custom-call | flops 3221225472 | bytes 6291456 | tf_op jit(solution)/shard_map/pallas_call | solution.py:178
  50.6 1.4 convolution_convert_fusion.2
  57.1 3.4 %collective-permute-done.13 = bf16[32,2048]{1,0:T(8,128)(2,1)S(1)} collective-permute-done((bf16[32,2048]{1,0:T(8,128)(2,1)S(1)}, bf16[32,2048]{1,0:T(8,128)(2,1)S(1)}, u32[]{:S(2)}, u32[]{:S(2)}) %collective-permute-start.13) | collective-permute-done | bytes 131104 | tf_op jit(solution)/shard_map/ppermute | solution.py:21
  61.8 7.7 %collective-permute-done.14 = bf16[32,2048]{1,0:T(8,128)(2,1)S(1)} collective-permute-done((bf16[32,2048]{1,0:T(8,128)(2,1)S(1)}, bf16[32,2048]{1,0:T(8,128)(2,1)S(1)}, u32[]{:S(2)}, u32[]{:S(2)}) %collective-permute-start.14) | collective-permute-done | bytes 131104 | tf_op jit(solution)/shard_map/ppermute | solution.py:21
  69.6 2.7 %collective-permute-start.16 = (bf16[32,2048]{1,0:T(8,128)(2,1)S(1)}, bf16[32,2048]{1,0:T(8,128)(2,1)S(1)}, u32[]{:S(2)}, u32[]{:S(2)}) collective-permute-start(bf16[32,2048]{1,0:T(8,128)(2,1)S(1)} %multiply_convert_fusion.1), channel_id=1, source_target_pairs={{0,4},{4,8},{8,12},{12,0},{1,5},{5,9},{9,13},{13,1},{2,6},{6,10},{... | collective-permute-start | bytes 393224 | tf_op jit(solution)/shard_map/ppermute | solution.py:26
  72.3 1.3 collective-permute-start.17
  75.7 12.8 %shard_map.230 = (bf16[128,2048]{1,0:T(8,128)(2,1)}, bf16[128,2048]{1,0:T(8,128)(2,1)}) custom-call(bf16[128,2048]{1,0:T(8,128)(2,1)} %pad_maximum_fusion.2.x_ref, bf16[128,2048]{1,0:T(8,128)(2,1)} %convolution_convert_fusion.1.hb_ref, bf16[2048,2048]{1,0:T(8,128)(2,1)} %refs_10_.1, bf16[2048,2048]{1,0:T(8,128)(2,1)} %refs_11_.1), custom_call_target="tpu_custom_call" | custom-call | flops 4294967296 | bytes 16777216 | tf_op jit(solution)/shard_map/pallas_call | solution.py:383
  89.7 1.5 collective-permute-done.19
  92.2 1.8 collective-permute-start.20
  94.1 1.5 collective-permute-start.24
  95.9 2.0 collective-permute-done.20
  98.3 2.7 %collective-permute-start.21 = (bf16[32,2048]{1,0:T(8,128)(2,1)S(1)}, bf16[32,2048]{1,0:T(8,128)(2,1)S(1)}, u32[]{:S(2)}, u32[]{:S(2)}) collective-permute-start(bf16[32,2048]{1,0:T(8,128)(2,1)S(1)} %get-tuple-element.90.refs_0_), channel_id=1, source_target_pairs={{0,4},{4,8},{8,12},{12,0},{1,5},{5,9},{9,13},{13,1},{2,6},{6,10},{... | collective-permute-start | bytes 393224 | tf_op jit(solution)/shard_map/ppermute | solution.py:26
  102.0 1.5 collective-permute-start.23
  103.4 14.2 %shard_map.231.refs_8_ = bf16[1024,2048]{1,0:T(8,128)(2,1)} custom-call(bf16[1024,2048]{1,0:T(8,128)(2,1)} %all-gather.2.cloned.1.call-done.cot_hbm.refs_9_, bf16[2048,2048]{1,0:T(8,128)(2,1)} %wd_ref.1), custom_call_target="tpu_custom_call" | custom-call | flops 8589934592 | bytes 12582912 | tf_op jit(solution)/shard_map/pallas_call | solution.py:427
  117.7 1.3 collective-permute-start.26
  121.9 4.6 %convolution_convert_fusion = bf16[128,2048]{1,0:T(8,128)(2,1)S(1)} fusion(bf16[128,2048]{1,0:T(8,128)(2,1)S(1)} %copy-done.4, bf16[2048,2048]{1,0:T(8,128)(2,1)} %wd_ref.1), kind=kOutput, calls=%fused_computation | convolution fusion | flops 1074003968 | bytes 9437184 | tf_op jit(solution)/shard_map/dot_general | solution.py:648
  127.0 1.4 collective-permute-done.28.refs_9_
  128.4 1.5 collective-permute-done.29.refs_13_
  132.1 1.5 copy.39.refs_23_
  135.3 15.8 %shard_map.232 = (f32[4,256,512]{2,1,0:T(8,128)}, bf16[1,4,256,512]{3,2,1,0:T(8,128)(2,1)}, bf16[128,2048]{1,0:T(8,128)(2,1)}) custom-call(s32[16]{0:T(128)} %concatenate.38.at_ref, s32[2]{0:T(128)} %add_multiply_fusion.starts_ref, bf16[32,2048]{1,0:T(8,128)(2,1)} %copy-done.8, bf16[32,2048]{1,0:T(8,128)(2,1)} %copy-done.13, bf16[32,2048]{1,0:T(8,128)(2,1)} %copy-done.16, ...), custom_call_target="tpu_custom_call" | custom-call | flops 2952790016 | bytes 9437184 | tf_op jit(solution)/shard_map/pallas_call | solution.py:316
  151.2 1.8 pad_maximum_fusion
  154.0 1.5 collective-permute-start.47
  159.8 30.5 %shard_map.233 = (f32[256,2048]{1,0:T(8,128)}, f32[256,2048]{1,0:T(8,128)}, f32[2048,256]{1,0:T(8,128)}, f32[256,1]{1,0:T(8,128)}) custom-call(s32[33]{0:T(128)} %concatenate.42.at_ref, bf16[128,2048]{1,0:T(8,128)(2,1)} %copy-done.23, bf16[128,2048]{1,0:T(8,128)(2,1)} %collective-permute-done.25.refs_1_, bf16[128,2048]{1,0:T(8,128)(2,1)} %collective-permute-done.24.refs_2_, ...), custom_call_target="tpu_custom_call" | custom-call | flops 20401094656 | bytes 25165824 | tf_op jit(solution)/shard_map/pallas_call | solution.py:512
  193.5 2.4 %add_reduce_fusion = (f32[256]{0:T(256)S(1)}, f32[256,512]{1,0:T(8,128)}, f32[256,512]{1,0:T(8,128)}, f32[256,512]{1,0:T(8,128)}) fusion(bf16[2048,512]{1,0:T(8,128)(2,1)} %refs_27_.1, s32[]{:T(128)S(6)} %select_n.101, bf16[2048,512]{1,0:T(8,128)(2,1)} %refs_26_.1, bf16[2048,512]{1,0:T(8,128)(2,1)} %refs_25_.1, f32[4,256,512]{2,1,0:T(8,128)S(1)} %convert_add_fusion), kind=kLoop, calls=%fused_computation.23 | loop fusion | flops 1179392 | bytes 3933188 | tf_op jit(solution)/shard_map/reduce_sum | solution.py:686
  197.1 3.1 %collective-permute-done.45 = bf16[32,4096]{1,0:T(8,128)(2,1)S(1)} collective-permute-done((bf16[32,4096]{1,0:T(8,128)(2,1)S(1)}, bf16[32,4096]{1,0:T(8,128)(2,1)S(1)}, u32[]{:S(2)}, u32[]{:S(2)}) %collective-permute-start.45) | collective-permute-done | bytes 262176 | tf_op jit(solution)/shard_map/ppermute | solution.py:21
  201.4 2.5 %collective-permute-done.49 = f32[2,256]{1,0:T(2,128)S(1)} collective-permute-done((f32[2,256]{1,0:T(2,128)S(1)}, f32[2,256]{1,0:T(2,128)S(1)}, u32[]{:S(2)}, u32[]{:S(2)}) %collective-permute-start.49) | collective-permute-done | bytes 2080 | tf_op jit(solution)/shard_map/ppermute | solution.py:21
  (243 shorter events, 45.2 us)
Async XLA Ops:
  7.2 96.3 %all-gather.2.cloned.1.call-start = ((), (), s32[]{:S(2)}) async-start(), calls=%async_computation | async-start | bytes 4325376 | tf_op jit(solution)/shard_map/all_gather | solution.py:574
  10.3 13.8 %collective-permute-start = (bf16[32,2048]{1,0:T(8,128)(2,1)S(1)}, bf16[32,2048]{1,0:T(8,128)(2,1)S(1)}, u32[]{:S(2)}, u32[]{:S(2)}) collective-permute-start(bf16[32,2048]{1,0:T(8,128)(2,1)S(1)} %get-tuple-element.175.refs_0_), channel_id=1, source_target_pairs={{0,4},{4,8},{8,12},{12,0},{1,5},{5,9},{9,13},{13,1},{2,6},{6,10},{... | collective-permute-start | bytes 393224 | tf_op jit(solution)/shard_map/ppermute | solution.py:26
  13.3 11.2 %collective-permute-start.1 = (bf16[32,2048]{1,0:T(8,128)(2,1)S(1)}, bf16[32,2048]{1,0:T(8,128)(2,1)S(1)}, u32[]{:S(2)}, u32[]{:S(2)}) collective-permute-start(bf16[32,2048]{1,0:T(8,128)(2,1)S(1)} %get-tuple-element.175.refs_0_), channel_id=1, source_target_pairs={{0,8},{4,12},{8,0},{12,4},{1,9},{5,13},{9,1},{13,5},{2,10},{6,14},... | collective-permute-start | bytes 393224 | tf_op jit(solution)/shard_map/ppermute | solution.py:26
  15.9 8.6 %collective-permute-start.2 = (bf16[32,2048]{1,0:T(8,128)(2,1)S(1)}, bf16[32,2048]{1,0:T(8,128)(2,1)S(1)}, u32[]{:S(2)}, u32[]{:S(2)}) collective-permute-start(bf16[32,2048]{1,0:T(8,128)(2,1)S(1)} %get-tuple-element.175.refs_0_), channel_id=1, source_target_pairs={{0,12},{4,0},{8,4},{12,8},{1,13},{5,1},{9,5},{13,9},{2,14},{6,2},{... | collective-permute-start | bytes 393224 | tf_op jit(solution)/shard_map/ppermute | solution.py:26
  24.5 10.7 %collective-permute-start.3 = (bf16[32,2048]{1,0:T(8,128)(2,1)S(1)}, bf16[32,2048]{1,0:T(8,128)(2,1)S(1)}, u32[]{:S(2)}, u32[]{:S(2)}) collective-permute-start(bf16[32,2048]{1,0:T(8,128)(2,1)S(1)} %collective-permute-done.refs_4_), channel_id=1, source_target_pairs={{0,2},{1,3},{2,0},{3,1},{4,6},{5,7},{6,4},{7,5},{8,10},{9,11},{10,... | collective-permute-start | bytes 393224 | tf_op jit(solution)/shard_map/ppermute | solution.py:21
  26.1 9.1 %collective-permute-start.4 = (bf16[32,2048]{1,0:T(8,128)(2,1)S(1)}, bf16[32,2048]{1,0:T(8,128)(2,1)S(1)}, u32[]{:S(2)}, u32[]{:S(2)}) collective-permute-start(bf16[32,2048]{1,0:T(8,128)(2,1)S(1)} %collective-permute-done.1.refs_8_), channel_id=1, source_target_pairs={{0,2},{1,3},{2,0},{3,1},{4,6},{5,7},{6,4},{7,5},{8,10},{9,11},{10,... | collective-permute-start | bytes 393224 | tf_op jit(solution)/shard_map/ppermute | solution.py:21
  26.6 9.9 %collective-permute-start.5 = (bf16[32,2048]{1,0:T(8,128)(2,1)S(1)}, bf16[32,2048]{1,0:T(8,128)(2,1)S(1)}, u32[]{:S(2)}, u32[]{:S(2)}) collective-permute-start(bf16[32,2048]{1,0:T(8,128)(2,1)S(1)} %collective-permute-done.2.refs_12_), channel_id=1, source_target_pairs={{0,2},{1,3},{2,0},{3,1},{4,6},{5,7},{6,4},{7,5},{8,10},{9,11},{10,... | collective-permute-start | bytes 393224 | tf_op jit(solution)/shard_map/ppermute | solution.py:21
  54.8 5.8 %collective-permute-start.13 = (bf16[32,2048]{1,0:T(8,128)(2,1)S(1)}, bf16[32,2048]{1,0:T(8,128)(2,1)S(1)}, u32[]{:S(2)}, u32[]{:S(2)}) collective-permute-start(bf16[32,2048]{1,0:T(8,128)(2,1)S(1)} %slice.246), channel_id=1, source_target_pairs={{0,2},{1,3},{2,0},{3,1},{4,6},{5,7},{6,4},{7,5},{8,10},{9,11},{10,... | collective-permute-start | bytes 393224 | tf_op jit(solution)/shard_map/ppermute | solution.py:21
  60.8 8.6 %collective-permute-start.14 = (bf16[32,2048]{1,0:T(8,128)(2,1)S(1)}, bf16[32,2048]{1,0:T(8,128)(2,1)S(1)}, u32[]{:S(2)}, u32[]{:S(2)}) collective-permute-start(bf16[32,2048]{1,0:T(8,128)(2,1)S(1)} %multiply_convert_fusion.1), channel_id=1, source_target_pairs={{0,2},{1,3},{2,0},{3,1},{4,6},{5,7},{6,4},{7,5},{8,10},{9,11},{10,... | collective-permute-start | bytes 393224 | tf_op jit(solution)/shard_map/ppermute | solution.py:21
  69.5 5.3 %collective-permute-start.15 = (bf16[64,2048]{1,0:T(8,128)(2,1)S(1)}, bf16[64,2048]{1,0:T(8,128)(2,1)S(1)}, u32[]{:S(2)}, u32[]{:S(2)}) collective-permute-start(bf16[64,2048]{1,0:T(8,128)(2,1)S(1)} %pad_maximum_fusion.4), channel_id=1, source_target_pairs={{0,1},{1,0},{2,3},{3,2},{4,5},{5,4},{6,7},{7,6},{8,9},{9,8},{10,11... | collective-permute-start | bytes 786440 | tf_op jit(solution)/shard_map/ppermute | solution.py:21
  69.6 19.0 %collective-permute-start.16 = (bf16[32,2048]{1,0:T(8,128)(2,1)S(1)}, bf16[32,2048]{1,0:T(8,128)(2,1)S(1)}, u32[]{:S(2)}, u32[]{:S(2)}) collective-permute-start(bf16[32,2048]{1,0:T(8,128)(2,1)S(1)} %multiply_convert_fusion.1), channel_id=1, source_target_pairs={{0,4},{4,8},{8,12},{12,0},{1,5},{5,9},{9,13},{13,1},{2,6},{6,10},{... | collective-permute-start | bytes 393224 | tf_op jit(solution)/shard_map/ppermute | solution.py:26
  72.3 16.2 %collective-permute-start.17 = (bf16[32,2048]{1,0:T(8,128)(2,1)S(1)}, bf16[32,2048]{1,0:T(8,128)(2,1)S(1)}, u32[]{:S(2)}, u32[]{:S(2)}) collective-permute-start(bf16[32,2048]{1,0:T(8,128)(2,1)S(1)} %multiply_convert_fusion.1), channel_id=1, source_target_pairs={{0,8},{4,12},{8,0},{12,4},{1,9},{5,13},{9,1},{13,5},{2,10},{6,14},... | collective-permute-start | bytes 393224 | tf_op jit(solution)/shard_map/ppermute | solution.py:26
  73.6 15.0 %collective-permute-start.18 = (bf16[32,2048]{1,0:T(8,128)(2,1)S(1)}, bf16[32,2048]{1,0:T(8,128)(2,1)S(1)}, u32[]{:S(2)}, u32[]{:S(2)}) collective-permute-start(bf16[32,2048]{1,0:T(8,128)(2,1)S(1)} %multiply_convert_fusion.1), channel_id=1, source_target_pairs={{0,12},{4,0},{8,4},{12,8},{1,13},{5,1},{9,5},{13,9},{2,14},{6,2},{... | collective-permute-start | bytes 393224 | tf_op jit(solution)/shard_map/ppermute | solution.py:26
  92.2 5.7 %collective-permute-start.20 = (bf16[32,2048]{1,0:T(8,128)(2,1)S(1)}, bf16[32,2048]{1,0:T(8,128)(2,1)S(1)}, u32[]{:S(2)}, u32[]{:S(2)}) collective-permute-start(bf16[32,2048]{1,0:T(8,128)(2,1)S(1)} %slice.245), channel_id=1, source_target_pairs={{0,2},{1,3},{2,0},{3,1},{4,6},{5,7},{6,4},{7,5},{8,10},{9,11},{10,... | collective-permute-start | bytes 393224 | tf_op jit(solution)/shard_map/ppermute | solution.py:21
  94.1 23.6 %collective-permute-start.24 = (bf16[128,2048]{1,0:T(8,128)(2,1)S(1)}, bf16[128,2048]{1,0:T(8,128)(2,1)}, u32[]{:S(2)}, u32[]{:S(2)}) collective-permute-start(bf16[128,2048]{1,0:T(8,128)(2,1)S(1)} %constant_dynamic-update-slice_fusion.refs_0_), channel_id=1, source_target_pairs={{0,16},{16,0},{1,17},{17,1},{2,18},{18,2},{3,19},{19,3},{4,20},{20... | collective-permute-start | bytes 1572872 | tf_op jit(solution)/shard_map/ppermute | solution.py:26
  95.6 22.1 %collective-permute-start.25 = (bf16[128,2048]{1,0:T(8,128)(2,1)S(1)}, bf16[128,2048]{1,0:T(8,128)(2,1)}, u32[]{:S(2)}, u32[]{:S(2)}) collective-permute-start(bf16[128,2048]{1,0:T(8,128)(2,1)S(1)} %constant_dynamic-update-slice_fusion.refs_0_), channel_id=1, source_target_pairs={{0,2},{1,3},{2,0},{3,1},{4,6},{5,7},{6,4},{7,5},{8,10},{9,11},{10,... | collective-permute-start | bytes 1572872 | tf_op jit(solution)/shard_map/ppermute | solution.py:21
  98.3 19.4 %collective-permute-start.21 = (bf16[32,2048]{1,0:T(8,128)(2,1)S(1)}, bf16[32,2048]{1,0:T(8,128)(2,1)S(1)}, u32[]{:S(2)}, u32[]{:S(2)}) collective-permute-start(bf16[32,2048]{1,0:T(8,128)(2,1)S(1)} %get-tuple-element.90.refs_0_), channel_id=1, source_target_pairs={{0,4},{4,8},{8,12},{12,0},{1,5},{5,9},{9,13},{13,1},{2,6},{6,10},{... | collective-permute-start | bytes 393224 | tf_op jit(solution)/shard_map/ppermute | solution.py:26
  101.0 16.7 %collective-permute-start.22 = (bf16[32,2048]{1,0:T(8,128)(2,1)S(1)}, bf16[32,2048]{1,0:T(8,128)(2,1)S(1)}, u32[]{:S(2)}, u32[]{:S(2)}) collective-permute-start(bf16[32,2048]{1,0:T(8,128)(2,1)S(1)} %get-tuple-element.90.refs_0_), channel_id=1, source_target_pairs={{0,8},{4,12},{8,0},{12,4},{1,9},{5,13},{9,1},{13,5},{2,10},{6,14},... | collective-permute-start | bytes 393224 | tf_op jit(solution)/shard_map/ppermute | solution.py:26
  102.0 15.8 %collective-permute-start.23 = (bf16[32,2048]{1,0:T(8,128)(2,1)S(1)}, bf16[32,2048]{1,0:T(8,128)(2,1)S(1)}, u32[]{:S(2)}, u32[]{:S(2)}) collective-permute-start(bf16[32,2048]{1,0:T(8,128)(2,1)S(1)} %get-tuple-element.90.refs_0_), channel_id=1, source_target_pairs={{0,12},{4,0},{8,4},{12,8},{1,13},{5,1},{9,5},{13,9},{2,14},{6,2},{... | collective-permute-start | bytes 393224 | tf_op jit(solution)/shard_map/ppermute | solution.py:26
  117.7 8.8 %collective-permute-start.26 = (bf16[32,2048]{1,0:T(8,128)(2,1)S(1)}, bf16[32,2048]{1,0:T(8,128)(2,1)S(1)}, u32[]{:S(2)}, u32[]{:S(2)}) collective-permute-start(bf16[32,2048]{1,0:T(8,128)(2,1)S(1)} %get-tuple-element.90.refs_0_), channel_id=1, source_target_pairs={{0,2},{1,3},{2,0},{3,1},{4,6},{5,7},{6,4},{7,5},{8,10},{9,11},{10,... | collective-permute-start | bytes 393224 | tf_op jit(solution)/shard_map/ppermute | solution.py:21
  119.0 8.0 %collective-permute-start.27 = (bf16[32,2048]{1,0:T(8,128)(2,1)S(1)}, bf16[32,2048]{1,0:T(8,128)(2,1)S(1)}, u32[]{:S(2)}, u32[]{:S(2)}) collective-permute-start(bf16[32,2048]{1,0:T(8,128)(2,1)S(1)} %collective-permute-done.21.refs_4_), channel_id=1, source_target_pairs={{0,2},{1,3},{2,0},{3,1},{4,6},{5,7},{6,4},{7,5},{8,10},{9,11},{10,... | collective-permute-start | bytes 393224 | tf_op jit(solution)/shard_map/ppermute | solution.py:21
  119.8 8.6 %collective-permute-start.28 = (bf16[32,2048]{1,0:T(8,128)(2,1)S(1)}, bf16[32,2048]{1,0:T(8,128)(2,1)S(1)}, u32[]{:S(2)}, u32[]{:S(2)}) collective-permute-start(bf16[32,2048]{1,0:T(8,128)(2,1)S(1)} %collective-permute-done.22.refs_8_), channel_id=1, source_target_pairs={{0,2},{1,3},{2,0},{3,1},{4,6},{5,7},{6,4},{7,5},{8,10},{9,11},{10,... | collective-permute-start | bytes 393224 | tf_op jit(solution)/shard_map/ppermute | solution.py:21
  121.0 8.9 %collective-permute-start.29 = (bf16[32,2048]{1,0:T(8,128)(2,1)S(1)}, bf16[32,2048]{1,0:T(8,128)(2,1)}, u32[]{:S(2)}, u32[]{:S(2)}) collective-permute-start(bf16[32,2048]{1,0:T(8,128)(2,1)S(1)} %collective-permute-done.23.refs_12_), channel_id=1, source_target_pairs={{0,2},{1,3},{2,0},{3,1},{4,6},{5,7},{6,4},{7,5},{8,10},{9,11},{10,... | collective-permute-start | bytes 393224 | tf_op jit(solution)/shard_map/ppermute | solution.py:21
  133.6 20.4 %collective-permute-start.40 = (bf16[128,2048]{1,0:T(8,128)(2,1)}, bf16[128,2048]{1,0:T(8,128)(2,1)}, u32[]{:S(2)}, u32[]{:S(2)}) collective-permute-start(bf16[128,2048]{1,0:T(8,128)(2,1)} %collective-permute-done.24.refs_2_), channel_id=1, source_target_pairs={{0,2},{1,3},{2,0},{3,1},{4,6},{5,7},{6,4},{7,5},{8,10},{9,11},{10,... | collective-permute-start | bytes 1572872 | tf_op jit(solution)/shard_map/ppermute | solution.py:21
  153.0 4.0 %collective-permute-start.41 = (bf16[128,2048]{1,0:T(8,128)(2,1)}, bf16[128,2048]{1,0:T(8,128)(2,1)S(1)}, u32[]{:S(2)}, u32[]{:S(2)}) collective-permute-start(bf16[128,2048]{1,0:T(8,128)(2,1)} %copy-done.23), channel_id=1, source_target_pairs={{0,1},{1,0},{2,3},{3,2},{4,5},{5,4},{6,7},{7,6},{8,9},{9,8},{10,11... | collective-permute-start | bytes 1572872 | tf_op jit(solution)/shard_map/ppermute | solution.py:21
  153.5 4.6 %collective-permute-start.43 = (bf16[128,2048]{1,0:T(8,128)(2,1)}, bf16[128,2048]{1,0:T(8,128)(2,1)S(1)}, u32[]{:S(2)}, u32[]{:S(2)}) collective-permute-start(bf16[128,2048]{1,0:T(8,128)(2,1)} %collective-permute-done.24.refs_2_), channel_id=1, source_target_pairs={{0,1},{1,0},{2,3},{3,2},{4,5},{5,4},{6,7},{7,6},{8,9},{9,8},{10,11... | collective-permute-start | bytes 1572872 | tf_op jit(solution)/shard_map/ppermute | solution.py:21
  153.5 4.6 %collective-permute-start.42 = (bf16[128,2048]{1,0:T(8,128)(2,1)}, bf16[128,2048]{1,0:T(8,128)(2,1)S(1)}, u32[]{:S(2)}, u32[]{:S(2)}) collective-permute-start(bf16[128,2048]{1,0:T(8,128)(2,1)} %collective-permute-done.25.refs_1_), channel_id=1, source_target_pairs={{0,1},{1,0},{2,3},{3,2},{4,5},{5,4},{6,7},{7,6},{8,9},{9,8},{10,11... | collective-permute-start | bytes 1572872 | tf_op jit(solution)/shard_map/ppermute | solution.py:21
  154.0 38.9 %collective-permute-start.47 = (bf16[4,256,512]{2,1,0:T(8,128)(2,1)}, bf16[4,256,512]{2,1,0:T(8,128)(2,1)S(1)}, u32[]{:S(2)}, u32[]{:S(2)}) collective-permute-start(bf16[4,256,512]{2,1,0:T(8,128)(2,1)} %bitcast.80), channel_id=1, source_target_pairs={{0,16},{16,0},{1,17},{17,1},{2,18},{18,2},{3,19},{19,3},{4,20},{20... | collective-permute-start | bytes 3145736 | tf_op jit(solution)/shard_map/ppermute | solution.py:26
  157.0 33.3 %collective-permute-start.39 = (bf16[32,4096]{1,0:T(8,128)(2,1)S(1)}, bf16[32,4096]{1,0:T(8,128)(2,1)S(1)}, u32[]{:S(2)}, u32[]{:S(2)}) collective-permute-start(bf16[32,4096]{1,0:T(8,128)(2,1)S(1)} %slice.244), channel_id=1, source_target_pairs={{0,2},{1,3},{2,0},{3,1},{4,6},{5,7},{6,4},{7,5},{8,10},{9,11},{10,... | collective-permute-start | bytes 786440 | tf_op jit(solution)/shard_map/ppermute | solution.py:21
  191.8 8.4 %collective-permute-start.45 = (bf16[32,4096]{1,0:T(8,128)(2,1)S(1)}, bf16[32,4096]{1,0:T(8,128)(2,1)S(1)}, u32[]{:S(2)}, u32[]{:S(2)}) collective-permute-start(bf16[32,4096]{1,0:T(8,128)(2,1)S(1)} %get-tuple-element.180), channel_id=1, source_target_pairs={{0,2},{1,3},{2,0},{3,1},{4,6},{5,7},{6,4},{7,5},{8,10},{9,11},{10,... | collective-permute-start | bytes 786440 | tf_op jit(solution)/shard_map/ppermute | solution.py:21
  195.9 4.4 %collective-permute-start.48 = (f32[2,256]{1,0:T(2,128)S(1)}, f32[2,256]{1,0:T(2,128)S(1)}, u32[]{:S(2)}, u32[]{:S(2)}) collective-permute-start(f32[2,256]{1,0:T(2,128)S(1)} %pad_maximum_fusion.6), channel_id=1, source_target_pairs={{0,1},{1,0},{2,3},{3,2},{4,5},{5,4},{6,7},{7,6},{8,9},{9,8},{10,11... | collective-permute-start | bytes 6152 | tf_op jit(solution)/shard_map/ppermute | solution.py:21
  200.2 4.4 %collective-permute-start.46 = (bf16[64,4096]{1,0:T(8,128)(2,1)S(1)}, bf16[64,4096]{1,0:T(8,128)(2,1)S(1)}, u32[]{:S(2)}, u32[]{:S(2)}) collective-permute-start(bf16[64,4096]{1,0:T(8,128)(2,1)S(1)} %pad_maximum_fusion.3), channel_id=1, source_target_pairs={{0,1},{1,0},{2,3},{3,2},{4,5},{5,4},{6,7},{7,6},{8,9},{9,8},{10,11... | collective-permute-start | bytes 1572872 | tf_op jit(solution)/shard_map/ppermute | solution.py:21
  (64 other events, 366.3 us)
Sparse Core Ops, SparseCore 0:
  18.1 70.5 all-gather.1

commit v3 on v2

--- a/solution.py
+++ b/solution.py
@@ -49,20 +49,23 @@
     return order
 
 
-def gather_tensor(rows):
+def gather_tensor(rows, beside=()):
     for bit in reversed(bits_of(lax.axis_size("tensor"))):
-        rows = jnp.concatenate([rows, swap(rows, "tensor", bit)], axis=0)
+        got = after(swap(rows, "tensor", bit), beside)
+        rows, beside = jnp.concatenate([rows, got], axis=0), ()
     return rows
 
 
 def scatter_tensor(rows, beside=()):
     bits = bits_of(lax.axis_size("tensor"))
     for bit in bits:
-        half = rows.shape[0] // 2
-        got = swap(rows[half:].astype(BF), "tensor", bit)
+        if not isinstance(rows, tuple):
+            half = rows.shape[0] // 2
+            rows = rows[:half], rows[half:]
+        got = swap(rows[1].astype(BF), "tensor", bit)
         if bit == bits[-1]:
             got = after(got, beside)
-        rows = rows[:half].astype(F32) + got.astype(F32)
+        rows = rows[0].astype(F32) + got.astype(F32)
     return rows
 
 
@@ -121,13 +124,98 @@
 
 
 NEVER = -1e30
+VMEM_WHOLE = pl.BlockSpec(memory_space=pltpu.VMEM)
+HBM_WHOLE = pl.BlockSpec(memory_space=pl.ANY)
+
+
+def fetch_kernel(count, *refs):
+    sources, targets, sem = refs[:count], refs[count : 2 * count], refs[-1]
+    copies = [
+        pltpu.make_async_copy(source, target, sem.at[i])
+        for i, (source, target) in enumerate(zip(sources, targets, strict=True))
+    ]
+    for copy in copies:
+        copy.start()
+    for copy in copies:
+        copy.wait()
+
+
+def fetch(*weights):
+    return pl.pallas_call(
+        functools.partial(fetch_kernel, len(weights)),
+        in_specs=[HBM_WHOLE] * len(weights),
+        out_specs=[VMEM_WHOLE] * len(weights),
+        out_shape=[pltpu.VMEM(weight.shape, weight.dtype) for weight in weights],
+        scratch_shapes=[pltpu.SemaphoreType.DMA((len(weights),))],
+        compiler_params=pltpu.CompilerParams(vmem_limit_bytes=2 * MIB),
+        cost_estimate=pl.CostEstimate(
+            flops=0, bytes_accessed=0, transcendentals=0
+        ),
+    )(*[in_hbm(weight) for weight in weights])
+
+
+def arrange_kernel(
+    at_ref, rows_hbm, cot_hbm, gain_ref, normed_ref, mine_ref, cots_ref, cot_mine_ref,
+    inputs_ref, scaled_ref, root_ref, rows_in, rows_sem, cot_sem,
+):
+    chunk = mine_ref.shape[0]
+    spots = chunk_places(at_ref, 0, normed_ref.shape[0] // chunk, chunk)
+    parts = [slice(i * chunk, (i + 1) * chunk) for i in range(len(spots))]
+    copies = []
+    for i, (spot, part) in enumerate(zip(spots, parts, strict=True)):
+        copies.append((
+            pltpu.make_async_copy(rows_hbm.at[spot], rows_in.at[part], rows_sem.at[i]),
+            pltpu.make_async_copy(cot_hbm.at[spot], cots_ref.at[part], cot_sem.at[i]),
+        ))
+    for pair in copies:
+        for copy in pair:
+            copy.start()
+    gain = gain_ref[...].astype(F32)
+    for i, (part, pair) in enumerate(zip(parts, copies, strict=True)):
+        pair[0].wait()
+        rows = rows_in[part, :].astype(F32)
+        root = lax.rsqrt(jnp.mean(rows * rows, axis=-1, keepdims=True) + EPS)
+        normed = (rows * root * gain).astype(BF)
+        normed_ref[part, :] = normed
+        pair[1].wait()
+        if i == 0:
+            mine_ref[...] = normed
+            cot_mine_ref[...] = cots_ref[part, :]
+            inputs_ref[...] = rows
+            scaled_ref[...] = rows * root
+            root_ref[...] = jnp.broadcast_to(root, root_ref.shape)
+
+
+def arrange(places, rows, cot, gain):
+    count, width = rows.shape
+    slots = places.shape[0]
+    chunk = count // slots
+    shapes = [(count, width), (chunk, width)] * 2
+    more = [(chunk, width)] * 3
+    return pl.pallas_call(
+        arrange_kernel,
+        in_specs=[pl.BlockSpec(memory_space=pltpu.SMEM), HBM_WHOLE, HBM_WHOLE, VMEM_WHOLE],
+        out_specs=[VMEM_WHOLE] * 7,
+        out_shape=[jax.ShapeDtypeStruct(shape, BF) for shape in shapes]
+        + [jax.ShapeDtypeStruct(shape, F32) for shape in more],
+        scratch_shapes=[pltpu.VMEM((count, width), BF),
+                        pltpu.SemaphoreType.DMA((slots,)), pltpu.SemaphoreType.DMA((slots,))],
+        compiler_params=pltpu.CompilerParams(vmem_limit_bytes=16 * MIB),
+        cost_estimate=pl.CostEstimate(
+            flops=8 * count * width, bytes_accessed=8 * count * width, transcendentals=0
+        ),
+    )(places, in_hbm(rows), in_hbm(cot), gain)
+
+
+def column_of(row):
+    return jnp.broadcast_to(row, (HD, row.shape[1])).T[:, :1]
 
 
 def attend_kernel(chunk, slots, scale, shift, at_ref, *refs):
-    count = len(refs) - 17
+    count = len(refs) - 16
     pieces = refs[:count]
-    (own_spot_ref, own_doc_ref, doc_ref, cos_ref, sin_ref, wq_ref, wk_ref, wv_ref,
-     q_ref, k_ref, v_ref, att_ref, mass_ref, seq_hbm, x, sem, out_sem) = refs[count:]
+    (doc_ref, cos_ref, sin_ref, wq_ref, wk_ref, wv_ref, q_ref, k_ref, v_ref, att_ref, mass_ref,
+     seq_hbm, x, doc_column, sem, out_sem) = refs[count:]
     step, last = pl.program_id(0), pl.num_programs(0) - 1
     place_rows(step, pieces, chunk_places(at_ref, 0, count, chunk), x, sem)
     keep = pltpu.make_async_copy(x, seq_hbm, out_sem)
@@ -137,17 +225,22 @@
         keep.start()
 
     cos, sin = cos_ref[...], sin_ref[...]
-    shape = (own_spot_ref.shape[0], doc_ref.shape[1])
-    allowed = (lax.broadcasted_iota(jnp.int32, shape, 1) <= own_spot_ref[...]) & (
-        own_doc_ref[...] == doc_ref[...]
-    )
-    bias = jnp.where(allowed, shift, NEVER)
+    own = chunk_places(at_ref, 0, slots, chunk)
+    doc_column[...] = column_of(doc_ref[...])
+    shape = (chunk, doc_ref.shape[1])
+    bias = []
+    for i, spot in enumerate(own):
+        own_spots = lax.broadcasted_iota(jnp.int32, shape, 0) + at_ref[i] * chunk
+        allowed = (lax.broadcasted_iota(jnp.int32, shape, 1) <= own_spots) & (
+            doc_column[spot, :] == doc_ref[...]
+        )
+        bias.append(jnp.where(allowed, shift, NEVER))
+    bias = jnp.concatenate(bias, axis=0)
     rows = x[...]
     q_all = dot(rows, wq_ref[...])
     k_all = dot(rows, wk_ref[...])
     v_all = dot(rows, wv_ref[...]).astype(BF)
     v_ref[...] = v_all
-    own = chunk_places(at_ref, 0, slots, chunk)
     for j in range(q_all.shape[1] // HD):
         cols = slice(j * HD, (j + 1) * HD)
         q_ref[:, cols] = rope_rows(q_all[:, cols], cos, sin).astype(BF)
@@ -163,9 +256,9 @@
         keep.wait()
 
 
-def attend(places, pieces, own_spots, own_docs, docs, cos, sin, wq, wk, wv, slots, scale, shift):
+def attend(places, pieces, docs, cos, sin, wq, wk, wv, slots, scale, shift):
     chunk, width = pieces[0].shape
-    seq, rows = chunk * len(pieces), own_spots.shape[0]
+    seq, rows = chunk * len(pieces), chunk * slots
     cols = wq.shape[1]
     heads = cols // HD
     step = min(2, heads)
@@ -179,7 +272,7 @@
         functools.partial(attend_kernel, chunk, slots, scale, shift),
         grid=(heads // step,),
         in_specs=[pl.BlockSpec(memory_space=pltpu.SMEM)] + [hbm] * len(pieces)
-        + [whole(rows, 1), whole(rows, 1), whole(1, seq), whole(seq, HD), whole(seq, HD)]
+        + [whole(1, seq), whole(seq, HD), whole(seq, HD)]
         + [wspec] * 3,
         out_specs=[sspec, sspec, sspec,
                    pl.BlockSpec((rows, step * HD), lambda i: (0, i)),
@@ -188,21 +281,20 @@
         out_shape=[jax.ShapeDtypeStruct((seq, cols), BF)] * 3
         + [jax.ShapeDtypeStruct((rows, cols), BF), jax.ShapeDtypeStruct((heads, rows, 1), F32),
            jax.ShapeDtypeStruct((seq, width), BF)],
-        scratch_shapes=[pltpu.VMEM((seq, width), BF),
+        scratch_shapes=[pltpu.VMEM((seq, width), BF), pltpu.VMEM((seq, 1), jnp.int32),
                         pltpu.SemaphoreType.DMA((len(pieces),)), pltpu.SemaphoreType.DMA],
         compiler_params=pltpu.CompilerParams(vmem_limit_bytes=56 * MIB),
         cost_estimate=pl.CostEstimate(
             flops=2 * seq * width * cols * 3, bytes_accessed=6 * width * cols, transcendentals=0
         ),
-    )(places, *pieces, own_spots, own_docs, docs, cos, sin,
-      wq, wk, wv)
+    )(places, *pieces, docs, cos, sin, wq, wk, wv)
 
 
 def attend_back_kernel(chunk, slots, scale, shift, at_ref, starts_ref, *refs):
-    count = len(refs) - 23
+    count = len(refs) - 24
     pieces = refs[:count]
-    (wo_ref, q_ref, k_ref, v_ref, cos_ref, sin_ref, doc_row_ref, doc_ref,
-     x_hbm, wq_hbm, wk_hbm, wv_hbm, mine_ref, theirs_ref, first_ref,
+    (wo_ref, q_ref, k_ref, v_ref, cos_ref, sin_ref, doc_row_ref, more_ref,
+     x_hbm, wq_hbm, wk_hbm, wv_hbm, mine_ref, theirs_ref, first_ref, give_ref,
      bb, x_cols, w_cols, acc, every, bb_sem, x_sem, w_sem) = refs[count:]
     step = pl.program_id(0)
     owners = x_cols.shape[0]
@@ -225,12 +317,13 @@
     parts = [slice(i * block, (i + 1) * block) for i in range(seq // block)]
     heads = [slice(j * HD, (j + 1) * HD) for j in range(width // HD)]
     weights, attended = {}, []
+    doc_column = column_of(doc_row_ref[...])
     for i, part in enumerate(parts):
         shape = (block, part.stop)
         allowed = (
             lax.broadcasted_iota(jnp.int32, shape, 1)
             <= lax.broadcasted_iota(jnp.int32, shape, 0) + part.start
-        ) & (doc_ref[part, :] == doc_row_ref[:, : part.stop])
+        ) & (doc_column[part, :] == doc_row_ref[:, : part.stop])
         bias = jnp.where(allowed, shift, NEVER)
         row = []
         for j, cols in enumerate(heads):
@@ -294,11 +387,15 @@
 
     @pl.when(step == pl.num_programs(0) - 1)
     def _():
-        first_ref[...] = acc[...].astype(BF)
+        total, half = acc[...].astype(BF), acc.shape[0] // 2
+        for n, at in enumerate((slice(0, half), slice(half, 2 * half))):
+            keep_ref = first_ref if n == 0 else give_ref
+            keep_ref[:, : acc.shape[1]] = total[at]
+            keep_ref[:, acc.shape[1] :] = more_ref[at, :]
 
 
 def attend_back(
-    places, starts, pieces, wo, q, k, v, cos, sin, docs, doc_column, x_seq, wq, wk, wv,
+    places, starts, pieces, wo, q, k, v, cos, sin, docs, more, x_seq, wq, wk, wv,
     size, slots, scale, shift,
 ):
     seq, width = x_seq.shape
@@ -318,14 +415,15 @@
         grid=(heads // step,),
         in_specs=[pl.BlockSpec(memory_space=pltpu.SMEM)] * 2 + [hbm] * len(pieces)
         + [pl.BlockSpec((step * HD, width), lambda i: (i, 0)),
-           sspec, sspec, sspec, whole(seq, HD), whole(seq, HD), whole(1, seq), whole(seq, 1)]
+           sspec, sspec, sspec, whole(seq, HD), whole(seq, HD), whole(1, seq), whole(*more.shape)]
         + [hbm] * 4,
         out_specs=[pl.BlockSpec((4, size, step * HD), lambda i: (0, 0, i)),
                    pl.BlockSpec((owners - 1, 4, size, step * HD), lambda i: (0, 0, 0, i)),
-                   whole(own, width)],
+                   whole(own // 2, 2 * width), whole(own // 2, 2 * width)],
         out_shape=[jax.ShapeDtypeStruct((4, size, cols), F32),
                    jax.ShapeDtypeStruct((owners - 1, 4, size, cols), BF),
-                   jax.ShapeDtypeStruct((own, width), BF)],
+                   jax.ShapeDtypeStruct((own // 2, 2 * width), BF),
+                   jax.ShapeDtypeStruct((own // 2, 2 * width), BF)],
         scratch_shapes=[pltpu.VMEM((seq, width), BF), pltpu.VMEM((owners, seq, size), BF),
                         pltpu.VMEM((3, width, step * HD), BF),
                         pltpu.VMEM((own, width), F32),
@@ -340,7 +438,7 @@
         ),
     )(
         places, starts, *pieces, in_hbm(wo), q, k, v, cos, sin,
-        docs, doc_column, in_hbm(x_seq), in_hbm(wq), in_hbm(wk), in_hbm(wv),
+        docs, more, in_hbm(x_seq), in_hbm(wq), in_hbm(wk), in_hbm(wv),
     )
 
 
@@ -353,60 +451,54 @@
     return hidden, gate_back, up_back
 
 
-def mlp_kernel(x_ref, hb_ref, wg_ref, wu_ref, hidden_ref, back_ref, acc):
-    step = pl.program_id(0)
-    x, wg, wu = x_ref[...], wg_ref[...], wu_ref[...]
-    hidden, gate_back, up_back = gate_math(dot(x, wg), dot(x, wu), hb_ref[...].astype(F32))
-    hidden_ref[...] = hidden
-    back = dot_nt(gate_back, wg) + dot_nt(up_back, wu)
-
-    @pl.when(step == 0)
-    def _():
-        acc[...] = back
-
-    @pl.when(step > 0)
-    def _():
-        acc[...] += back
-
-    @pl.when(step == pl.num_programs(0) - 1)
-    def _():
-        back_ref[...] = acc[...].astype(BF)
+def mlp_kernel(
+    block, x_ref, hb_ref, wg_ref, wu_ref, hidden_ref, gate_ref, up_ref, back_ref
+):
+    x, total = x_ref[...], None
+    for i in range(wg_ref.shape[1] // block):
+        at = slice(i * block, (i + 1) * block)
+        wg, wu = wg_ref[:, at], wu_ref[:, at]
+        hidden_ref[:, at], gate_back, up_back = gate_math(
+            dot(x, wg), dot(x, wu), hb_ref[:, at].astype(F32)
+        )
+        gate_ref[:, at] = gate_back
+        up_ref[:, at] = up_back
+        back = dot_nt(gate_back, wg) + dot_nt(up_back, wu)
+        total = back if total is None else total + back
+    back_ref[...] = total.astype(BF)
 
 
 def mlp(x, hidden_back, wg, wu):
     rows, width = x.shape
     units = wg.shape[1]
-    block = min(512, units)
-    whole = pl.BlockSpec((rows, width), lambda i: (0, 0), pipeline_mode=pl.Buffered(1))
-    wspec = pl.BlockSpec((width, block), lambda i: (0, i))
-    uspec = pl.BlockSpec((rows, block), lambda i: (0, i))
     return pl.pallas_call(
-        mlp_kernel,
-        grid=(units // block,),
-        in_specs=[whole, uspec, wspec, wspec],
-        out_specs=[uspec, whole],
+        functools.partial(mlp_kernel, min(512, units)),
+        in_specs=[VMEM_WHOLE] * 4,
+        out_specs=[VMEM_WHOLE] * 4,
         out_shape=[
-            jax.ShapeDtypeStruct((rows, units), BF), jax.ShapeDtypeStruct((rows, width), BF)
+            *[jax.ShapeDtypeStruct((rows, units), BF)] * 3, jax.ShapeDtypeStruct((rows, width), BF)
         ],
-        scratch_shapes=[pltpu.VMEM((rows, width), F32)],
-        compiler_params=pltpu.CompilerParams(vmem_limit_bytes=56 * MIB),
+        compiler_params=pltpu.CompilerParams(vmem_limit_bytes=20 * MIB),
         cost_estimate=pl.CostEstimate(
-            flops=8 * rows * width * units, bytes_accessed=4 * width * units, transcendentals=0
+            flops=0, bytes_accessed=0, transcendentals=0
         ),
-    )(x, hidden_back, in_hbm(wg), in_hbm(wu))
-
-
-def hidden_back_kernel(tile, cot_hbm, wd_ref, out_ref, cot, sem):
-    tiles = [pl.ds(i * tile, tile) for i in range(cot.shape[0] // tile)]
-    copies = [
-        pltpu.make_async_copy(cot_hbm.at[at], cot.at[at], sem.at[i]) for i, at in enumerate(tiles)
-    ]
+    )(x, hidden_back, in_vmem(wg), in_vmem(wu))
+
+
+def hidden_back_kernel(tile, at_ref, cot_hbm, wd_ref, out_ref, cot, sem):
+    copies = []
+    for i in range(cot.shape[0] // tile):
+        source = pl.ds(pl.multiple_of(at_ref[i] * tile, tile), tile)
+        target = cot.at[pl.ds(i * tile, tile)]
+        copies.append(pltpu.make_async_copy(cot_hbm.at[source], target, sem.at[i]))
 
     def every_tile(waits):
         wd = wd_ref[...]
-        for copy, at in zip(copies, tiles, strict=True):
+        for i in range(0, len(copies), 2):
             if waits:
-                copy.wait()
+                copies[i].wait()
+                copies[i + 1].wait()
+            at = pl.ds(i * tile, 2 * tile)
             out_ref[at, :] = dot_nt(cot[at, :], wd).astype(BF)
 
     @pl.when(pl.program_id(0) == 0)
@@ -420,32 +512,34 @@
         every_tile(False)
 
 
-def hidden_back_of(cot, wd):
+def hidden_back_of(turns, cot, wd):
     rows, width = cot.shape
-    units = wd.shape[0]
-    block, tile = min(512, units), 256
+    units, tiles = wd.shape[0], turns.shape[0]
+    block = min(512, units)
     return pl.pallas_call(
-        functools.partial(hidden_back_kernel, tile),
+        functools.partial(hidden_back_kernel, rows // tiles),
         grid=(units // block,),
-        in_specs=[pl.BlockSpec(memory_space=pl.ANY),
+        in_specs=[pl.BlockSpec(memory_space=pltpu.SMEM), HBM_WHOLE,
                   pl.BlockSpec((block, width), lambda i: (i, 0))],
         out_specs=pl.BlockSpec((rows, block), lambda i: (0, i)),
         out_shape=jax.ShapeDtypeStruct((rows, units), BF),
-        scratch_shapes=[pltpu.VMEM((rows, width), BF), pltpu.SemaphoreType.DMA((rows // tile,))],
+        scratch_shapes=[pltpu.VMEM((rows, width), BF), pltpu.SemaphoreType.DMA((tiles,))],
         compiler_params=pltpu.CompilerParams(vmem_limit_bytes=56 * MIB),
         cost_estimate=pl.CostEstimate(
             flops=2 * rows * width * units, bytes_accessed=2 * width * (rows + units),
             transcendentals=0,
         ),
-    )(cot, in_hbm(wd))
+    )(turns, in_hbm(cot), in_hbm(wd))
 
 
 def mlp_grad_kernel(count, chunk, at_ref, *refs):
     pieces = refs[:count]
-    hb_ref, cb_ref, wg_ref, wu_ref = refs[count : count + 4]
-    gg_ref, ug_ref, dg_ref, gain_ref, x_all, hid, gbk, ubk, sem = refs[-9:]
-    size = cb_ref.shape[1]
-    per = pieces[0].shape[0] // chunk
+    (own_hid, own_gate, own_up, hb_ref, cot_hbm, wg_ref, wu_ref, gg_ref, ug_ref, dg_ref, gain_ref,
+     x_all, cb, hid, gbk, ubk, gain_sum, sem, cot_sem) = refs[count:]
+    size = cb.shape[1]
+    tile = pieces[0].shape[0]
+    per = tile // chunk
+    tiles = x_all.shape[0] // tile
     own = pl.ds(pl.multiple_of(at_ref[0] * size, size), size)
 
     @pl.when(pl.program_id(0) == 0)
@@ -455,14 +549,26 @@
             spot = pl.ds(pl.multiple_of(at_ref[1 + i] * chunk, chunk), chunk)
             part = pieces[i // per].at[pl.ds(i % per * chunk, chunk)]
             copies.append(pltpu.make_async_copy(part, x_all.at[spot], sem.at[i]))
+        base = 1 + count * per
+        for i in range(per):
+            spot = pl.ds(pl.multiple_of(at_ref[base + tiles + i] * chunk, chunk), chunk)
+            target = cb.at[pl.ds(i * chunk, chunk)]
+            copies.append(pltpu.make_async_copy(cot_hbm.at[spot, own], target, cot_sem.at[i]))
+        for i in range(1, tiles):
+            spot = pl.ds(pl.multiple_of(at_ref[base + i] * tile, tile), tile)
+            target = cb.at[pl.ds(i * tile, tile)]
+            copies.append(
+                pltpu.make_async_copy(cot_hbm.at[spot, own], target, cot_sem.at[per + i])
+            )
         for copy in copies:
             copy.start()
         for copy in copies:
             copy.wait()
 
+    hid[:tile, :], gbk[:tile, :], ubk[:tile, :] = own_hid[...], own_gate[...], own_up[...]
     wg, wu = wg_ref[...], wu_ref[...]
-    for i in range(x_all.shape[0] // 128):
-        at = pl.ds(i * 128, 128)
+    for i in range(1, tiles):
+        at = pl.ds(i * tile, tile)
         x = x_all[at, :]
         hid[at, :], gbk[at, :], ubk[at, :] = gate_math(
             dot(x, wg), dot(x, wu), hb_ref[at, :].astype(F32)
@@ -472,7 +578,7 @@
     up_grad = dot_tn(xb, ubk[...])
     gg_ref[...] = gate_grad
     ug_ref[...] = up_grad
-    dg_ref[...] = dot_tn(hid[...], cb_ref[...])
+    dg_ref[...] = dot_tn(hid[...], cb[...])
     gain = jnp.sum(
         wg_ref[own, :].astype(F32) * gate_grad + wu_ref[own, :].astype(F32) * up_grad,
         axis=1, keepdims=True,
@@ -480,48 +586,51 @@
 
     @pl.when(pl.program_id(0) == 0)
     def _():
-        gain_ref[...] = gain
+        gain_sum[...] = gain
 
     @pl.when(pl.program_id(0) > 0)
     def _():
-        gain_ref[...] += gain
-
-
-def mlp_grad(places, chunk, pieces, cot, hb, wg, wu, size, first, count, before):
+        gain_sum[...] += gain
+
+    @pl.when(pl.program_id(0) == pl.num_programs(0) - 1)
+    def _():
+        gain_ref[...] = jnp.broadcast_to(gain_sum[...], (size, HD)).T[:1, :]
+
+
+def mlp_grad(places, chunk, pieces, own, cot, hb, wg, wu, size):
     tile, width = pieces[0].shape
     rows, units = hb.shape
-    block = min(256, count)
-    skip = first // block
-    wspec = pl.BlockSpec((width, block), lambda i, at: (0, i + skip))
-    hbm = pl.BlockSpec(memory_space=pl.ANY)
+    block = min(256, units)
+    wspec = pl.BlockSpec((width, block), lambda i, at: (0, i))
+    ospec = pl.BlockSpec((tile, block), lambda i, at: (0, i))
     grid_spec = pltpu.PrefetchScalarGridSpec(
         num_scalar_prefetch=1,
-        grid=(count // block,),
-        in_specs=[hbm] * len(pieces)
-        + [pl.BlockSpec((rows, block), lambda i, at: (0, i + skip)),
-           pl.BlockSpec((rows, size), lambda i, at: (0, at[0]), pipeline_mode=pl.Buffered(1)),
-           wspec, wspec]
-        + [hbm] * len(before),
-        out_specs=[pl.BlockSpec((size, block), lambda i, at: (0, i + skip))] * 2
-        + [pl.BlockSpec((block, size), lambda i, at: (i + skip, 0)),
-           pl.BlockSpec((size, 1), lambda i, at: (0, 0))],
-        scratch_shapes=[pltpu.VMEM((rows, width), BF)]
+        grid=(units // block,),
+        in_specs=[HBM_WHOLE] * len(pieces) + [ospec] * 3
+        + [pl.BlockSpec((rows, block), lambda i, at: (0, i)), HBM_WHOLE, wspec, wspec],
+        out_specs=[pl.BlockSpec((size, block), lambda i, at: (0, i))] * 2
+        + [pl.BlockSpec((block, size), lambda i, at: (i, 0)),
+           pl.BlockSpec((1, size), lambda i, at: (0, 0))],
+        scratch_shapes=[pltpu.VMEM((rows, width), BF), pltpu.VMEM((rows, size), BF)]
         + [pltpu.VMEM((rows, block), BF)] * 3
-        + [pltpu.SemaphoreType.DMA((rows // chunk,))],
+        + [pltpu.VMEM((size, 1), F32), pltpu.SemaphoreType.DMA((rows // chunk,)),
+           pltpu.SemaphoreType.DMA((tile // chunk + rows // tile,))],
     )
     return pl.pallas_call(
         functools.partial(mlp_grad_kernel, len(pieces), chunk),
         grid_spec=grid_spec,
         out_shape=[jax.ShapeDtypeStruct((size, units), F32)] * 2
-        + [jax.ShapeDtypeStruct((units, size), F32), jax.ShapeDtypeStruct((size, 1), F32)],
-        input_output_aliases={len(pieces) + 5 + i: i for i in range(len(before))},
+        + [jax.ShapeDtypeStruct((units, size), F32), jax.ShapeDtypeStruct((1, size), F32)],
         compiler_params=pltpu.CompilerParams(vmem_limit_bytes=56 * MIB),
         cost_estimate=pl.CostEstimate(
-            flops=2 * rows * count * (2 * width + 3 * size),
-            bytes_accessed=4 * width * count + 4 * rows * width,
+            flops=2 * rows * units * (2 * width + 3 * size),
+            bytes_accessed=4 * width * units + 4 * rows * width,
             transcendentals=0,
         ),
-    )(places, *pieces, hb, cot, in_hbm(wg), in_hbm(wu), *before)
+    )(
+        places, *pieces, *[in_hbm(rows) for rows in own], in_hbm(hb), in_hbm(cot),
+        in_hbm(wg), in_hbm(wu),
+    )
 
 
 def row_mean(values):
@@ -551,14 +660,10 @@
     scale, shift = HD ** (-0.5), -math.log(length)
     gain_first, gain_second = attn_gain.astype(F32), mlp_gain.astype(F32)
 
-    def slotted(values):
-        return jnp.concatenate(
-            [lax.dynamic_slice_in_dim(values, (place ^ s) * chunk, chunk, 0) for s in slots], axis=0
-        )
-
-    inputs32 = slotted(activations[0]).astype(F32)
-    scaled_first, root_first = norm_parts(inputs32)
-    normed_first = (scaled_first * gain_first).astype(BF)
+    slot_places = jnp.stack([place ^ slot for slot in slots])
+    normed_first, mine, cot, cot_mine, inputs_mine, scaled_mine, root_mine = arrange(
+        slot_places, activations[0], cotangent[0], attn_gain[None]
+    )
 
     bits = list(reversed(bits_of(n_t)))
 
@@ -570,10 +675,9 @@
                 lists = after(lists, beside)
         return lists
 
-    mine, *rings = ring_of(normed_first[:chunk])
+    rings = ring_of(mine)[1:]
     cot_all = lax.all_gather(
-        lax.dynamic_slice_in_dim(after(cotangent[0], normed_first), place * chunk, chunk, 0),
-        ("dp", "ctx", "tensor"), axis=0, tiled=True,
+        cot_mine, ("dp", "ctx", "tensor"), axis=0, tiled=True
     )
 
     ring_at = (ctx - jnp.arange(n_ctx, dtype=jnp.int32) + n_ctx) % n_ctx
@@ -581,37 +685,37 @@
         ring_at[k : k + 1] * n_t + (place ^ slot) for k in range(n_ctx) for slot in slots
     ])
     docs = doc_ids
-    doc_column = doc_ids.reshape(length, 1)
     out_cols = width // (n_dp * n_ctx)
     owners = jnp.stack([((dp + step) % n_dp) * n_ctx + ctx for step in range(n_dp)])
     starts = owners * out_cols
     owner = owners[0]
+    tiles = n_dp * n_ctx
+    turns = (owner + jnp.arange(tiles, dtype=jnp.int32)) % tiles
     places = [owner[None]]
     for flip in (0, 1):
         for step in range(n_dp):
-            for slot in slots[: n_t // 2]:
+            for index in range(n_t // 2):
                 group = ((dp - step + n_dp) % n_dp) * n_ctx + ring_at
-                places.append(group * n_t + (place ^ slot ^ flip))
-    places = jnp.concatenate(places)
-    own_spots = slotted(ctx * rows + jnp.arange(rows, dtype=jnp.int32)[:, None])
-    own_docs = slotted(
-        lax.dynamic_slice_in_dim(doc_ids.reshape(length, 1), ctx * rows, rows, 0)
-    )
+                group = (group - owner + tiles) % tiles
+                inside = jnp.where(
+                    group == 0, index + flip * (n_t // 2), place ^ slots[index] ^ flip
+                )
+                places.append(group * n_t + inside)
+    places = jnp.concatenate(places + [turns, owner * n_t + slot_places])
     frequency = np.float32(10000.0) ** (
         -np.arange(HD // 2, dtype=np.float32) * np.float32(2.0) / np.float32(HD)
     )
     angles = np.arange(length, dtype=np.float32)[:, None] * frequency[None, :]
     cos = jnp.asarray(np.concatenate([np.cos(angles), np.cos(angles)], axis=1))
     sin = jnp.asarray(np.concatenate([-np.sin(angles), np.sin(angles)], axis=1))
-    cot = slotted(cotangent[0])
-    rings = after(rings, seq_places, own_spots, own_docs, cot, starts, places, doc_column)
+    rings = after(rings, seq_places, starts, places, turns)
     hidden_back = lax.dot_general(
         after(cot, rings), down_weight, (((1,), (1,)), ((), ())), preferred_element_type=F32
     ).astype(BF)
     seq_pieces = spread(rings, hidden_back)
     own_pieces = [normed_first[i * chunk : (i + 1) * chunk] for i in range(n_t)]
     q, k, v, attended, mass, x_seq = attend(
-        seq_places, own_pieces + sum(seq_pieces, []), own_spots, own_docs, docs, cos, sin,
+        seq_places, own_pieces + sum(seq_pieces, []), docs, cos, sin,
         query_weight, key_weight, value_weight, n_t, scale, shift,
     )
     attn_mass = from_slots(mass[:, :, 0].T, slots, place)
@@ -627,32 +731,36 @@
     branch = scatter_tensor(
         jnp.dot(attended, out_weight, preferred_element_type=F32).astype(BF), attn_mass
     )
-    middle = inputs32[:chunk] + branch
+    middle = inputs_mine + branch
     scaled_second, root_second = norm_parts(middle)
     normed_chunk = (scaled_second * gain_second).astype(BF)
-    normed_second = gather_tensor(normed_chunk)
+    gate, up = fetch(after(gate_weight, normed_chunk), up_weight)
+    normed_second = gather_tensor(normed_chunk, (gate, up))
     chunk_rings = ring_of(normed_chunk)
-    hidden, second_part = mlp(normed_second, hidden_back, gate_weight, up_weight)
+    hidden, gate_back, up_back, second_part = mlp(normed_second, hidden_back, gate, up)
     second_part, chunk_rings = lax.optimization_barrier((second_part, chunk_rings))
     x_near = [jnp.concatenate(chunk_rings, axis=0)]
     x_far = over_dp(x_near)
     x_near_more = over_tensor(x_near, bits[:-1])[1:]
     second_back = scatter_tensor(second_part)
-    middle_back = cot[:chunk].astype(F32) + norm_back(
+    middle_back = cot_mine.astype(F32) + norm_back(
         second_back, scaled_second, root_second, gain_second
     )
     branch_back = middle_back.astype(BF)
-    bb_rings = ring_of(branch_back)
-    hidden_back_all = hidden_back_of(after(cot_all, branch_back), down_weight)
-    bb_rings, x_far, x_near_more = after((bb_rings, x_far, x_near_more), hidden_back_all)
+    bb_rings = ring_of(branch_back)[1:]
+    bb_own = over_tensor([branch_back], bits[:-1])
+    hidden_back_all = hidden_back_of(turns, after(cot_all, branch_back), down_weight)
+    bb_rings, bb_own, x_far, x_near_more = after(
+        (bb_rings, bb_own, x_far, x_near_more), hidden_back_all
+    )
     mlp_part = jnp.dot(
         after(hidden, bb_rings), down_weight, preferred_element_type=F32
     ).astype(BF)
-    bb_pieces = spread(bb_rings, mlp_part)
+    bb_pieces = [over_tensor(bb_own, bits[-1:])] + spread(bb_rings, mlp_part)
     x_far_more = over_tensor(x_far, bits[:-1])[len(x_far) :]
 
-    mine_grads, theirs_grads, first_part = attend_back(
-        seq_places, starts, sum(bb_pieces, []), out_weight, q, k, v, cos, sin, docs, doc_column,
+    mine_grads, theirs_grads, kept_half, given_half = attend_back(
+        seq_places, starts, sum(bb_pieces, []), out_weight, q, k, v, cos, sin, docs, mlp_part,
         x_seq, query_weight, key_weight, value_weight, out_cols, n_t, scale, shift,
     )
 
@@ -661,16 +769,15 @@
     x_pieces = over_tensor(x_near + x_near_more + x_far + x_far_more, bits[-1:])
 
     gate_grad, up_grad, down_grad, mlp_gain_sum = mlp_grad(
-        after(places, first_part), chunk, x_pieces, cot_all, hidden_back_all,
-        gate_weight, up_weight, out_cols, 0, gate_weight.shape[1], (),
-    )
-    mlp_gain_sum = mlp_gain_sum[:, 0]
+        after(places, kept_half), chunk, x_pieces, (hidden, gate_back, up_back), cot_all,
+        hidden_back_all, gate_weight, up_weight, out_cols,
+    )
+    mlp_gain_sum = mlp_gain_sum[0]
     theirs = after(theirs, gate_grad)
-    both = scatter_tensor(jnp.concatenate([first_part, mlp_part], axis=1), gate_grad)
+    both = scatter_tensor((kept_half, given_half), gate_grad)
     first_back, mlp_out = both[:, :width], both[:, width:]
-    scaled_chunk, root_chunk = scaled_first[:chunk], root_first[:chunk]
     input_grad = (
-        middle_back + norm_back(first_back, scaled_chunk, root_chunk, gain_first)
+        middle_back + norm_back(first_back, scaled_mine, root_mine, gain_first)
     ).astype(BF)
     layer_out = (middle + mlp_out).astype(BF)
     results = gather_tensor(jnp.concatenate([layer_out, input_grad], axis=1))
@@ -688,7 +795,7 @@
         + rows_of(value_weight) * value_grad, axis=1,
     )
     gains = jnp.stack([attn_gain_sum, mlp_gain_sum])
-    for bit in bits_of(n_t):
+    for bit in bits:
         gains = gains + swap(gains, "tensor", bit)
     gain_grads = gains / lax.dynamic_slice_in_dim(
         jnp.stack([gain_first, gain_second]), owner * out_cols, out_cols, 1

time: 213 us -> 205 us (0.962)
  other arithmetic: 12.9 us -> 7.03 us
  waiting for transfers between devices: 27 us -> 21.6 us
  starting transfers between devices: 41.5 us -> 46.6 us
  local copies, waits for them, and re-layouts: 17.1 us -> 12.1 us
    ppermute x39, waiting for transfers between devices: 26.6 us -> 14.5 us  [swap(): return lax.ppermute(values, axis, [(i, i ^ distance) for i in range(count)])]
    ppermute x11, waiting for transfers between devices: 0.43 us -> 7.11 us  [turn(): lax.ppermute(values, axis, [(i, (i + shift) % count) for i in range(count)])]
    pallas_call x2 -> x4, Pallas kernels: 27 us -> 30.9 us  [the longest x1 14.2 us: hidden_back_of(): pl.pallas_call(functools.partial(hidden_back_kernel, rows // tiles), grid...]
    ppermute x11, starting transfers between devices: 20.5 us -> 24.3 us  [turn(): lax.ppermute(values, axis, [(i, (i + shift) % count) for i in range(count)])]
    concatenate x6 -> x3, other arithmetic: 2.79 us -> 0.1 us  [gather_tensor(): rows, beside = (jnp.concatenate([rows, got], axis=0), ())]
  transfers between devices with their start and end apart: 51 -> 51, of which waited for: 15 -> 16; matrix products, arithmetic and copies ran while one was open for 16% -> 14% of each run, Pallas kernels for 39% -> 41%
where the time goes in v3:
time: 205 us; the launch traced here: 203 us
  Pallas kernels  85.5 us (42%)
  starting transfers between devices  46.6 us (23%)
  waiting for transfers between devices  21.6 us (11%)
  between operations  17.4 us (8%)
  matrix products  13.1 us (6%)
  local copies, waits for them, and re-layouts  12.1 us (6%)
  other arithmetic  7.03 us (3%)
    pallas_call x1, Pallas kernels, mlp_grad(): pl.pallas_call(functools.partial(mlp_grad_kernel, len(pieces), chunk), gr...  28.4 us
    ppermute x11, starting transfers between devices, turn(): lax.ppermute(values, axis, [(i, (i + shift) % count) for i in range(count)])  24.3 us
    ppermute x39, starting transfers between devices, swap(): return lax.ppermute(values, axis, [(i, i ^ distance) for i in range(count)])  22.3 us
    pallas_call x1, Pallas kernels, attend_back(): pl.pallas_call(functools.partial(attend_back_kernel, chunk, slots, scale,...  16.2 us
    ppermute x39, waiting for transfers between devices, swap(): return lax.ppermute(values, axis, [(i, i ^ distance) for i in range(count)])  14.5 us
    pallas_call x1, Pallas kernels, hidden_back_of(): pl.pallas_call(functools.partial(hidden_back_kernel, rows // tiles), grid...  14.2 us
    pallas_call x1, Pallas kernels, attend(): pl.pallas_call(functools.partial(attend_kernel, chunk, slots, scale, shif...  10.1 us
    pallas_call x1, Pallas kernels, mlp(): pl.pallas_call(functools.partial(mlp_kernel, min(512, units)), in_specs=[...  8.04 us
  transfers between devices with their start and end apart: 51, of which 16 were waited for; matrix products, arithmetic and copies ran while one was open for 14% of the time, Pallas kernels for 41%

profile of v3, /device:TPU:0, one launch (start us, length us, event | category | flops | bytes accessed | tf_op | source)
XLA Modules:
  0.0 203.4 jit_solution(13670383912766349220)
XLA Ops:
  8.0 2.8 %shard_map.229 = (bf16[128,2048]{1,0:T(8,128)(2,1)S(1)}, bf16[32,2048]{1,0:T(8,128)(2,1)S(1)}, bf16[128,2048]{1,0:T(8,128)(2,1)S(1)}, bf16[32,2048]{1,0:T(8,128)...) custom-call(s32[4]{0:T(128)S(1)} %get-tuple-element.204.at_ref, ...), custom_call_target="tpu_custom_call" | custom-call | flops 2097152 | bytes 2097152 | tf_op jit(solution)/shard_map/pallas_call | solution.py:195
  10.8 3.1 %collective-permute-start = (bf16[32,2048]{1,0:T(8,128)(2,1)S(1)}, bf16[32,2048]{1,0:T(8,128)(2,1)S(1)}, u32[]{:S(2)}, u32[]{:S(2)}) collective-permute-start(bf16[32,2048]{1,0:T(8,128)(2,1)S(1)} %get-tuple-element.77), channel_id=1, source_target_pairs={{0,4},{4,8},{8,12},{12,0},{1,5},{5,9},{9,13},{13,1},{2,6},{6,10},{... | collective-permute-start | bytes 393224 | tf_op jit(solution)/shard_map/ppermute | solution.py:26
  13.9 2.6 %collective-permute-start.1 = (bf16[32,2048]{1,0:T(8,128)(2,1)S(1)}, bf16[32,2048]{1,0:T(8,128)(2,1)S(1)}, u32[]{:S(2)}, u32[]{:S(2)}) collective-permute-start(bf16[32,2048]{1,0:T(8,128)(2,1)S(1)} %get-tuple-element.77), channel_id=1, source_target_pairs={{0,8},{4,12},{8,0},{12,4},{1,9},{5,13},{9,1},{13,5},{2,10},{6,14},... | collective-permute-start | bytes 393224 | tf_op jit(solution)/shard_map/ppermute | solution.py:26
  16.5 1.3 collective-permute-start.2
  23.1 2.1 %collective-permute-done.1.refs_8_ = bf16[32,2048]{1,0:T(8,128)(2,1)S(1)} collective-permute-done((bf16[32,2048]{1,0:T(8,128)(2,1)S(1)}, bf16[32,2048]{1,0:T(8,128)(2,1)S(1)}, u32[]{:S(2)}, u32[]{:S(2)}) %collective-permute-start.1) | collective-permute-done | bytes 131104 | tf_op jit(solution)/shard_map/ppermute | solution.py:26
  25.2 1.6 collective-permute-start.3
  27.2 1.5 collective-permute-start.5
  28.7 6.3 %convolution_convert_fusion.1.hb_ref = bf16[128,2048]{1,0:T(8,128)(2,1)S(1)} fusion(bf16[128,2048]{1,0:T(8,128)(2,1)S(1)} %get-tuple-element.82, bf16[2048,2048]{1,0:T(8,128)(2,1)} %wd_ref.1), kind=kOutput, calls=%fused_computation.1 | convolution fusion | flops 1074003968 | bytes 9437184 | tf_op jit(solution)/shard_map/dot_general | solution.py:712
  39.5 10.1 %shard_map.230 = (bf16[512,512]{1,0:T(8,128)(2,1)}, bf16[512,512]{1,0:T(8,128)(2,1)}, bf16[512,512]{1,0:T(8,128)(2,1)}, bf16[128,512]{1,0:T(8,128)(2,1)}, f32[4,...) custom-call(s32[16]{0:T(128)} %concatenate.22.at_ref, bf16[32,2048]{1,0:T(8,128)(2,1)} %get-tuple-element.183.refs_0_, ...), custom_call_target="tpu_custom_call" | custom-call | flops 3221225472 | bytes 6291456 | tf_op jit(solution)/shard_map/pallas_call | solution.py:271
  49.7 1.4 convolution_convert_fusion.2
  51.5 1.2 collective-permute-done.12
  52.8 1.6 collective-permute-start.13
  55.2 3.2 %collective-permute-done.13 = bf16[32,2048]{1,0:T(8,128)(2,1)S(1)} collective-permute-done((bf16[32,2048]{1,0:T(8,128)(2,1)S(1)}, bf16[32,2048]{1,0:T(8,128)(2,1)S(1)}, u32[]{:S(2)}, u32[]{:S(2)}) %collective-permute-start.13) | collective-permute-done | bytes 131104 | tf_op jit(solution)/shard_map/ppermute | solution.py:21
  58.7 1.6 collective-permute-start.14
  60.3 5.8 %shard_map.231 = (bf16[2048,2048]{1,0:T(8,128)(2,1)S(1)}, bf16[2048,2048]{1,0:T(8,128)(2,1)S(1)}) custom-call(bf16[2048,2048]{1,0:T(8,128)(2,1)} %refs_13_.1, bf16[2048,2048]{1,0:T(8,128)(2,1)} %refs_14_.1), custom_call_target="tpu_custom_call" | custom-call | tf_op jit(solution)/shard_map/pallas_call | solution.py:144
  67.4 6.0 %collective-permute-start.16 = (bf16[32,2048]{1,0:T(8,128)(2,1)S(1)}, bf16[32,2048]{1,0:T(8,128)(2,1)S(1)}, u32[]{:S(2)}, u32[]{:S(2)}) collective-permute-start(bf16[32,2048]{1,0:T(8,128)(2,1)S(1)} %multiply_convert_fusion), channel_id=1, source_target_pairs={{0,4},{4,8},{8,12},{12,0},{1,5},{5,9},{9,13},{13,1},{2,6},{6,10},{... | collective-permute-start | bytes 393224 | tf_op jit(solution)/shard_map/ppermute | solution.py:26
  73.4 2.5 %collective-permute-start.18 = (bf16[32,2048]{1,0:T(8,128)(2,1)S(1)}, bf16[32,2048]{1,0:T(8,128)(2,1)S(1)}, u32[]{:S(2)}, u32[]{:S(2)}) collective-permute-start(bf16[32,2048]{1,0:T(8,128)(2,1)S(1)} %multiply_convert_fusion), channel_id=1, source_target_pairs={{0,12},{4,0},{8,4},{12,8},{1,13},{5,1},{9,5},{13,9},{2,14},{6,2},{... | collective-permute-start | bytes 393224 | tf_op jit(solution)/shard_map/ppermute | solution.py:26
  75.9 8.0 %shard_map.232 = (bf16[128,2048]{1,0:T(8,128)(2,1)S(1)}, bf16[128,2048]{1,0:T(8,128)(2,1)S(1)}, bf16[128,2048]{1,0:T(8,128)(2,1)S(1)}, bf16[128,2048]{1,0:T(8,128)(2,1)S(1)}) custom-call(bf16[128,2048]{1,0:T(8,128)(2,1)S(1)} %pad_maximum_fusion.x_ref, bf16[128,2048]{1,0:T(8,128)(2,1)S(1)} %convolution_convert_fusion.1.hb_ref, ...), custom_call_target="tpu_custom_call" | custom-call | tf_op jit(solution)/shard_map/pallas_call | solution.py:474
  83.9 2.1 %collective-permute-done.17 = bf16[32,2048]{1,0:T(8,128)(2,1)S(1)} collective-permute-done((bf16[32,2048]{1,0:T(8,128)(2,1)S(1)}, bf16[32,2048]{1,0:T(8,128)(2,1)S(1)}, u32[]{:S(2)}, u32[]{:S(2)}) %collective-permute-start.17) | collective-permute-done | bytes 131104 | tf_op jit(solution)/shard_map/ppermute | solution.py:26
  90.0 1.5 collective-permute-start.25
  92.4 1.8 collective-permute-done.20
  95.5 3.4 %collective-permute-start.21 = (bf16[32,2048]{1,0:T(8,128)(2,1)S(1)}, bf16[32,2048]{1,0:T(8,128)(2,1)S(1)}, u32[]{:S(2)}, u32[]{:S(2)}) collective-permute-start(bf16[32,2048]{1,0:T(8,128)(2,1)S(1)} %get-tuple-element.104.refs_0_), channel_id=1, source_target_pairs={{0,4},{4,8},{8,12},{12,0},{1,5},{5,9},{9,13},{13,1},{2,6},{6,10},{... | collective-permute-start | bytes 393224 | tf_op jit(solution)/shard_map/ppermute | solution.py:26
  98.9 2.1 %collective-permute-start.22 = (bf16[32,2048]{1,0:T(8,128)(2,1)S(1)}, bf16[32,2048]{1,0:T(8,128)(2,1)S(1)}, u32[]{:S(2)}, u32[]{:S(2)}) collective-permute-start(bf16[32,2048]{1,0:T(8,128)(2,1)S(1)} %get-tuple-element.104.refs_0_), channel_id=1, source_target_pairs={{0,8},{4,12},{8,0},{12,4},{1,9},{5,13},{9,1},{13,5},{2,10},{6,14},... | collective-permute-start | bytes 393224 | tf_op jit(solution)/shard_map/ppermute | solution.py:26
  101.3 2.9 %collective-permute-done.25.refs_2_ = bf16[128,2048]{1,0:T(8,128)(2,1)S(1)} collective-permute-done((bf16[128,2048]{1,0:T(8,128)(2,1)}, bf16[128,2048]{1,0:T(8,128)(2,1)S(1)}, u32[]{:S(2)}, u32[]{:S(2)}) %collective-permute-start.25) | collective-permute-done | bytes 524320 | tf_op jit(solution)/shard_map/ppermute | solution.py:26
  105.2 14.2 %shard_map.233.refs_11_ = bf16[1024,2048]{1,0:T(8,128)(2,1)} custom-call(s32[8]{0:T(128)} %copy-done.26, bf16[1024,2048]{1,0:T(8,128)(2,1)} %all-gather.2.cloned.1.call-done.cot_hbm.refs_12_, bf16[2048,2048]{1,0:T(8,128)(2,1)} %wd_ref.1), custom_call_target="tpu_custom_call" | custom-call | flops 8589934592 | bytes 12582912 | tf_op jit(solution)/shard_map/pallas_call | solution.py:519
  122.7 5.5 %convolution_convert_fusion.refs_23_ = bf16[128,2048]{1,0:T(8,128)(2,1)} fusion(bf16[128,2048]{1,0:T(8,128)(2,1)S(1)} %get-tuple-element.110.refs_8_, bf16[2048,2048]{1,0:T(8,128)(2,1)} %wd_ref.1), kind=kOutput, calls=%fused_computation | convolution fusion | flops 1074003968 | bytes 9437184 | tf_op jit(solution)/shard_map/dot_general | solution.py:756
  133.2 16.2 %shard_map.234 = (f32[4,256,512]{2,1,0:T(8,128)}, bf16[1,4,256,512]{3,2,1,0:T(8,128)(2,1)}, bf16[64,4096]{1,0:T(8,128)(2,1)}, bf16[64,4096]{1,0:T(8,128)(2,1)}) custom-call(s32[16]{0:T(128)} %concatenate.22.at_ref, s32[2]{0:T(128)} %add_multiply_fusion.starts_ref, bf16[32,2048]{1,0:T(8,128)(2,1)} %copy-done.5, bf16[32,2048]{1,0:T(8,128)(2,1)} %copy-done.10, ...), custom_call_target="tpu_custom_call" | custom-call | flops 2952790016 | bytes 9437184 | tf_op jit(solution)/shard_map/pallas_call | solution.py:413
  150.5 1.5 collective-permute-start.47
  155.4 28.4 %shard_map.235 = (f32[256,2048]{1,0:T(8,128)}, f32[256,2048]{1,0:T(8,128)}, f32[2048,256]{1,0:T(8,128)}, f32[1,256]{1,0:T(1,128)}) custom-call(s32[45]{0:T(128)} %concatenate.23.at_ref, bf16[128,2048]{1,0:T(8,128)(2,1)} %constant_dynamic-update-slice_fusion.refs_0_, bf16[128,2048]{1,0:T(8,128)(2,1)} %copy-done.28, bf16[128,2048]{1,0:T(8,128)(2,1)} %copy-done.27, ...), custom_call_target="tpu_custom_call" | custom-call | flops 20401094656 | bytes 25165824 | tf_op jit(solution)/shard_map/pallas_call | solution.py:619
  185.8 2.4 %add_reduce_fusion = (f32[256]{0:T(256)S(1)}, f32[256,512]{1,0:T(8,128)}, f32[256,512]{1,0:T(8,128)}, f32[256,512]{1,0:T(8,128)}) fusion(bf16[2048,512]{1,0:T(8,128)(2,1)} %refs_27_.1, s32[]{:T(128)S(6)} %select_n.127, bf16[2048,512]{1,0:T(8,128)(2,1)} %refs_26_.1, bf16[2048,512]{1,0:T(8,128)(2,1)} %refs_25_.1, f32[4,256,512]{2,1,0:T(8,128)S(1)} %convert_add_fusion), kind=kLoop, calls=%fused_computation.15 | loop fusion | flops 1179392 | bytes 3933188 | tf_op jit(solution)/shard_map/reduce_sum | solution.py:793
  190.4 2.4 %collective-permute-done.45 = bf16[32,4096]{1,0:T(8,128)(2,1)S(1)} collective-permute-done((bf16[32,4096]{1,0:T(8,128)(2,1)S(1)}, bf16[32,4096]{1,0:T(8,128)(2,1)S(1)}, u32[]{:S(2)}, u32[]{:S(2)}) %collective-permute-start.45) | collective-permute-done | bytes 262176 | tf_op jit(solution)/shard_map/ppermute | solution.py:21
  193.5 1.3 collective-permute-done.49
  (230 shorter events, 37.8 us)
Async XLA Ops:
  7.2 94.1 %all-gather.2.cloned.1.call-start = ((), (), s32[]{:S(2)}) async-start(), calls=%async_computation | async-start | bytes 4325376 | tf_op jit(solution)/shard_map/all_gather | solution.py:679
  10.8 12.2 %collective-permute-start = (bf16[32,2048]{1,0:T(8,128)(2,1)S(1)}, bf16[32,2048]{1,0:T(8,128)(2,1)S(1)}, u32[]{:S(2)}, u32[]{:S(2)}) collective-permute-start(bf16[32,2048]{1,0:T(8,128)(2,1)S(1)} %get-tuple-element.77), channel_id=1, source_target_pairs={{0,4},{4,8},{8,12},{12,0},{1,5},{5,9},{9,13},{13,1},{2,6},{6,10},{... | collective-permute-start | bytes 393224 | tf_op jit(solution)/shard_map/ppermute | solution.py:26
  13.9 11.2 %collective-permute-start.1 = (bf16[32,2048]{1,0:T(8,128)(2,1)S(1)}, bf16[32,2048]{1,0:T(8,128)(2,1)S(1)}, u32[]{:S(2)}, u32[]{:S(2)}) collective-permute-start(bf16[32,2048]{1,0:T(8,128)(2,1)S(1)} %get-tuple-element.77), channel_id=1, source_target_pairs={{0,8},{4,12},{8,0},{12,4},{1,9},{5,13},{9,1},{13,5},{2,10},{6,14},... | collective-permute-start | bytes 393224 | tf_op jit(solution)/shard_map/ppermute | solution.py:26
  16.5 8.6 %collective-permute-start.2 = (bf16[32,2048]{1,0:T(8,128)(2,1)S(1)}, bf16[32,2048]{1,0:T(8,128)(2,1)S(1)}, u32[]{:S(2)}, u32[]{:S(2)}) collective-permute-start(bf16[32,2048]{1,0:T(8,128)(2,1)S(1)} %get-tuple-element.77), channel_id=1, source_target_pairs={{0,12},{4,0},{8,4},{12,8},{1,13},{5,1},{9,5},{13,9},{2,14},{6,2},{... | collective-permute-start | bytes 393224 | tf_op jit(solution)/shard_map/ppermute | solution.py:26
  25.2 9.9 %collective-permute-start.3 = (bf16[32,2048]{1,0:T(8,128)(2,1)S(1)}, bf16[32,2048]{1,0:T(8,128)(2,1)S(1)}, u32[]{:S(2)}, u32[]{:S(2)}) collective-permute-start(bf16[32,2048]{1,0:T(8,128)(2,1)S(1)} %collective-permute-done.refs_4_), channel_id=1, source_target_pairs={{0,2},{1,3},{2,0},{3,1},{4,6},{5,7},{6,4},{7,5},{8,10},{9,11},{10,... | collective-permute-start | bytes 393224 | tf_op jit(solution)/shard_map/ppermute | solution.py:21
  26.7 8.3 %collective-permute-start.4 = (bf16[32,2048]{1,0:T(8,128)(2,1)S(1)}, bf16[32,2048]{1,0:T(8,128)(2,1)S(1)}, u32[]{:S(2)}, u32[]{:S(2)}) collective-permute-start(bf16[32,2048]{1,0:T(8,128)(2,1)S(1)} %collective-permute-done.1.refs_8_), channel_id=1, source_target_pairs={{0,2},{1,3},{2,0},{3,1},{4,6},{5,7},{6,4},{7,5},{8,10},{9,11},{10,... | collective-permute-start | bytes 393224 | tf_op jit(solution)/shard_map/ppermute | solution.py:21
  27.2 8.9 %collective-permute-start.5 = (bf16[32,2048]{1,0:T(8,128)(2,1)S(1)}, bf16[32,2048]{1,0:T(8,128)(2,1)S(1)}, u32[]{:S(2)}, u32[]{:S(2)}) collective-permute-start(bf16[32,2048]{1,0:T(8,128)(2,1)S(1)} %collective-permute-done.2.refs_12_), channel_id=1, source_target_pairs={{0,2},{1,3},{2,0},{3,1},{4,6},{5,7},{6,4},{7,5},{8,10},{9,11},{10,... | collective-permute-start | bytes 393224 | tf_op jit(solution)/shard_map/ppermute | solution.py:21
  52.8 5.7 %collective-permute-start.13 = (bf16[32,2048]{1,0:T(8,128)(2,1)S(1)}, bf16[32,2048]{1,0:T(8,128)(2,1)S(1)}, u32[]{:S(2)}, u32[]{:S(2)}) collective-permute-start(bf16[32,2048]{1,0:T(8,128)(2,1)S(1)} %slice.205), channel_id=1, source_target_pairs={{0,2},{1,3},{2,0},{3,1},{4,6},{5,7},{6,4},{7,5},{8,10},{9,11},{10,... | collective-permute-start | bytes 393224 | tf_op jit(solution)/shard_map/ppermute | solution.py:21
  58.7 8.6 %collective-permute-start.14 = (bf16[32,2048]{1,0:T(8,128)(2,1)S(1)}, bf16[32,2048]{1,0:T(8,128)(2,1)S(1)}, u32[]{:S(2)}, u32[]{:S(2)}) collective-permute-start(bf16[32,2048]{1,0:T(8,128)(2,1)S(1)} %multiply_convert_fusion), channel_id=1, source_target_pairs={{0,2},{1,3},{2,0},{3,1},{4,6},{5,7},{6,4},{7,5},{8,10},{9,11},{10,... | collective-permute-start | bytes 393224 | tf_op jit(solution)/shard_map/ppermute | solution.py:21
  67.3 8.5 %collective-permute-start.15 = (bf16[64,2048]{1,0:T(8,128)(2,1)S(1)}, bf16[64,2048]{1,0:T(8,128)(2,1)S(1)}, u32[]{:S(2)}, u32[]{:S(2)}) collective-permute-start(bf16[64,2048]{1,0:T(8,128)(2,1)S(1)} %pad_maximum_fusion.2), channel_id=1, source_target_pairs={{0,1},{1,0},{2,3},{3,2},{4,5},{5,4},{6,7},{7,6},{8,9},{9,8},{10,11... | collective-permute-start | bytes 786440 | tf_op jit(solution)/shard_map/ppermute | solution.py:21
  67.4 16.6 %collective-permute-start.16 = (bf16[32,2048]{1,0:T(8,128)(2,1)S(1)}, bf16[32,2048]{1,0:T(8,128)(2,1)S(1)}, u32[]{:S(2)}, u32[]{:S(2)}) collective-permute-start(bf16[32,2048]{1,0:T(8,128)(2,1)S(1)} %multiply_convert_fusion), channel_id=1, source_target_pairs={{0,4},{4,8},{8,12},{12,0},{1,5},{5,9},{9,13},{13,1},{2,6},{6,10},{... | collective-permute-start | bytes 393224 | tf_op jit(solution)/shard_map/ppermute | solution.py:26
  73.4 12.7 %collective-permute-start.17 = (bf16[32,2048]{1,0:T(8,128)(2,1)S(1)}, bf16[32,2048]{1,0:T(8,128)(2,1)S(1)}, u32[]{:S(2)}, u32[]{:S(2)}) collective-permute-start(bf16[32,2048]{1,0:T(8,128)(2,1)S(1)} %multiply_convert_fusion), channel_id=1, source_target_pairs={{0,8},{4,12},{8,0},{12,4},{1,9},{5,13},{9,1},{13,5},{2,10},{6,14},... | collective-permute-start | bytes 393224 | tf_op jit(solution)/shard_map/ppermute | solution.py:26
  73.4 12.7 %collective-permute-start.18 = (bf16[32,2048]{1,0:T(8,128)(2,1)S(1)}, bf16[32,2048]{1,0:T(8,128)(2,1)S(1)}, u32[]{:S(2)}, u32[]{:S(2)}) collective-permute-start(bf16[32,2048]{1,0:T(8,128)(2,1)S(1)} %multiply_convert_fusion), channel_id=1, source_target_pairs={{0,12},{4,0},{8,4},{12,8},{1,13},{5,1},{9,5},{13,9},{2,14},{6,2},{... | collective-permute-start | bytes 393224 | tf_op jit(solution)/shard_map/ppermute | solution.py:26
  88.2 6.0 %collective-permute-start.20 = (bf16[32,2048]{1,0:T(8,128)(2,1)S(1)}, bf16[32,2048]{1,0:T(8,128)(2,1)S(1)}, u32[]{:S(2)}, u32[]{:S(2)}) collective-permute-start(bf16[32,2048]{1,0:T(8,128)(2,1)S(1)} %slice.204), channel_id=1, source_target_pairs={{0,2},{1,3},{2,0},{3,1},{4,6},{5,7},{6,4},{7,5},{8,10},{9,11},{10,... | collective-permute-start | bytes 393224 | tf_op jit(solution)/shard_map/ppermute | solution.py:21
  90.0 14.2 %collective-permute-start.25 = (bf16[128,2048]{1,0:T(8,128)(2,1)}, bf16[128,2048]{1,0:T(8,128)(2,1)S(1)}, u32[]{:S(2)}, u32[]{:S(2)}) collective-permute-start(bf16[128,2048]{1,0:T(8,128)(2,1)} %constant_dynamic-update-slice_fusion.refs_0_), channel_id=1, source_target_pairs={{0,16},{16,0},{1,17},{17,1},{2,18},{18,2},{3,19},{19,3},{4,20},{20... | collective-permute-start | bytes 1572872 | tf_op jit(solution)/shard_map/ppermute | solution.py:26
  91.5 28.0 %collective-permute-start.26 = (bf16[128,2048]{1,0:T(8,128)(2,1)}, bf16[128,2048]{1,0:T(8,128)(2,1)S(1)}, u32[]{:S(2)}, u32[]{:S(2)}) collective-permute-start(bf16[128,2048]{1,0:T(8,128)(2,1)} %constant_dynamic-update-slice_fusion.refs_0_), channel_id=1, source_target_pairs={{0,2},{1,3},{2,0},{3,1},{4,6},{5,7},{6,4},{7,5},{8,10},{9,11},{10,... | collective-permute-start | bytes 1572872 | tf_op jit(solution)/shard_map/ppermute | solution.py:21
  95.5 24.0 %collective-permute-start.21 = (bf16[32,2048]{1,0:T(8,128)(2,1)S(1)}, bf16[32,2048]{1,0:T(8,128)(2,1)S(1)}, u32[]{:S(2)}, u32[]{:S(2)}) collective-permute-start(bf16[32,2048]{1,0:T(8,128)(2,1)S(1)} %get-tuple-element.104.refs_0_), channel_id=1, source_target_pairs={{0,4},{4,8},{8,12},{12,0},{1,5},{5,9},{9,13},{13,1},{2,6},{6,10},{... | collective-permute-start | bytes 393224 | tf_op jit(solution)/shard_map/ppermute | solution.py:26
  98.9 20.7 %collective-permute-start.22 = (bf16[32,2048]{1,0:T(8,128)(2,1)S(1)}, bf16[32,2048]{1,0:T(8,128)(2,1)S(1)}, u32[]{:S(2)}, u32[]{:S(2)}) collective-permute-start(bf16[32,2048]{1,0:T(8,128)(2,1)S(1)} %get-tuple-element.104.refs_0_), channel_id=1, source_target_pairs={{0,8},{4,12},{8,0},{12,4},{1,9},{5,13},{9,1},{13,5},{2,10},{6,14},... | collective-permute-start | bytes 393224 | tf_op jit(solution)/shard_map/ppermute | solution.py:26
  101.0 18.6 %collective-permute-start.23 = (bf16[32,2048]{1,0:T(8,128)(2,1)S(1)}, bf16[32,2048]{1,0:T(8,128)(2,1)S(1)}, u32[]{:S(2)}, u32[]{:S(2)}) collective-permute-start(bf16[32,2048]{1,0:T(8,128)(2,1)S(1)} %get-tuple-element.104.refs_0_), channel_id=1, source_target_pairs={{0,12},{4,0},{8,4},{12,8},{1,13},{5,1},{9,5},{13,9},{2,14},{6,2},{... | collective-permute-start | bytes 393224 | tf_op jit(solution)/shard_map/ppermute | solution.py:26
  104.2 15.3 %collective-permute-start.24 = (bf16[32,2048]{1,0:T(8,128)(2,1)S(1)}, bf16[32,2048]{1,0:T(8,128)(2,1)S(1)}, u32[]{:S(2)}, u32[]{:S(2)}) collective-permute-start(bf16[32,2048]{1,0:T(8,128)(2,1)S(1)} %get-tuple-element.104.refs_0_), channel_id=1, source_target_pairs={{0,2},{1,3},{2,0},{3,1},{4,6},{5,7},{6,4},{7,5},{8,10},{9,11},{10,... | collective-permute-start | bytes 393224 | tf_op jit(solution)/shard_map/ppermute | solution.py:21
  119.6 9.1 %collective-permute-start.29 = (bf16[32,2048]{1,0:T(8,128)(2,1)S(1)}, bf16[32,2048]{1,0:T(8,128)(2,1)S(1)}, u32[]{:S(2)}, u32[]{:S(2)}) collective-permute-start(bf16[32,2048]{1,0:T(8,128)(2,1)S(1)} %collective-permute-done.21.refs_4_), channel_id=1, source_target_pairs={{0,2},{1,3},{2,0},{3,1},{4,6},{5,7},{6,4},{7,5},{8,10},{9,11},{10,... | collective-permute-start | bytes 393224 | tf_op jit(solution)/shard_map/ppermute | solution.py:21
  120.7 8.0 %collective-permute-start.30 = (bf16[32,2048]{1,0:T(8,128)(2,1)S(1)}, bf16[32,2048]{1,0:T(8,128)(2,1)S(1)}, u32[]{:S(2)}, u32[]{:S(2)}) collective-permute-start(bf16[32,2048]{1,0:T(8,128)(2,1)S(1)} %collective-permute-done.22.refs_8_), channel_id=1, source_target_pairs={{0,2},{1,3},{2,0},{3,1},{4,6},{5,7},{6,4},{7,5},{8,10},{9,11},{10,... | collective-permute-start | bytes 393224 | tf_op jit(solution)/shard_map/ppermute | solution.py:21
  121.7 8.1 %collective-permute-start.31 = (bf16[32,2048]{1,0:T(8,128)(2,1)S(1)}, bf16[32,2048]{1,0:T(8,128)(2,1)S(1)}, u32[]{:S(2)}, u32[]{:S(2)}) collective-permute-start(bf16[32,2048]{1,0:T(8,128)(2,1)S(1)} %collective-permute-done.23.refs_12_), channel_id=1, source_target_pairs={{0,2},{1,3},{2,0},{3,1},{4,6},{5,7},{6,4},{7,5},{8,10},{9,11},{10,... | collective-permute-start | bytes 393224 | tf_op jit(solution)/shard_map/ppermute | solution.py:21
  128.2 2.6 %collective-permute-start.28 = (bf16[32,2048]{1,0:T(8,128)(2,1)S(1)}, bf16[32,2048]{1,0:T(8,128)(2,1)S(1)}, u32[]{:S(2)}, u32[]{:S(2)}) collective-permute-start(bf16[32,2048]{1,0:T(8,128)(2,1)S(1)} %collective-permute-done.24.refs_1_), channel_id=1, source_target_pairs={{0,1},{1,0},{2,3},{3,2},{4,5},{5,4},{6,7},{7,6},{8,9},{9,8},{10,11... | collective-permute-start | bytes 393224 | tf_op jit(solution)/shard_map/ppermute | solution.py:21
  131.4 19.1 %collective-permute-start.40 = (bf16[128,2048]{1,0:T(8,128)(2,1)S(1)}, bf16[128,2048]{1,0:T(8,128)(2,1)}, u32[]{:S(2)}, u32[]{:S(2)}) collective-permute-start(bf16[128,2048]{1,0:T(8,128)(2,1)S(1)} %collective-permute-done.25.refs_2_), channel_id=1, source_target_pairs={{0,2},{1,3},{2,0},{3,1},{4,6},{5,7},{6,4},{7,5},{8,10},{9,11},{10,... | collective-permute-start | bytes 1572872 | tf_op jit(solution)/shard_map/ppermute | solution.py:21
  149.7 3.5 %collective-permute-start.41 = (bf16[128,2048]{1,0:T(8,128)(2,1)}, bf16[128,2048]{1,0:T(8,128)(2,1)S(1)}, u32[]{:S(2)}, u32[]{:S(2)}) collective-permute-start(bf16[128,2048]{1,0:T(8,128)(2,1)} %constant_dynamic-update-slice_fusion.refs_0_), channel_id=1, source_target_pairs={{0,1},{1,0},{2,3},{3,2},{4,5},{5,4},{6,7},{7,6},{8,9},{9,8},{10,11... | collective-permute-start | bytes 1572872 | tf_op jit(solution)/shard_map/ppermute | solution.py:21
  150.0 4.2 %collective-permute-start.43 = (bf16[128,2048]{1,0:T(8,128)(2,1)S(1)}, bf16[128,2048]{1,0:T(8,128)(2,1)S(1)}, u32[]{:S(2)}, u32[]{:S(2)}) collective-permute-start(bf16[128,2048]{1,0:T(8,128)(2,1)S(1)} %collective-permute-done.25.refs_2_), channel_id=1, source_target_pairs={{0,1},{1,0},{2,3},{3,2},{4,5},{5,4},{6,7},{7,6},{8,9},{9,8},{10,11... | collective-permute-start | bytes 1572872 | tf_op jit(solution)/shard_map/ppermute | solution.py:21
  150.2 4.0 %collective-permute-start.42 = (bf16[128,2048]{1,0:T(8,128)(2,1)S(1)}, bf16[128,2048]{1,0:T(8,128)(2,1)S(1)}, u32[]{:S(2)}, u32[]{:S(2)}) collective-permute-start(bf16[128,2048]{1,0:T(8,128)(2,1)S(1)} %collective-permute-done.26.refs_1_), channel_id=1, source_target_pairs={{0,1},{1,0},{2,3},{3,2},{4,5},{5,4},{6,7},{7,6},{8,9},{9,8},{10,11... | collective-permute-start | bytes 1572872 | tf_op jit(solution)/shard_map/ppermute | solution.py:21
  150.5 34.9 %collective-permute-start.47 = (bf16[4,256,512]{2,1,0:T(8,128)(2,1)}, bf16[4,256,512]{2,1,0:T(8,128)(2,1)S(1)}, u32[]{:S(2)}, u32[]{:S(2)}) collective-permute-start(bf16[4,256,512]{2,1,0:T(8,128)(2,1)} %bitcast.50), channel_id=1, source_target_pairs={{0,16},{16,0},{1,17},{17,1},{2,18},{18,2},{3,19},{19,3},{4,20},{20... | collective-permute-start | bytes 3145736 | tf_op jit(solution)/shard_map/ppermute | solution.py:26
  153.2 30.5 %collective-permute-start.39 = (bf16[32,4096]{1,0:T(8,128)(2,1)S(1)}, bf16[32,4096]{1,0:T(8,128)(2,1)S(1)}, u32[]{:S(2)}, u32[]{:S(2)}) collective-permute-start(bf16[32,4096]{1,0:T(8,128)(2,1)S(1)} %slice.203), channel_id=1, source_target_pairs={{0,2},{1,3},{2,0},{3,1},{4,6},{5,7},{6,4},{7,5},{8,10},{9,11},{10,... | collective-permute-start | bytes 786440 | tf_op jit(solution)/shard_map/ppermute | solution.py:21
  184.3 8.5 %collective-permute-start.45 = (bf16[32,4096]{1,0:T(8,128)(2,1)S(1)}, bf16[32,4096]{1,0:T(8,128)(2,1)S(1)}, u32[]{:S(2)}, u32[]{:S(2)}) collective-permute-start(bf16[32,4096]{1,0:T(8,128)(2,1)S(1)} %get-tuple-element.184), channel_id=1, source_target_pairs={{0,2},{1,3},{2,0},{3,1},{4,6},{5,7},{6,4},{7,5},{8,10},{9,11},{10,... | collective-permute-start | bytes 786440 | tf_op jit(solution)/shard_map/ppermute | solution.py:21
  188.2 4.7 %collective-permute-start.48 = (f32[2,256]{1,0:T(2,128)S(1)}, f32[2,256]{1,0:T(2,128)S(1)}, u32[]{:S(2)}, u32[]{:S(2)}) collective-permute-start(f32[2,256]{1,0:T(2,128)S(1)} %pad_maximum_fusion.4), channel_id=1, source_target_pairs={{0,2},{1,3},{2,0},{3,1},{4,6},{5,7},{6,4},{7,5},{8,10},{9,11},{10,... | collective-permute-start | bytes 6152 | tf_op jit(solution)/shard_map/ppermute | solution.py:21
  (64 other events, 384.3 us)
Sparse Core Ops, SparseCore 0:
  11.4 74.7 all-gather.1

commit v4 on v3

--- a/solution.py
+++ b/solution.py
@@ -70,7 +70,7 @@
 
 
 def ring_of(rows):
-    return [rows] + [turn(rows, "ctx", k) for k in range(1, lax.axis_size("ctx"))]
+    return [rows] + [swap(rows, "ctx", k) for k in range(1, lax.axis_size("ctx"))]
 
 
 def from_slots(blocks, slots, place):
@@ -485,57 +485,112 @@
     )(x, hidden_back, in_vmem(wg), in_vmem(wu))
 
 
-def hidden_back_kernel(tile, at_ref, cot_hbm, wd_ref, out_ref, cot, sem):
+def tiles_of(sources, at_ref, first, tile):
+    listed = []
+    for n, source in enumerate(sources):
+        for i in range(source.shape[0] // tile):
+            index = at_ref[first + i] if n == 0 else i
+            at = pl.ds(pl.multiple_of(index * tile, tile), tile) if n == 0 else pl.ds(i * tile, tile)
+            listed.append((source, at))
+    return listed
+
+
+def hidden_back_kernel(tile, more, count, at_ref, *refs):
+    sources, (wd_ref, hidden_ref, before) = refs[:count], refs[count : count + 3]
+    out_ref, sum_ref, cot, total, sem = refs[-5:]
+    step, block = pl.program_id(0), wd_ref.shape[0]
     copies = []
-    for i in range(cot.shape[0] // tile):
-        source = pl.ds(pl.multiple_of(at_ref[i] * tile, tile), tile)
+    for i, (source, at) in enumerate(tiles_of(sources, at_ref, 0, tile)):
         target = cot.at[pl.ds(i * tile, tile)]
-        copies.append(pltpu.make_async_copy(cot_hbm.at[source], target, sem.at[i]))
+        copies.append(pltpu.make_async_copy(source.at[at], target, sem.at[i]))
 
     def every_tile(waits):
         wd = wd_ref[...]
+        own = dot(hidden_ref[...], wd)
         for i in range(0, len(copies), 2):
             if waits:
                 copies[i].wait()
                 copies[i + 1].wait()
             at = pl.ds(i * tile, 2 * tile)
             out_ref[at, :] = dot_nt(cot[at, :], wd).astype(BF)
-
-    @pl.when(pl.program_id(0) == 0)
+        return own
+
+    @pl.when(step == 0)
     def _():
         for copy in copies:
             copy.start()
-        every_tile(True)
-
-    @pl.when(pl.program_id(0) > 0)
-    def _():
-        every_tile(False)
-
-
-def hidden_back_of(turns, cot, wd):
-    rows, width = cot.shape
-    units, tiles = wd.shape[0], turns.shape[0]
-    block = min(512, units)
+        own = every_tile(True)
+        total[...] = own + before[...] if more else own
+
+    @pl.when(step > 0)
+    def _():
+        total[...] += every_tile(False)
+
+    @pl.when(step == pl.num_programs(0) - 1)
+    def _():
+        sum_ref[...] = total[...].astype(sum_ref.dtype)
+
+
+def hidden_back_of(turns, cots, wd, hidden, part, before=()):
+    width = cots[0].shape[1]
+    rows, units = sum(cot.shape[0] for cot in cots), wd.shape[0]
+    tiles = rows // hidden.shape[0]
+    block = min(512, units // 2)
+    steps = units // 2 // block
+    skip = part * steps
+    tile = hidden.shape[0]
+    whole = pl.BlockSpec((tile, width), lambda i: (0, 0), pipeline_mode=pl.Buffered(1))
     return pl.pallas_call(
-        functools.partial(hidden_back_kernel, rows // tiles),
-        grid=(units // block,),
-        in_specs=[pl.BlockSpec(memory_space=pltpu.SMEM), HBM_WHOLE,
-                  pl.BlockSpec((block, width), lambda i: (i, 0))],
-        out_specs=pl.BlockSpec((rows, block), lambda i: (0, i)),
-        out_shape=jax.ShapeDtypeStruct((rows, units), BF),
-        scratch_shapes=[pltpu.VMEM((rows, width), BF), pltpu.SemaphoreType.DMA((tiles,))],
+        functools.partial(hidden_back_kernel, tile, len(before) > 0, len(cots)),
+        grid=(steps,),
+        in_specs=[pl.BlockSpec(memory_space=pltpu.SMEM)] + [HBM_WHOLE] * len(cots)
+        + [pl.BlockSpec((block, width), lambda i: (i + skip, 0)),
+           pl.BlockSpec((tile, block), lambda i: (0, i + skip))]
+        + [whole, HBM_WHOLE][: len(before)],
+        out_specs=[pl.BlockSpec((rows, block), lambda i: (0, i + skip)), whole],
+        out_shape=[jax.ShapeDtypeStruct((rows, units), BF),
+                   jax.ShapeDtypeStruct((tile, width), BF if part else F32)],
+        scratch_shapes=[pltpu.VMEM((rows, width), BF), pltpu.VMEM((tile, width), F32),
+                        pltpu.SemaphoreType.DMA((tiles,))],
+        input_output_aliases={len(cots) + 4: 0} if before else {},
         compiler_params=pltpu.CompilerParams(vmem_limit_bytes=56 * MIB),
         cost_estimate=pl.CostEstimate(
-            flops=2 * rows * width * units, bytes_accessed=2 * width * (rows + units),
+            flops=rows * width * units, bytes_accessed=2 * width * (rows + units),
             transcendentals=0,
         ),
-    )(turns, in_hbm(cot), in_hbm(wd))
-
-
-def mlp_grad_kernel(count, chunk, at_ref, *refs):
-    pieces = refs[:count]
-    (own_hid, own_gate, own_up, hb_ref, cot_hbm, wg_ref, wu_ref, gg_ref, ug_ref, dg_ref, gain_ref,
-     x_all, cb, hid, gbk, ubk, gain_sum, sem, cot_sem) = refs[count:]
+    )(turns, *[in_hbm(cot) for cot in cots], in_hbm(wd), hidden, *before)
+
+
+def join_kernel(count, *refs):
+    pieces, out_ref, sem = refs[:count], refs[count], refs[-1]
+    size = pieces[0].shape[0]
+    copies = [
+        pltpu.make_async_copy(piece, out_ref.at[pl.ds(i * size, size)], sem.at[i])
+        for i, piece in enumerate(pieces)
+    ]
+    for copy in copies:
+        copy.start()
+    for copy in copies:
+        copy.wait()
+
+
+def join(pieces):
+    size, width = pieces[0].shape
+    return pl.pallas_call(
+        functools.partial(join_kernel, len(pieces)),
+        in_specs=[HBM_WHOLE] * len(pieces),
+        out_specs=pl.BlockSpec(memory_space=pl.ANY),
+        out_shape=jax.ShapeDtypeStruct((size * len(pieces), width), BF),
+        scratch_shapes=[pltpu.SemaphoreType.DMA((len(pieces),))],
+        compiler_params=pltpu.CompilerParams(vmem_limit_bytes=2 * MIB),
+        cost_estimate=pl.CostEstimate(flops=0, bytes_accessed=0, transcendentals=0),
+    )(*pieces)
+
+
+def mlp_grad_kernel(count, chunk, parts, at_ref, *refs):
+    pieces, cots, refs = refs[:count], refs[count : count + parts], refs[count + parts :]
+    (own_hid, own_gate, own_up, hb_ref, wg_ref, wu_ref, gg_ref, ug_ref, dg_ref, gain_ref,
+     x_all, cb, hid, gbk, ubk, gain_sum, sem, cot_sem) = refs
     size = cb.shape[1]
     tile = pieces[0].shape[0]
     per = tile // chunk
@@ -551,15 +606,15 @@
             copies.append(pltpu.make_async_copy(part, x_all.at[spot], sem.at[i]))
         base = 1 + count * per
         for i in range(per):
-            spot = pl.ds(pl.multiple_of(at_ref[base + tiles + i] * chunk, chunk), chunk)
+            spot = pl.ds(pl.multiple_of(at_ref[base + i] * chunk, chunk), chunk)
             target = cb.at[pl.ds(i * chunk, chunk)]
-            copies.append(pltpu.make_async_copy(cot_hbm.at[spot, own], target, cot_sem.at[i]))
-        for i in range(1, tiles):
-            spot = pl.ds(pl.multiple_of(at_ref[base + i] * tile, tile), tile)
-            target = cb.at[pl.ds(i * tile, tile)]
-            copies.append(
-                pltpu.make_async_copy(cot_hbm.at[spot, own], target, cot_sem.at[per + i])
-            )
+            copies.append(pltpu.make_async_copy(cots[0].at[spot, own], target, cot_sem.at[i]))
+        for i, (source, spot) in enumerate(tiles_of(cots, at_ref, base + per, tile)):
+            if i > 0:
+                target = cb.at[pl.ds(i * tile, tile)]
+                copies.append(
+                    pltpu.make_async_copy(source.at[spot, own], target, cot_sem.at[per + i])
+                )
         for copy in copies:
             copy.start()
         for copy in copies:
@@ -597,7 +652,7 @@
         gain_ref[...] = jnp.broadcast_to(gain_sum[...], (size, HD)).T[:1, :]
 
 
-def mlp_grad(places, chunk, pieces, own, cot, hb, wg, wu, size):
+def mlp_grad(places, chunk, pieces, own, cots, hb, wg, wu, size):
     tile, width = pieces[0].shape
     rows, units = hb.shape
     block = min(256, units)
@@ -606,8 +661,8 @@
     grid_spec = pltpu.PrefetchScalarGridSpec(
         num_scalar_prefetch=1,
         grid=(units // block,),
-        in_specs=[HBM_WHOLE] * len(pieces) + [ospec] * 3
-        + [pl.BlockSpec((rows, block), lambda i, at: (0, i)), HBM_WHOLE, wspec, wspec],
+        in_specs=[HBM_WHOLE] * (len(pieces) + len(cots)) + [ospec] * 3
+        + [pl.BlockSpec((rows, block), lambda i, at: (0, i)), wspec, wspec],
         out_specs=[pl.BlockSpec((size, block), lambda i, at: (0, i))] * 2
         + [pl.BlockSpec((block, size), lambda i, at: (i, 0)),
            pl.BlockSpec((1, size), lambda i, at: (0, 0))],
@@ -617,7 +672,7 @@
            pltpu.SemaphoreType.DMA((tile // chunk + rows // tile,))],
     )
     return pl.pallas_call(
-        functools.partial(mlp_grad_kernel, len(pieces), chunk),
+        functools.partial(mlp_grad_kernel, len(pieces), chunk, len(cots)),
         grid_spec=grid_spec,
         out_shape=[jax.ShapeDtypeStruct((size, units), F32)] * 2
         + [jax.ShapeDtypeStruct((units, size), F32), jax.ShapeDtypeStruct((1, size), F32)],
@@ -628,8 +683,8 @@
             transcendentals=0,
         ),
     )(
-        places, *pieces, *[in_hbm(rows) for rows in own], in_hbm(hb), in_hbm(cot),
-        in_hbm(wg), in_hbm(wu),
+        places, *pieces, *[in_hbm(cot) for cot in cots], *[in_hbm(rows) for rows in own],
+        in_hbm(hb), in_hbm(wg), in_hbm(wu),
     )
 
 
@@ -676,11 +731,9 @@
         return lists
 
     rings = ring_of(mine)[1:]
-    cot_all = lax.all_gather(
-        cot_mine, ("dp", "ctx", "tensor"), axis=0, tiled=True
-    )
-
-    ring_at = (ctx - jnp.arange(n_ctx, dtype=jnp.int32) + n_ctx) % n_ctx
+    cot_own = lax.all_gather(cot_mine, ("ctx", "tensor"), axis=0, tiled=True)
+
+    ring_at = ctx ^ jnp.arange(n_ctx, dtype=jnp.int32)
     seq_places = jnp.concatenate([
         ring_at[k : k + 1] * n_t + (place ^ slot) for k in range(n_ctx) for slot in slots
     ])
@@ -689,26 +742,28 @@
     owners = jnp.stack([((dp + step) % n_dp) * n_ctx + ctx for step in range(n_dp)])
     starts = owners * out_cols
     owner = owners[0]
-    tiles = n_dp * n_ctx
-    turns = (owner + jnp.arange(tiles, dtype=jnp.int32)) % tiles
+    half = place & 1
     places = [owner[None]]
     for flip in (0, 1):
         for step in range(n_dp):
             for index in range(n_t // 2):
-                group = ((dp - step + n_dp) % n_dp) * n_ctx + ring_at
-                group = (group - owner + tiles) % tiles
-                inside = jnp.where(
-                    group == 0, index + flip * (n_t // 2), place ^ slots[index] ^ flip
-                )
+                if step == 0:
+                    group = jnp.arange(n_ctx, dtype=jnp.int32)
+                else:
+                    other_half = ring_at // (n_ctx // 2) != half
+                    group = step * n_ctx + other_half * (n_ctx // 2) + ring_at % (n_ctx // 2)
+                inside = place ^ slots[index] ^ flip
+                if step == 0:
+                    inside = jnp.where(group == 0, index + flip * (n_t // 2), inside)
                 places.append(group * n_t + inside)
-    places = jnp.concatenate(places + [turns, owner * n_t + slot_places])
+    places = jnp.concatenate(places + [ctx * n_t + slot_places, ring_at])
     frequency = np.float32(10000.0) ** (
         -np.arange(HD // 2, dtype=np.float32) * np.float32(2.0) / np.float32(HD)
     )
     angles = np.arange(length, dtype=np.float32)[:, None] * frequency[None, :]
     cos = jnp.asarray(np.concatenate([np.cos(angles), np.cos(angles)], axis=1))
     sin = jnp.asarray(np.concatenate([-np.sin(angles), np.sin(angles)], axis=1))
-    rings = after(rings, seq_places, starts, places, turns)
+    rings = [after(ring, seq_places, starts, places) for ring in rings]
     hidden_back = lax.dot_general(
         after(cot, rings), down_weight, (((1,), (1,)), ((), ())), preferred_element_type=F32
     ).astype(BF)
@@ -734,12 +789,16 @@
     middle = inputs_mine + branch
     scaled_second, root_second = norm_parts(middle)
     normed_chunk = (scaled_second * gain_second).astype(BF)
+    cot_own = after(cot_own, normed_chunk)
+    size = length // 2
+    cot_half = lax.dynamic_slice_in_dim(cot_own, half * size, size, 0)
+    cot_far = [turn(cot_half, "dp", step) for step in range(1, n_dp)]
     gate, up = fetch(after(gate_weight, normed_chunk), up_weight)
     normed_second = gather_tensor(normed_chunk, (gate, up))
     chunk_rings = ring_of(normed_chunk)
     hidden, gate_back, up_back, second_part = mlp(normed_second, hidden_back, gate, up)
     second_part, chunk_rings = lax.optimization_barrier((second_part, chunk_rings))
-    x_near = [jnp.concatenate(chunk_rings, axis=0)]
+    x_near = [join(chunk_rings)]
     x_far = over_dp(x_near)
     x_near_more = over_tensor(x_near, bits[:-1])[1:]
     second_back = scatter_tensor(second_part)
@@ -747,16 +806,15 @@
         second_back, scaled_second, root_second, gain_second
     )
     branch_back = middle_back.astype(BF)
-    bb_rings = ring_of(branch_back)[1:]
-    bb_own = over_tensor([branch_back], bits[:-1])
-    hidden_back_all = hidden_back_of(turns, after(cot_all, branch_back), down_weight)
-    bb_rings, bb_own, x_far, x_near_more = after(
-        (bb_rings, bb_own, x_far, x_near_more), hidden_back_all
-    )
-    mlp_part = jnp.dot(
-        after(hidden, bb_rings), down_weight, preferred_element_type=F32
-    ).astype(BF)
-    bb_pieces = [over_tensor(bb_own, bits[-1:])] + spread(bb_rings, mlp_part)
+    bb_rings = ring_of(branch_back)
+    cots = [cot_own] + sum([[far, swap(far, "tensor", 1)] for far in cot_far], [])
+    cots = after(cots, branch_back)
+    hidden_back_all, mlp_part = hidden_back_of(ring_at, cots, down_weight, hidden, 0)
+    bb_rings, x_far, x_near_more = after((bb_rings, x_far, x_near_more), hidden_back_all)
+    hidden_back_all, mlp_part = hidden_back_of(
+        ring_at, after(cots, bb_rings), down_weight, hidden, 1, (mlp_part, hidden_back_all)
+    )
+    bb_pieces = spread(bb_rings, mlp_part)
     x_far_more = over_tensor(x_far, bits[:-1])[len(x_far) :]
 
     mine_grads, theirs_grads, kept_half, given_half = attend_back(
@@ -769,7 +827,7 @@
     x_pieces = over_tensor(x_near + x_near_more + x_far + x_far_more, bits[-1:])
 
     gate_grad, up_grad, down_grad, mlp_gain_sum = mlp_grad(
-        after(places, kept_half), chunk, x_pieces, (hidden, gate_back, up_back), cot_all,
+        after(places, kept_half), chunk, x_pieces, (hidden, gate_back, up_back), cots,
         hidden_back_all, gate_weight, up_weight, out_cols,
     )
     mlp_gain_sum = mlp_gain_sum[0]

time: 205 us -> 199 us (0.971)
  Pallas kernels: 85.5 us -> 93 us
  matrix products: 13.1 us -> 7.67 us
  starting transfers between devices: 46.6 us -> 41.7 us
    ppermute x11 -> x3, starting transfers between devices: 24.3 us -> 4.64 us  [turn(): lax.ppermute(values, axis, [(i, (i + shift) % count) for i in range(count)])]
    ppermute x39 -> x49, starting transfers between devices: 22.3 us -> 37.1 us  [swap(): return lax.ppermute(values, axis, [(i, i ^ distance) for i in range(count)])]
    pallas_call x2 -> x4, Pallas kernels: 42.6 us -> 49.5 us  [the longest x1 28.1 us: mlp_grad(): pl.pallas_call(functools.partial(mlp_grad_kernel, len(pieces), chunk, len...]
    dot_general x1 -> x0, matrix products: 5.47 us -> none  [per_device(): jnp.dot(after(hidden, bb_rings), down_weight, preferred_element_type=F32)]
    ppermute x11 -> x3, waiting for transfers between devices: 7.11 us -> 1.89 us  [turn(): lax.ppermute(values, axis, [(i, (i + shift) % count) for i in range(count)])]
    ppermute x39 -> x49, waiting for transfers between devices: 14.5 us -> 19.5 us  [swap(): return lax.ppermute(values, axis, [(i, i ^ distance) for i in range(count)])]
    unnamed x94 -> x97, local copies, waits for them, and re-layouts: 5.2 us -> 3.3 us
  transfers between devices with their start and end apart: 51 -> 53, of which waited for: 16 -> 13; matrix products, arithmetic and copies ran while one was open for 14% -> 11% of each run, Pallas kernels for 41% -> 45%
where the time goes in v4:
time: 199 us
  Pallas kernels  93 us (47%)
  starting transfers between devices  41.7 us (21%)
  waiting for transfers between devices  21.4 us (11%)
  between operations  17.6 us (9%)
  local copies, waits for them, and re-layouts  10.7 us (5%)
  matrix products  7.67 us (4%)
  other arithmetic  6.9 us (3%)
    ppermute x49, starting transfers between devices, swap(): return lax.ppermute(values, axis, [(i, i ^ distance) for i in range(count)])  37.1 us
    pallas_call x1, Pallas kernels, mlp_grad(): pl.pallas_call(functools.partial(mlp_grad_kernel, len(pieces), chunk, len...  28.1 us
    pallas_call x2, Pallas kernels, hidden_back_of(): pl.pallas_call(functools.partial(hidden_back_kernel, tile, len(before) >...  20.7 us
    ppermute x49, waiting for transfers between devices, swap(): return lax.ppermute(values, axis, [(i, i ^ distance) for i in range(count)])  19.5 us
    pallas_call x1, Pallas kernels, attend_back(): pl.pallas_call(functools.partial(attend_back_kernel, chunk, slots, scale,...  16.4 us
    pallas_call x1, Pallas kernels, attend(): pl.pallas_call(functools.partial(attend_kernel, chunk, slots, scale, shif...  10.4 us
    pallas_call x1, Pallas kernels, mlp(): pl.pallas_call(functools.partial(mlp_kernel, min(512, units)), in_specs=[...  8.03 us
    dot_general x1, matrix products, per_device(): lax.dot_general(after(cot, rings), down_weight, (((1,), (1,)), ((), ())),...  6.27 us
  transfers between devices with their start and end apart: 53, of which 13 were waited for; matrix products, arithmetic and copies ran while one was open for 11% of the time, Pallas kernels for 45%

profile of v4, /device:TPU:0, one launch (start us, length us, event | category | flops | bytes accessed | tf_op | source)
XLA Modules:
  0.0 199.0 jit_solution(15935413849745217821)
XLA Ops:
  8.0 2.8 %shard_map.229 = (bf16[128,2048]{1,0:T(8,128)(2,1)S(1)}, bf16[32,2048]{1,0:T(8,128)(2,1)S(1)}, bf16[128,2048]{1,0:T(8,128)(2,1)S(1)}, bf16[32,2048]{1,0:T(8,128)...) custom-call(s32[4]{0:T(128)S(1)} %get-tuple-element.191.at_ref, ...), custom_call_target="tpu_custom_call" | custom-call | flops 2097152 | bytes 2097152 | tf_op jit(solution)/shard_map/pallas_call | solution.py:195
  10.8 3.1 %collective-permute-start = (bf16[32,2048]{1,0:T(8,128)(2,1)S(1)}, bf16[32,2048]{1,0:T(8,128)(2,1)S(1)}, u32[]{:S(2)}, u32[]{:S(2)}) collective-permute-start(bf16[32,2048]{1,0:T(8,128)(2,1)S(1)} %get-tuple-element.87), channel_id=1, source_target_pairs={{0,4},{4,0},{8,12},{12,8},{1,5},{5,1},{9,13},{13,9},{2,6},{6,2},{1... | collective-permute-start | bytes 393224 | tf_op jit(solution)/shard_map/ppermute | solution.py:21
  13.9 2.6 %collective-permute-start.2 = (bf16[32,2048]{1,0:T(8,128)(2,1)S(1)}, bf16[32,2048]{1,0:T(8,128)(2,1)S(1)}, u32[]{:S(2)}, u32[]{:S(2)}) collective-permute-start(bf16[32,2048]{1,0:T(8,128)(2,1)S(1)} %get-tuple-element.87), channel_id=1, source_target_pairs={{0,8},{4,12},{8,0},{12,4},{1,9},{5,13},{9,1},{13,5},{2,10},{6,14},... | collective-permute-start | bytes 393224 | tf_op jit(solution)/shard_map/ppermute | solution.py:21
  21.6 5.2 %collective-permute-done.2.refs_8_ = bf16[32,2048]{1,0:T(8,128)(2,1)S(1)} collective-permute-done((bf16[32,2048]{1,0:T(8,128)(2,1)S(1)}, bf16[32,2048]{1,0:T(8,128)(2,1)S(1)}, u32[]{:S(2)}, u32[]{:S(2)}) %collective-permute-start.2) | collective-permute-done | bytes 131104 | tf_op jit(solution)/shard_map/ppermute | solution.py:21
  26.8 1.6 collective-permute-start.1
  28.9 1.5 collective-permute-start.5
  30.4 6.3 %convolution_convert_fusion.hb_ref = bf16[128,2048]{1,0:T(8,128)(2,1)S(1)} fusion(bf16[128,2048]{1,0:T(8,128)(2,1)S(1)} %get-tuple-element.92, bf16[2048,2048]{1,0:T(8,128)(2,1)} %refs_3_.3), kind=kOutput, calls=%fused_computation | convolution fusion | flops 1074003968 | bytes 9437184 | tf_op jit(solution)/shard_map/dot_general | solution.py:767
  40.2 10.4 %shard_map.230 = (bf16[512,512]{1,0:T(8,128)(2,1)}, bf16[512,512]{1,0:T(8,128)(2,1)}, bf16[512,512]{1,0:T(8,128)(2,1)}, bf16[128,512]{1,0:T(8,128)(2,1)}, f32[4,...) custom-call(s32[16]{0:T(128)} %concatenate.19.at_ref, bf16[32,2048]{1,0:T(8,128)(2,1)} %get-tuple-element.201.refs_0_, ...), custom_call_target="tpu_custom_call" | custom-call | flops 3221225472 | bytes 6291456 | tf_op jit(solution)/shard_map/pallas_call | solution.py:271
  50.7 1.4 convolution_convert_fusion.1
  52.4 1.3 collective-permute-done.12
  55.9 3.5 %collective-permute-done.13 = bf16[32,2048]{1,0:T(8,128)(2,1)S(1)} collective-permute-done((bf16[32,2048]{1,0:T(8,128)(2,1)S(1)}, bf16[32,2048]{1,0:T(8,128)(2,1)S(1)}, u32[]{:S(2)}, u32[]{:S(2)}) %collective-permute-start.13) | collective-permute-done | bytes 131104 | tf_op jit(solution)/shard_map/ppermute | solution.py:21
  60.9 1.3 constant_dynamic-slice_fusion
  62.2 1.6 collective-permute-start.26
  63.8 5.8 %shard_map.231 = (bf16[2048,2048]{1,0:T(8,128)(2,1)S(1)}, bf16[2048,2048]{1,0:T(8,128)(2,1)S(1)}) custom-call(bf16[2048,2048]{1,0:T(8,128)(2,1)} %refs_15_.1, bf16[2048,2048]{1,0:T(8,128)(2,1)} %refs_16_.5), custom_call_target="tpu_custom_call" | custom-call | tf_op jit(solution)/shard_map/pallas_call | solution.py:144
  69.7 2.8 %collective-permute-start.16 = (bf16[32,2048]{1,0:T(8,128)(2,1)S(1)}, bf16[32,2048]{1,0:T(8,128)(2,1)S(1)}, u32[]{:S(2)}, u32[]{:S(2)}) collective-permute-start(bf16[32,2048]{1,0:T(8,128)(2,1)S(1)} %multiply_convert_fusion.refs_0_), channel_id=1, source_target_pairs={{0,4},{4,0},{8,12},{12,8},{1,5},{5,1},{9,13},{13,9},{2,6},{6,2},{1... | collective-permute-start | bytes 393224 | tf_op jit(solution)/shard_map/ppermute | solution.py:21
  73.5 1.5 collective-permute-start.18
  75.0 8.0 %shard_map.232 = (bf16[128,2048]{1,0:T(8,128)(2,1)S(1)}, bf16[128,2048]{1,0:T(8,128)(2,1)S(1)}, bf16[128,2048]{1,0:T(8,128)(2,1)S(1)}, bf16[128,2048]{1,0:T(8,128)(2,1)S(1)}) custom-call(bf16[128,2048]{1,0:T(8,128)(2,1)S(1)} %pad_maximum_fusion.x_ref, bf16[128,2048]{1,0:T(8,128)(2,1)S(1)} %convolution_convert_fusion.hb_ref, ...), custom_call_target="tpu_custom_call" | custom-call | tf_op jit(solution)/shard_map/pallas_call | solution.py:474
  83.1 2.3 %collective-permute-done.17.refs_2_ = bf16[32,2048]{1,0:T(8,128)(2,1)S(1)} collective-permute-done((bf16[32,2048]{1,0:T(8,128)(2,1)S(1)}, bf16[32,2048]{1,0:T(8,128)(2,1)S(1)}, u32[]{:S(2)}, u32[]{:S(2)}) %collective-permute-start.17) | collective-permute-done | bytes 131104 | tf_op jit(solution)/shard_map/ppermute | solution.py:21
  85.5 1.9 collective-permute-done.26.refs_1_.refs_9_
  88.8 1.5 collective-permute-start.24
  90.3 1.5 collective-permute-start.25
  91.8 2.1 %collective-permute-done.20 = bf16[32,2048]{1,0:T(8,128)(2,1)S(1)} collective-permute-done((bf16[32,2048]{1,0:T(8,128)(2,1)S(1)}, bf16[32,2048]{1,0:T(8,128)(2,1)S(1)}, u32[]{:S(2)}, u32[]{:S(2)}) %collective-permute-start.20) | collective-permute-done | bytes 131104 | tf_op jit(solution)/shard_map/ppermute | solution.py:21
  95.2 1.8 collective-permute-start.21
  97.8 1.8 collective-permute-start.23
  99.6 10.2 %shard_map.234 = (bf16[1024,2048]{1,0:T(8,128)(2,1)}, f32[128,2048]{1,0:T(8,128)}) custom-call(s32[4]{0:T(128)} %copy-done.25, bf16[512,2048]{1,0:T(8,128)(2,1)} %all-gather.2.cloned.1.call-done.refs_0_.refs_8_, bf16[256,2048]{1,0:T(8,128)(2,1)} %copy-done.6, bf16[256,2048]{1,0:T(8,128)(2,1)} %copy-done.7, bf16[2048,2048]{1,0:T(8,128)(2,1)} %refs_3_.3, ...), custom_call_target="tpu_custom_call" | custom-call | flops 4294967296 | bytes 12582912 | tf_op jit(solution)/shard_map/pallas_call | solution.py:543
  114.0 10.5 %shard_map.235 = (bf16[1024,2048]{1,0:T(8,128)(2,1)}, bf16[128,2048]{1,0:T(8,128)(2,1)}) custom-call(s32[4]{0:T(128)} %copy-done.25, bf16[512,2048]{1,0:T(8,128)(2,1)} %all-gather.2.cloned.1.call-done.refs_0_.refs_8_, bf16[256,2048]{1,0:T(8,128)(2,1)} %copy-done.6, bf16[256,2048]{1,0:T(8,128)(2,1)} %copy-done.7, ...), custom_call_target="tpu_custom_call", output_to_operand_aliasing={{0}: (7, {})} | custom-call | flops 4294967296 | bytes 12582912 | tf_op jit(solution)/shard_map/pallas_call | solution.py:543
  128.6 16.4 %shard_map.236 = (f32[4,256,512]{2,1,0:T(8,128)}, bf16[1,4,256,512]{3,2,1,0:T(8,128)(2,1)}, bf16[64,4096]{1,0:T(8,128)(2,1)}, bf16[64,4096]{1,0:T(8,128)(2,1)}) custom-call(s32[16]{0:T(128)} %concatenate.19.at_ref, s32[2]{0:T(128)} %add_multiply_fusion.starts_ref, bf16[32,2048]{1,0:T(8,128)(2,1)} %copy-done.8, bf16[32,2048]{1,0:T(8,128)(2,1)} %copy-done.13, ...), custom_call_target="tpu_custom_call" | custom-call | flops 2952790016 | bytes 9437184 | tf_op jit(solution)/shard_map/pallas_call | solution.py:413
  146.2 1.5 collective-permute-start.49
  151.2 28.1 %shard_map.237 = (f32[256,2048]{1,0:T(8,128)}, f32[256,2048]{1,0:T(8,128)}, f32[2048,256]{1,0:T(8,128)}, f32[1,256]{1,0:T(1,128)}) custom-call(s32[41]{0:T(128)} %concatenate.20.at_ref, bf16[128,2048]{1,0:T(8,128)(2,1)} %copy-done, bf16[128,2048]{1,0:T(8,128)(2,1)} %copy-done.31, bf16[128,2048]{1,0:T(8,128)(2,1)} %copy-done.30, ...), custom_call_target="tpu_custom_call" | custom-call | flops 20401094656 | bytes 25165824 | tf_op jit(solution)/shard_map/pallas_call | solution.py:674
  181.3 2.4 %add_reduce_fusion = (f32[256]{0:T(256)S(1)}, f32[256,512]{1,0:T(8,128)}, f32[256,512]{1,0:T(8,128)}, f32[256,512]{1,0:T(8,128)}) fusion(bf16[2048,512]{1,0:T(8,128)(2,1)} %refs_27_.1, s32[]{:T(128)S(6)} %select_n.82, bf16[2048,512]{1,0:T(8,128)(2,1)} %refs_26_.1, bf16[2048,512]{1,0:T(8,128)(2,1)} %refs_25_.1, f32[4,256,512]{2,1,0:T(8,128)S(1)} %convert_add_fusion), kind=kLoop, calls=%fused_computation.14 | loop fusion | flops 1179392 | bytes 3933188 | tf_op jit(solution)/shard_map/reduce_sum | solution.py:851
  185.9 2.5 %collective-permute-done.47 = bf16[32,4096]{1,0:T(8,128)(2,1)S(1)} collective-permute-done((bf16[32,4096]{1,0:T(8,128)(2,1)S(1)}, bf16[32,4096]{1,0:T(8,128)(2,1)S(1)}, u32[]{:S(2)}, u32[]{:S(2)}) %collective-permute-start.47) | collective-permute-done | bytes 262176 | tf_op jit(solution)/shard_map/ppermute | solution.py:21
  189.1 1.3 collective-permute-done.51
  (238 shorter events, 35.0 us)
Async XLA Ops:
  7.2 53.7 %all-gather.2.cloned.1.call-start = ((), (), s32[]{:S(2)}) async-start(), calls=%async_computation | async-start | bytes 2228224 | tf_op jit(solution)/shard_map/all_gather | solution.py:734
  10.8 10.8 %collective-permute-start = (bf16[32,2048]{1,0:T(8,128)(2,1)S(1)}, bf16[32,2048]{1,0:T(8,128)(2,1)S(1)}, u32[]{:S(2)}, u32[]{:S(2)}) collective-permute-start(bf16[32,2048]{1,0:T(8,128)(2,1)S(1)} %get-tuple-element.87), channel_id=1, source_target_pairs={{0,4},{4,0},{8,12},{12,8},{1,5},{5,1},{9,13},{13,9},{2,6},{6,2},{1... | collective-permute-start | bytes 393224 | tf_op jit(solution)/shard_map/ppermute | solution.py:21
  13.9 12.9 %collective-permute-start.2 = (bf16[32,2048]{1,0:T(8,128)(2,1)S(1)}, bf16[32,2048]{1,0:T(8,128)(2,1)S(1)}, u32[]{:S(2)}, u32[]{:S(2)}) collective-permute-start(bf16[32,2048]{1,0:T(8,128)(2,1)S(1)} %get-tuple-element.87), channel_id=1, source_target_pairs={{0,8},{4,12},{8,0},{12,4},{1,9},{5,13},{9,1},{13,5},{2,10},{6,14},... | collective-permute-start | bytes 393224 | tf_op jit(solution)/shard_map/ppermute | solution.py:21
  16.5 10.3 %collective-permute-start.4 = (bf16[32,2048]{1,0:T(8,128)(2,1)S(1)}, bf16[32,2048]{1,0:T(8,128)(2,1)S(1)}, u32[]{:S(2)}, u32[]{:S(2)}) collective-permute-start(bf16[32,2048]{1,0:T(8,128)(2,1)S(1)} %get-tuple-element.87), channel_id=1, source_target_pairs={{0,12},{4,8},{8,4},{12,0},{1,13},{5,9},{9,5},{13,1},{2,14},{6,10},... | collective-permute-start | bytes 393224 | tf_op jit(solution)/shard_map/ppermute | solution.py:21
  26.8 9.9 %collective-permute-start.1 = (bf16[32,2048]{1,0:T(8,128)(2,1)S(1)}, bf16[32,2048]{1,0:T(8,128)(2,1)S(1)}, u32[]{:S(2)}, u32[]{:S(2)}) collective-permute-start(bf16[32,2048]{1,0:T(8,128)(2,1)S(1)} %collective-permute-done.refs_4_), channel_id=1, source_target_pairs={{0,2},{1,3},{2,0},{3,1},{4,6},{5,7},{6,4},{7,5},{8,10},{9,11},{10,... | collective-permute-start | bytes 393224 | tf_op jit(solution)/shard_map/ppermute | solution.py:21
  28.4 8.3 %collective-permute-start.3 = (bf16[32,2048]{1,0:T(8,128)(2,1)S(1)}, bf16[32,2048]{1,0:T(8,128)(2,1)S(1)}, u32[]{:S(2)}, u32[]{:S(2)}) collective-permute-start(bf16[32,2048]{1,0:T(8,128)(2,1)S(1)} %collective-permute-done.2.refs_8_), channel_id=1, source_target_pairs={{0,2},{1,3},{2,0},{3,1},{4,6},{5,7},{6,4},{7,5},{8,10},{9,11},{10,... | collective-permute-start | bytes 393224 | tf_op jit(solution)/shard_map/ppermute | solution.py:21
  28.9 7.8 %collective-permute-start.5 = (bf16[32,2048]{1,0:T(8,128)(2,1)S(1)}, bf16[32,2048]{1,0:T(8,128)(2,1)S(1)}, u32[]{:S(2)}, u32[]{:S(2)}) collective-permute-start(bf16[32,2048]{1,0:T(8,128)(2,1)S(1)} %collective-permute-done.4.refs_12_), channel_id=1, source_target_pairs={{0,2},{1,3},{2,0},{3,1},{4,6},{5,7},{6,4},{7,5},{8,10},{9,11},{10,... | collective-permute-start | bytes 393224 | tf_op jit(solution)/shard_map/ppermute | solution.py:21
  53.8 5.6 %collective-permute-start.13 = (bf16[32,2048]{1,0:T(8,128)(2,1)S(1)}, bf16[32,2048]{1,0:T(8,128)(2,1)S(1)}, u32[]{:S(2)}, u32[]{:S(2)}) collective-permute-start(bf16[32,2048]{1,0:T(8,128)(2,1)S(1)} %slice.205), channel_id=1, source_target_pairs={{0,2},{1,3},{2,0},{3,1},{4,6},{5,7},{6,4},{7,5},{8,10},{9,11},{10,... | collective-permute-start | bytes 393224 | tf_op jit(solution)/shard_map/ppermute | solution.py:21
  59.7 10.0 %collective-permute-start.14 = (bf16[32,2048]{1,0:T(8,128)(2,1)S(1)}, bf16[32,2048]{1,0:T(8,128)(2,1)S(1)}, u32[]{:S(2)}, u32[]{:S(2)}) collective-permute-start(bf16[32,2048]{1,0:T(8,128)(2,1)S(1)} %multiply_convert_fusion.refs_0_), channel_id=1, source_target_pairs={{0,2},{1,3},{2,0},{3,1},{4,6},{5,7},{6,4},{7,5},{8,10},{9,11},{10,... | collective-permute-start | bytes 393224 | tf_op jit(solution)/shard_map/ppermute | solution.py:21
  62.2 25.2 %collective-permute-start.26 = (bf16[256,2048]{1,0:T(8,128)(2,1)S(1)}, bf16[256,2048]{1,0:T(8,128)(2,1)S(1)}, u32[]{:S(2)}, u32[]{:S(2)}) collective-permute-start(bf16[256,2048]{1,0:T(8,128)(2,1)S(1)} %constant_dynamic-slice_fusion), channel_id=1, source_target_pairs={{0,16},{16,0},{1,17},{17,1},{2,18},{18,2},{3,19},{19,3},{4,20},{20... | collective-permute-start | bytes 3145736 | tf_op jit(solution)/shard_map/ppermute | solution.py:26
  69.7 5.3 %collective-permute-start.15 = (bf16[64,2048]{1,0:T(8,128)(2,1)S(1)}, bf16[64,2048]{1,0:T(8,128)(2,1)S(1)}, u32[]{:S(2)}, u32[]{:S(2)}) collective-permute-start(bf16[64,2048]{1,0:T(8,128)(2,1)S(1)} %pad_maximum_fusion.2), channel_id=1, source_target_pairs={{0,1},{1,0},{2,3},{3,2},{4,5},{5,4},{6,7},{7,6},{8,9},{9,8},{10,11... | collective-permute-start | bytes 786440 | tf_op jit(solution)/shard_map/ppermute | solution.py:21
  69.7 13.3 %collective-permute-start.16 = (bf16[32,2048]{1,0:T(8,128)(2,1)S(1)}, bf16[32,2048]{1,0:T(8,128)(2,1)S(1)}, u32[]{:S(2)}, u32[]{:S(2)}) collective-permute-start(bf16[32,2048]{1,0:T(8,128)(2,1)S(1)} %multiply_convert_fusion.refs_0_), channel_id=1, source_target_pairs={{0,4},{4,0},{8,12},{12,8},{1,5},{5,1},{9,13},{13,9},{2,6},{6,2},{1... | collective-permute-start | bytes 393224 | tf_op jit(solution)/shard_map/ppermute | solution.py:21
  72.5 12.9 %collective-permute-start.17 = (bf16[32,2048]{1,0:T(8,128)(2,1)S(1)}, bf16[32,2048]{1,0:T(8,128)(2,1)S(1)}, u32[]{:S(2)}, u32[]{:S(2)}) collective-permute-start(bf16[32,2048]{1,0:T(8,128)(2,1)S(1)} %multiply_convert_fusion.refs_0_), channel_id=1, source_target_pairs={{0,8},{4,12},{8,0},{12,4},{1,9},{5,13},{9,1},{13,5},{2,10},{6,14},... | collective-permute-start | bytes 393224 | tf_op jit(solution)/shard_map/ppermute | solution.py:21
  73.5 12.0 %collective-permute-start.18 = (bf16[32,2048]{1,0:T(8,128)(2,1)S(1)}, bf16[32,2048]{1,0:T(8,128)(2,1)S(1)}, u32[]{:S(2)}, u32[]{:S(2)}) collective-permute-start(bf16[32,2048]{1,0:T(8,128)(2,1)S(1)} %multiply_convert_fusion.refs_0_), channel_id=1, source_target_pairs={{0,12},{4,8},{8,4},{12,0},{1,13},{5,9},{9,5},{13,1},{2,14},{6,10},... | collective-permute-start | bytes 393224 | tf_op jit(solution)/shard_map/ppermute | solution.py:21
  87.4 10.4 %collective-permute-start.27 = (bf16[256,2048]{1,0:T(8,128)(2,1)S(1)}, bf16[256,2048]{1,0:T(8,128)(2,1)S(1)}, u32[]{:S(2)}, u32[]{:S(2)}) collective-permute-start(bf16[256,2048]{1,0:T(8,128)(2,1)S(1)} %collective-permute-done.26.refs_1_.refs_9_), channel_id=1, source_target_pairs={{0,1},{1,0},{2,3},{3,2},{4,5},{5,4},{6,7},{7,6},{8,9},{9,8},{10,11... | collective-permute-start | bytes 3145736 | tf_op jit(solution)/shard_map/ppermute | solution.py:21
  87.5 6.4 %collective-permute-start.20 = (bf16[32,2048]{1,0:T(8,128)(2,1)S(1)}, bf16[32,2048]{1,0:T(8,128)(2,1)S(1)}, u32[]{:S(2)}, u32[]{:S(2)}) collective-permute-start(bf16[32,2048]{1,0:T(8,128)(2,1)S(1)} %slice.204), channel_id=1, source_target_pairs={{0,2},{1,3},{2,0},{3,1},{4,6},{5,7},{6,4},{7,5},{8,10},{9,11},{10,... | collective-permute-start | bytes 393224 | tf_op jit(solution)/shard_map/ppermute | solution.py:21
  88.8 21.0 %collective-permute-start.24 = (bf16[128,2048]{1,0:T(8,128)(2,1)S(1)}, bf16[128,2048]{1,0:T(8,128)(2,1)S(1)}, u32[]{:S(2)}, u32[]{:S(2)}) collective-permute-start(bf16[128,2048]{1,0:T(8,128)(2,1)S(1)} %shard_map.233.refs_0_), channel_id=1, source_target_pairs={{0,16},{16,0},{1,17},{17,1},{2,18},{18,2},{3,19},{19,3},{4,20},{20... | collective-permute-start | bytes 1572872 | tf_op jit(solution)/shard_map/ppermute | solution.py:26
  90.3 19.5 %collective-permute-start.25 = (bf16[128,2048]{1,0:T(8,128)(2,1)S(1)}, bf16[128,2048]{1,0:T(8,128)(2,1)S(1)}, u32[]{:S(2)}, u32[]{:S(2)}) collective-permute-start(bf16[128,2048]{1,0:T(8,128)(2,1)S(1)} %shard_map.233.refs_0_), channel_id=1, source_target_pairs={{0,2},{1,3},{2,0},{3,1},{4,6},{5,7},{6,4},{7,5},{8,10},{9,11},{10,... | collective-permute-start | bytes 1572872 | tf_op jit(solution)/shard_map/ppermute | solution.py:21
  95.2 14.7 %collective-permute-start.21 = (bf16[32,2048]{1,0:T(8,128)(2,1)S(1)}, bf16[32,2048]{1,0:T(8,128)(2,1)S(1)}, u32[]{:S(2)}, u32[]{:S(2)}) collective-permute-start(bf16[32,2048]{1,0:T(8,128)(2,1)S(1)} %get-tuple-element.128.refs_0_), channel_id=1, source_target_pairs={{0,4},{4,0},{8,12},{12,8},{1,5},{5,1},{9,13},{13,9},{2,6},{6,2},{1... | collective-permute-start | bytes 393224 | tf_op jit(solution)/shard_map/ppermute | solution.py:21
  96.9 12.9 %collective-permute-start.22 = (bf16[32,2048]{1,0:T(8,128)(2,1)S(1)}, bf16[32,2048]{1,0:T(8,128)(2,1)S(1)}, u32[]{:S(2)}, u32[]{:S(2)}) collective-permute-start(bf16[32,2048]{1,0:T(8,128)(2,1)S(1)} %get-tuple-element.128.refs_0_), channel_id=1, source_target_pairs={{0,8},{4,12},{8,0},{12,4},{1,9},{5,13},{9,1},{13,5},{2,10},{6,14},... | collective-permute-start | bytes 393224 | tf_op jit(solution)/shard_map/ppermute | solution.py:21
  97.8 12.0 %collective-permute-start.23 = (bf16[32,2048]{1,0:T(8,128)(2,1)S(1)}, bf16[32,2048]{1,0:T(8,128)(2,1)S(1)}, u32[]{:S(2)}, u32[]{:S(2)}) collective-permute-start(bf16[32,2048]{1,0:T(8,128)(2,1)S(1)} %get-tuple-element.128.refs_0_), channel_id=1, source_target_pairs={{0,12},{4,8},{8,4},{12,0},{1,13},{5,9},{9,5},{13,1},{2,14},{6,10},... | collective-permute-start | bytes 393224 | tf_op jit(solution)/shard_map/ppermute | solution.py:21
  109.9 14.7 %collective-permute-start.28 = (bf16[32,2048]{1,0:T(8,128)(2,1)S(1)}, bf16[32,2048]{1,0:T(8,128)(2,1)S(1)}, u32[]{:S(2)}, u32[]{:S(2)}) collective-permute-start(bf16[32,2048]{1,0:T(8,128)(2,1)S(1)} %get-tuple-element.128.refs_0_), channel_id=1, source_target_pairs={{0,2},{1,3},{2,0},{3,1},{4,6},{5,7},{6,4},{7,5},{8,10},{9,11},{10,... | collective-permute-start | bytes 393224 | tf_op jit(solution)/shard_map/ppermute | solution.py:21
  110.9 13.7 %collective-permute-start.29 = (bf16[32,2048]{1,0:T(8,128)(2,1)S(1)}, bf16[32,2048]{1,0:T(8,128)(2,1)S(1)}, u32[]{:S(2)}, u32[]{:S(2)}) collective-permute-start(bf16[32,2048]{1,0:T(8,128)(2,1)S(1)} %collective-permute-done.21.refs_4_), channel_id=1, source_target_pairs={{0,2},{1,3},{2,0},{3,1},{4,6},{5,7},{6,4},{7,5},{8,10},{9,11},{10,... | collective-permute-start | bytes 393224 | tf_op jit(solution)/shard_map/ppermute | solution.py:21
  112.0 12.6 %collective-permute-start.30 = (bf16[32,2048]{1,0:T(8,128)(2,1)S(1)}, bf16[32,2048]{1,0:T(8,128)(2,1)S(1)}, u32[]{:S(2)}, u32[]{:S(2)}) collective-permute-start(bf16[32,2048]{1,0:T(8,128)(2,1)S(1)} %collective-permute-done.22.refs_8_), channel_id=1, source_target_pairs={{0,2},{1,3},{2,0},{3,1},{4,6},{5,7},{6,4},{7,5},{8,10},{9,11},{10,... | collective-permute-start | bytes 393224 | tf_op jit(solution)/shard_map/ppermute | solution.py:21
  112.9 11.7 %collective-permute-start.31 = (bf16[32,2048]{1,0:T(8,128)(2,1)S(1)}, bf16[32,2048]{1,0:T(8,128)(2,1)S(1)}, u32[]{:S(2)}, u32[]{:S(2)}) collective-permute-start(bf16[32,2048]{1,0:T(8,128)(2,1)S(1)} %collective-permute-done.23.refs_12_), channel_id=1, source_target_pairs={{0,2},{1,3},{2,0},{3,1},{4,6},{5,7},{6,4},{7,5},{8,10},{9,11},{10,... | collective-permute-start | bytes 393224 | tf_op jit(solution)/shard_map/ppermute | solution.py:21
  126.8 19.4 %collective-permute-start.42 = (bf16[128,2048]{1,0:T(8,128)(2,1)S(1)}, bf16[128,2048]{1,0:T(8,128)(2,1)}, u32[]{:S(2)}, u32[]{:S(2)}) collective-permute-start(bf16[128,2048]{1,0:T(8,128)(2,1)S(1)} %collective-permute-done.24.refs_2_), channel_id=1, source_target_pairs={{0,2},{1,3},{2,0},{3,1},{4,6},{5,7},{6,4},{7,5},{8,10},{9,11},{10,... | collective-permute-start | bytes 1572872 | tf_op jit(solution)/shard_map/ppermute | solution.py:21
  145.7 4.3 %collective-permute-start.45 = (bf16[128,2048]{1,0:T(8,128)(2,1)S(1)}, bf16[128,2048]{1,0:T(8,128)(2,1)S(1)}, u32[]{:S(2)}, u32[]{:S(2)}) collective-permute-start(bf16[128,2048]{1,0:T(8,128)(2,1)S(1)} %collective-permute-done.24.refs_2_), channel_id=1, source_target_pairs={{0,1},{1,0},{2,3},{3,2},{4,5},{5,4},{6,7},{7,6},{8,9},{9,8},{10,11... | collective-permute-start | bytes 1572872 | tf_op jit(solution)/shard_map/ppermute | solution.py:21
  145.9 4.1 %collective-permute-start.44 = (bf16[128,2048]{1,0:T(8,128)(2,1)S(1)}, bf16[128,2048]{1,0:T(8,128)(2,1)S(1)}, u32[]{:S(2)}, u32[]{:S(2)}) collective-permute-start(bf16[128,2048]{1,0:T(8,128)(2,1)S(1)} %collective-permute-done.25.refs_1_), channel_id=1, source_target_pairs={{0,1},{1,0},{2,3},{3,2},{4,5},{5,4},{6,7},{7,6},{8,9},{9,8},{10,11... | collective-permute-start | bytes 1572872 | tf_op jit(solution)/shard_map/ppermute | solution.py:21
  146.2 34.7 %collective-permute-start.49 = (bf16[4,256,512]{2,1,0:T(8,128)(2,1)}, bf16[4,256,512]{2,1,0:T(8,128)(2,1)S(1)}, u32[]{:S(2)}, u32[]{:S(2)}) collective-permute-start(bf16[4,256,512]{2,1,0:T(8,128)(2,1)} %bitcast.48), channel_id=1, source_target_pairs={{0,16},{16,0},{1,17},{17,1},{2,18},{18,2},{3,19},{19,3},{4,20},{20... | collective-permute-start | bytes 3145736 | tf_op jit(solution)/shard_map/ppermute | solution.py:26
  149.0 30.3 %collective-permute-start.41 = (bf16[32,4096]{1,0:T(8,128)(2,1)S(1)}, bf16[32,4096]{1,0:T(8,128)(2,1)S(1)}, u32[]{:S(2)}, u32[]{:S(2)}) collective-permute-start(bf16[32,4096]{1,0:T(8,128)(2,1)S(1)} %slice.203), channel_id=1, source_target_pairs={{0,2},{1,3},{2,0},{3,1},{4,6},{5,7},{6,4},{7,5},{8,10},{9,11},{10,... | collective-permute-start | bytes 786440 | tf_op jit(solution)/shard_map/ppermute | solution.py:21
  179.8 8.5 %collective-permute-start.47 = (bf16[32,4096]{1,0:T(8,128)(2,1)S(1)}, bf16[32,4096]{1,0:T(8,128)(2,1)S(1)}, u32[]{:S(2)}, u32[]{:S(2)}) collective-permute-start(bf16[32,4096]{1,0:T(8,128)(2,1)S(1)} %get-tuple-element.202), channel_id=1, source_target_pairs={{0,2},{1,3},{2,0},{3,1},{4,6},{5,7},{6,4},{7,5},{8,10},{9,11},{10,... | collective-permute-start | bytes 786440 | tf_op jit(solution)/shard_map/ppermute | solution.py:21
  183.7 4.7 %collective-permute-start.50 = (f32[2,256]{1,0:T(2,128)S(1)}, f32[2,256]{1,0:T(2,128)S(1)}, u32[]{:S(2)}, u32[]{:S(2)}) collective-permute-start(f32[2,256]{1,0:T(2,128)S(1)} %pad_maximum_fusion.4), channel_id=1, source_target_pairs={{0,2},{1,3},{2,0},{3,1},{4,6},{5,7},{6,4},{7,5},{8,10},{9,11},{10,... | collective-permute-start | bytes 6152 | tf_op jit(solution)/shard_map/ppermute | solution.py:21
  (69 other events, 435.8 us)
Sparse Core Ops, SparseCore 0:
  16.6 44.0 all-gather.1

commit v5 on v4

--- a/solution.py
+++ b/solution.py
@@ -170,7 +170,7 @@
     for pair in copies:
         for copy in pair:
             copy.start()
-    gain = gain_ref[...].astype(F32)
+    gain = gain_ref[...].astype(F32).reshape(1, -1)
     for i, (part, pair) in enumerate(zip(parts, copies, strict=True)):
         pair[0].wait()
         rows = rows_in[part, :].astype(F32)
@@ -501,17 +501,22 @@
     step, block = pl.program_id(0), wd_ref.shape[0]
     copies = []
     for i, (source, at) in enumerate(tiles_of(sources, at_ref, 0, tile)):
-        target = cot.at[pl.ds(i * tile, tile)]
-        copies.append(pltpu.make_async_copy(source.at[at], target, sem.at[i]))
+        if i > 0:
+            target = cot.at[pl.ds(i * tile, tile)]
+            copies.append(pltpu.make_async_copy(source.at[at], target, sem.at[i]))
+    rows = len(copies) * tile
+    parts = -(-rows // 512)
+    size = rows // parts
 
     def every_tile(waits):
         wd = wd_ref[...]
         own = dot(hidden_ref[...], wd)
-        for i in range(0, len(copies), 2):
-            if waits:
-                copies[i].wait()
-                copies[i + 1].wait()
-            at = pl.ds(i * tile, 2 * tile)
+        done = 0
+        for i in range(parts):
+            while waits and done * tile < (i + 1) * size:
+                copies[done].wait()
+                done += 1
+            at = pl.ds(tile + i * size, size)
             out_ref[at, :] = dot_nt(cot[at, :], wd).astype(BF)
         return own
 
@@ -717,7 +722,7 @@
 
     slot_places = jnp.stack([place ^ slot for slot in slots])
     normed_first, mine, cot, cot_mine, inputs_mine, scaled_mine, root_mine = arrange(
-        slot_places, activations[0], cotangent[0], attn_gain[None]
+        slot_places, activations[0], cotangent[0], attn_gain
     )
 
     bits = list(reversed(bits_of(n_t)))

time: 199 us -> 198 us (level)
    unnamed x97 -> x99, local copies, waits for them, and re-layouts: 3.3 us -> 4.18 us
where the time goes in v5:
time: 198 us
  Pallas kernels  91.7 us (46%)
  starting transfers between devices  41.7 us (21%)
  waiting for transfers between devices  21.2 us (11%)
  between operations  17.6 us (9%)
  local copies, waits for them, and re-layouts  10.9 us (6%)
  matrix products  7.67 us (4%)
  other arithmetic  7.02 us (4%)
    ppermute x49, starting transfers between devices, swap(): return lax.ppermute(values, axis, [(i, i ^ distance) for i in range(count)])  37 us
    pallas_call x1, Pallas kernels, mlp_grad(): pl.pallas_call(functools.partial(mlp_grad_kernel, len(pieces), chunk, len...  28.1 us
    pallas_call x2, Pallas kernels, hidden_back_of(): pl.pallas_call(functools.partial(hidden_back_kernel, tile, len(before) >...  19.5 us
    ppermute x49, waiting for transfers between devices, swap(): return lax.ppermute(values, axis, [(i, i ^ distance) for i in range(count)])  19.3 us
    pallas_call x1, Pallas kernels, attend_back(): pl.pallas_call(functools.partial(attend_back_kernel, chunk, slots, scale,...  16.4 us
    pallas_call x1, Pallas kernels, attend(): pl.pallas_call(functools.partial(attend_kernel, chunk, slots, scale, shif...  10.4 us
    pallas_call x1, Pallas kernels, mlp(): pl.pallas_call(functools.partial(mlp_kernel, min(512, units)), in_specs=[...  8.03 us
    dot_general x1, matrix products, per_device(): lax.dot_general(after(cot, rings), down_weight, (((1,), (1,)), ((), ())),...  6.28 us
  transfers between devices with their start and end apart: 53, of which 13 were waited for; matrix products, arithmetic and copies ran while one was open for 11% of the time, Pallas kernels for 45%

profile of v5, /device:TPU:0, one launch (start us, length us, event | category | flops | bytes accessed | tf_op | source)
XLA Modules:
  0.0 197.9 jit_solution(11697676503528282453)
XLA Ops:
  8.0 2.8 %shard_map.229 = (bf16[128,2048]{1,0:T(8,128)(2,1)S(1)}, bf16[32,2048]{1,0:T(8,128)(2,1)S(1)}, bf16[128,2048]{1,0:T(8,128)(2,1)S(1)}, bf16[32,2048]{1,0:T(8,128)...) custom-call(s32[4]{0:T(128)S(1)} %get-tuple-element.191.at_ref, ...), custom_call_target="tpu_custom_call" | custom-call | flops 2097152 | bytes 2097152 | tf_op jit(solution)/shard_map/pallas_call | solution.py:195
  10.8 3.1 %collective-permute-start = (bf16[32,2048]{1,0:T(8,128)(2,1)S(1)}, bf16[32,2048]{1,0:T(8,128)(2,1)S(1)}, u32[]{:S(2)}, u32[]{:S(2)}) collective-permute-start(bf16[32,2048]{1,0:T(8,128)(2,1)S(1)} %get-tuple-element.87), channel_id=1, source_target_pairs={{0,4},{4,0},{8,12},{12,8},{1,5},{5,1},{9,13},{13,9},{2,6},{6,2},{1... | collective-permute-start | bytes 393224 | tf_op jit(solution)/shard_map/ppermute | solution.py:21
  13.9 2.6 %collective-permute-start.2 = (bf16[32,2048]{1,0:T(8,128)(2,1)S(1)}, bf16[32,2048]{1,0:T(8,128)(2,1)S(1)}, u32[]{:S(2)}, u32[]{:S(2)}) collective-permute-start(bf16[32,2048]{1,0:T(8,128)(2,1)S(1)} %get-tuple-element.87), channel_id=1, source_target_pairs={{0,8},{4,12},{8,0},{12,4},{1,9},{5,13},{9,1},{13,5},{2,10},{6,14},... | collective-permute-start | bytes 393224 | tf_op jit(solution)/shard_map/ppermute | solution.py:21
  21.7 5.1 %collective-permute-done.2.refs_8_ = bf16[32,2048]{1,0:T(8,128)(2,1)S(1)} collective-permute-done((bf16[32,2048]{1,0:T(8,128)(2,1)S(1)}, bf16[32,2048]{1,0:T(8,128)(2,1)S(1)}, u32[]{:S(2)}, u32[]{:S(2)}) %collective-permute-start.2) | collective-permute-done | bytes 131104 | tf_op jit(solution)/shard_map/ppermute | solution.py:21
  26.8 1.6 collective-permute-start.1
  28.9 1.5 collective-permute-start.5
  30.4 6.3 %convolution_convert_fusion.hb_ref = bf16[128,2048]{1,0:T(8,128)(2,1)S(1)} fusion(bf16[128,2048]{1,0:T(8,128)(2,1)S(1)} %get-tuple-element.92, bf16[2048,2048]{1,0:T(8,128)(2,1)} %refs_3_.3), kind=kOutput, calls=%fused_computation | convolution fusion | flops 1074003968 | bytes 9437184 | tf_op jit(solution)/shard_map/dot_general | solution.py:772
  40.2 10.4 %shard_map.230 = (bf16[512,512]{1,0:T(8,128)(2,1)}, bf16[512,512]{1,0:T(8,128)(2,1)}, bf16[512,512]{1,0:T(8,128)(2,1)}, bf16[128,512]{1,0:T(8,128)(2,1)}, f32[4,...) custom-call(s32[16]{0:T(128)} %concatenate.19.at_ref, bf16[32,2048]{1,0:T(8,128)(2,1)} %get-tuple-element.201.refs_0_, ...), custom_call_target="tpu_custom_call" | custom-call | flops 3221225472 | bytes 6291456 | tf_op jit(solution)/shard_map/pallas_call | solution.py:271
  50.7 1.4 convolution_convert_fusion.1
  52.4 1.3 collective-permute-done.12
  55.9 3.5 %collective-permute-done.13 = bf16[32,2048]{1,0:T(8,128)(2,1)S(1)} collective-permute-done((bf16[32,2048]{1,0:T(8,128)(2,1)S(1)}, bf16[32,2048]{1,0:T(8,128)(2,1)S(1)}, u32[]{:S(2)}, u32[]{:S(2)}) %collective-permute-start.13) | collective-permute-done | bytes 131104 | tf_op jit(solution)/shard_map/ppermute | solution.py:21
  60.9 1.3 constant_dynamic-slice_fusion
  62.2 1.6 collective-permute-start.26
  63.8 5.8 %shard_map.231 = (bf16[2048,2048]{1,0:T(8,128)(2,1)S(1)}, bf16[2048,2048]{1,0:T(8,128)(2,1)S(1)}) custom-call(bf16[2048,2048]{1,0:T(8,128)(2,1)} %refs_15_.1, bf16[2048,2048]{1,0:T(8,128)(2,1)} %refs_16_.5), custom_call_target="tpu_custom_call" | custom-call | tf_op jit(solution)/shard_map/pallas_call | solution.py:144
  69.7 2.8 %collective-permute-start.16 = (bf16[32,2048]{1,0:T(8,128)(2,1)S(1)}, bf16[32,2048]{1,0:T(8,128)(2,1)S(1)}, u32[]{:S(2)}, u32[]{:S(2)}) collective-permute-start(bf16[32,2048]{1,0:T(8,128)(2,1)S(1)} %multiply_convert_fusion.refs_0_), channel_id=1, source_target_pairs={{0,4},{4,0},{8,12},{12,8},{1,5},{5,1},{9,13},{13,9},{2,6},{6,2},{1... | collective-permute-start | bytes 393224 | tf_op jit(solution)/shard_map/ppermute | solution.py:21
  73.4 1.5 collective-permute-start.18
  75.0 8.0 %shard_map.232 = (bf16[128,2048]{1,0:T(8,128)(2,1)S(1)}, bf16[128,2048]{1,0:T(8,128)(2,1)S(1)}, bf16[128,2048]{1,0:T(8,128)(2,1)S(1)}, bf16[128,2048]{1,0:T(8,128)(2,1)S(1)}) custom-call(bf16[128,2048]{1,0:T(8,128)(2,1)S(1)} %pad_maximum_fusion.x_ref, bf16[128,2048]{1,0:T(8,128)(2,1)S(1)} %convolution_convert_fusion.hb_ref, ...), custom_call_target="tpu_custom_call" | custom-call | tf_op jit(solution)/shard_map/pallas_call | solution.py:474
  83.1 2.3 %collective-permute-done.17.refs_2_ = bf16[32,2048]{1,0:T(8,128)(2,1)S(1)} collective-permute-done((bf16[32,2048]{1,0:T(8,128)(2,1)S(1)}, bf16[32,2048]{1,0:T(8,128)(2,1)S(1)}, u32[]{:S(2)}, u32[]{:S(2)}) %collective-permute-start.17) | collective-permute-done | bytes 131104 | tf_op jit(solution)/shard_map/ppermute | solution.py:21
  85.5 1.9 collective-permute-done.26.refs_1_.refs_9_
  88.8 1.5 collective-permute-start.24
  90.3 1.5 collective-permute-start.25
  91.8 2.1 %collective-permute-done.20 = bf16[32,2048]{1,0:T(8,128)(2,1)S(1)} collective-permute-done((bf16[32,2048]{1,0:T(8,128)(2,1)S(1)}, bf16[32,2048]{1,0:T(8,128)(2,1)S(1)}, u32[]{:S(2)}, u32[]{:S(2)}) %collective-permute-start.20) | collective-permute-done | bytes 131104 | tf_op jit(solution)/shard_map/ppermute | solution.py:21
  95.2 1.7 collective-permute-start.21
  97.8 1.8 collective-permute-start.23
  99.6 9.6 %shard_map.234 = (bf16[1024,2048]{1,0:T(8,128)(2,1)}, f32[128,2048]{1,0:T(8,128)}) custom-call(s32[4]{0:T(128)} %copy-done.27, bf16[512,2048]{1,0:T(8,128)(2,1)} %all-gather.2.cloned.1.call-done.refs_0_.refs_8_, bf16[256,2048]{1,0:T(8,128)(2,1)} %copy-done.8, bf16[256,2048]{1,0:T(8,128)(2,1)} %copy-done.9, bf16[2048,2048]{1,0:T(8,128)(2,1)} %refs_3_.3, ...), custom_call_target="tpu_custom_call" | custom-call | flops 4294967296 | bytes 12582912 | tf_op jit(solution)/shard_map/pallas_call | solution.py:548
  113.4 9.9 %shard_map.235 = (bf16[1024,2048]{1,0:T(8,128)(2,1)}, bf16[128,2048]{1,0:T(8,128)(2,1)}) custom-call(s32[4]{0:T(128)} %copy-done.27, bf16[512,2048]{1,0:T(8,128)(2,1)} %all-gather.2.cloned.1.call-done.refs_0_.refs_8_, bf16[256,2048]{1,0:T(8,128)(2,1)} %copy-done.8, bf16[256,2048]{1,0:T(8,128)(2,1)} %copy-done.9, ...), custom_call_target="tpu_custom_call", output_to_operand_aliasing={{0}: (7, {})} | custom-call | flops 4294967296 | bytes 12582912 | tf_op jit(solution)/shard_map/pallas_call | solution.py:548
  127.4 16.4 %shard_map.236 = (f32[4,256,512]{2,1,0:T(8,128)}, bf16[1,4,256,512]{3,2,1,0:T(8,128)(2,1)}, bf16[64,4096]{1,0:T(8,128)(2,1)}, bf16[64,4096]{1,0:T(8,128)(2,1)}) custom-call(s32[16]{0:T(128)} %concatenate.19.at_ref, s32[2]{0:T(128)} %add_multiply_fusion.starts_ref, bf16[32,2048]{1,0:T(8,128)(2,1)} %copy-done.10, bf16[32,2048]{1,0:T(8,128)(2,1)} %copy-done.15, ...), custom_call_target="tpu_custom_call" | custom-call | flops 2952790016 | bytes 9437184 | tf_op jit(solution)/shard_map/pallas_call | solution.py:413
  145.0 1.6 collective-permute-start.49
  150.1 28.1 %shard_map.237 = (f32[256,2048]{1,0:T(8,128)}, f32[256,2048]{1,0:T(8,128)}, f32[2048,256]{1,0:T(8,128)}, f32[1,256]{1,0:T(1,128)}) custom-call(s32[41]{0:T(128)} %concatenate.20.at_ref, bf16[128,2048]{1,0:T(8,128)(2,1)} %copy-done, bf16[128,2048]{1,0:T(8,128)(2,1)} %copy-done.32, bf16[128,2048]{1,0:T(8,128)(2,1)} %copy-done.31, ...), custom_call_target="tpu_custom_call" | custom-call | flops 20401094656 | bytes 25165824 | tf_op jit(solution)/shard_map/pallas_call | solution.py:679
  180.2 2.4 %add_reduce_fusion = (f32[256]{0:T(256)S(1)}, f32[256,512]{1,0:T(8,128)}, f32[256,512]{1,0:T(8,128)}, f32[256,512]{1,0:T(8,128)}) fusion(bf16[2048,512]{1,0:T(8,128)(2,1)} %refs_27_.1, s32[]{:T(128)S(6)} %select_n.82, bf16[2048,512]{1,0:T(8,128)(2,1)} %refs_26_.1, bf16[2048,512]{1,0:T(8,128)(2,1)} %refs_25_.1, f32[4,256,512]{2,1,0:T(8,128)S(1)} %convert_add_fusion), kind=kLoop, calls=%fused_computation.14 | loop fusion | flops 1179392 | bytes 3933188 | tf_op jit(solution)/shard_map/reduce_sum | solution.py:856
  184.7 2.5 %collective-permute-done.47 = bf16[32,4096]{1,0:T(8,128)(2,1)S(1)} collective-permute-done((bf16[32,4096]{1,0:T(8,128)(2,1)S(1)}, bf16[32,4096]{1,0:T(8,128)(2,1)S(1)}, u32[]{:S(2)}, u32[]{:S(2)}) %collective-permute-start.47) | collective-permute-done | bytes 262176 | tf_op jit(solution)/shard_map/ppermute | solution.py:21
  188.0 1.3 collective-permute-done.51
  (239 shorter events, 35.1 us)
Async XLA Ops:
  7.2 53.7 %all-gather.2.cloned.1.call-start = ((), (), s32[]{:S(2)}) async-start(), calls=%async_computation | async-start | bytes 2228224 | tf_op jit(solution)/shard_map/all_gather | solution.py:739
  10.8 10.9 %collective-permute-start = (bf16[32,2048]{1,0:T(8,128)(2,1)S(1)}, bf16[32,2048]{1,0:T(8,128)(2,1)S(1)}, u32[]{:S(2)}, u32[]{:S(2)}) collective-permute-start(bf16[32,2048]{1,0:T(8,128)(2,1)S(1)} %get-tuple-element.87), channel_id=1, source_target_pairs={{0,4},{4,0},{8,12},{12,8},{1,5},{5,1},{9,13},{13,9},{2,6},{6,2},{1... | collective-permute-start | bytes 393224 | tf_op jit(solution)/shard_map/ppermute | solution.py:21
  13.9 12.9 %collective-permute-start.2 = (bf16[32,2048]{1,0:T(8,128)(2,1)S(1)}, bf16[32,2048]{1,0:T(8,128)(2,1)S(1)}, u32[]{:S(2)}, u32[]{:S(2)}) collective-permute-start(bf16[32,2048]{1,0:T(8,128)(2,1)S(1)} %get-tuple-element.87), channel_id=1, source_target_pairs={{0,8},{4,12},{8,0},{12,4},{1,9},{5,13},{9,1},{13,5},{2,10},{6,14},... | collective-permute-start | bytes 393224 | tf_op jit(solution)/shard_map/ppermute | solution.py:21
  16.5 10.3 %collective-permute-start.4 = (bf16[32,2048]{1,0:T(8,128)(2,1)S(1)}, bf16[32,2048]{1,0:T(8,128)(2,1)S(1)}, u32[]{:S(2)}, u32[]{:S(2)}) collective-permute-start(bf16[32,2048]{1,0:T(8,128)(2,1)S(1)} %get-tuple-element.87), channel_id=1, source_target_pairs={{0,12},{4,8},{8,4},{12,0},{1,13},{5,9},{9,5},{13,1},{2,14},{6,10},... | collective-permute-start | bytes 393224 | tf_op jit(solution)/shard_map/ppermute | solution.py:21
  26.8 9.9 %collective-permute-start.1 = (bf16[32,2048]{1,0:T(8,128)(2,1)S(1)}, bf16[32,2048]{1,0:T(8,128)(2,1)S(1)}, u32[]{:S(2)}, u32[]{:S(2)}) collective-permute-start(bf16[32,2048]{1,0:T(8,128)(2,1)S(1)} %collective-permute-done.refs_4_), channel_id=1, source_target_pairs={{0,2},{1,3},{2,0},{3,1},{4,6},{5,7},{6,4},{7,5},{8,10},{9,11},{10,... | collective-permute-start | bytes 393224 | tf_op jit(solution)/shard_map/ppermute | solution.py:21
  28.4 8.3 %collective-permute-start.3 = (bf16[32,2048]{1,0:T(8,128)(2,1)S(1)}, bf16[32,2048]{1,0:T(8,128)(2,1)S(1)}, u32[]{:S(2)}, u32[]{:S(2)}) collective-permute-start(bf16[32,2048]{1,0:T(8,128)(2,1)S(1)} %collective-permute-done.2.refs_8_), channel_id=1, source_target_pairs={{0,2},{1,3},{2,0},{3,1},{4,6},{5,7},{6,4},{7,5},{8,10},{9,11},{10,... | collective-permute-start | bytes 393224 | tf_op jit(solution)/shard_map/ppermute | solution.py:21
  28.9 7.8 %collective-permute-start.5 = (bf16[32,2048]{1,0:T(8,128)(2,1)S(1)}, bf16[32,2048]{1,0:T(8,128)(2,1)S(1)}, u32[]{:S(2)}, u32[]{:S(2)}) collective-permute-start(bf16[32,2048]{1,0:T(8,128)(2,1)S(1)} %collective-permute-done.4.refs_12_), channel_id=1, source_target_pairs={{0,2},{1,3},{2,0},{3,1},{4,6},{5,7},{6,4},{7,5},{8,10},{9,11},{10,... | collective-permute-start | bytes 393224 | tf_op jit(solution)/shard_map/ppermute | solution.py:21
  53.8 5.6 %collective-permute-start.13 = (bf16[32,2048]{1,0:T(8,128)(2,1)S(1)}, bf16[32,2048]{1,0:T(8,128)(2,1)S(1)}, u32[]{:S(2)}, u32[]{:S(2)}) collective-permute-start(bf16[32,2048]{1,0:T(8,128)(2,1)S(1)} %slice.205), channel_id=1, source_target_pairs={{0,2},{1,3},{2,0},{3,1},{4,6},{5,7},{6,4},{7,5},{8,10},{9,11},{10,... | collective-permute-start | bytes 393224 | tf_op jit(solution)/shard_map/ppermute | solution.py:21
  59.6 10.0 %collective-permute-start.14 = (bf16[32,2048]{1,0:T(8,128)(2,1)S(1)}, bf16[32,2048]{1,0:T(8,128)(2,1)S(1)}, u32[]{:S(2)}, u32[]{:S(2)}) collective-permute-start(bf16[32,2048]{1,0:T(8,128)(2,1)S(1)} %multiply_convert_fusion.refs_0_), channel_id=1, source_target_pairs={{0,2},{1,3},{2,0},{3,1},{4,6},{5,7},{6,4},{7,5},{8,10},{9,11},{10,... | collective-permute-start | bytes 393224 | tf_op jit(solution)/shard_map/ppermute | solution.py:21
  62.2 25.2 %collective-permute-start.26 = (bf16[256,2048]{1,0:T(8,128)(2,1)S(1)}, bf16[256,2048]{1,0:T(8,128)(2,1)S(1)}, u32[]{:S(2)}, u32[]{:S(2)}) collective-permute-start(bf16[256,2048]{1,0:T(8,128)(2,1)S(1)} %constant_dynamic-slice_fusion), channel_id=1, source_target_pairs={{0,16},{16,0},{1,17},{17,1},{2,18},{18,2},{3,19},{19,3},{4,20},{20... | collective-permute-start | bytes 3145736 | tf_op jit(solution)/shard_map/ppermute | solution.py:26
  69.6 5.3 %collective-permute-start.15 = (bf16[64,2048]{1,0:T(8,128)(2,1)S(1)}, bf16[64,2048]{1,0:T(8,128)(2,1)S(1)}, u32[]{:S(2)}, u32[]{:S(2)}) collective-permute-start(bf16[64,2048]{1,0:T(8,128)(2,1)S(1)} %pad_maximum_fusion.2), channel_id=1, source_target_pairs={{0,1},{1,0},{2,3},{3,2},{4,5},{5,4},{6,7},{7,6},{8,9},{9,8},{10,11... | collective-permute-start | bytes 786440 | tf_op jit(solution)/shard_map/ppermute | solution.py:21
  69.7 13.3 %collective-permute-start.16 = (bf16[32,2048]{1,0:T(8,128)(2,1)S(1)}, bf16[32,2048]{1,0:T(8,128)(2,1)S(1)}, u32[]{:S(2)}, u32[]{:S(2)}) collective-permute-start(bf16[32,2048]{1,0:T(8,128)(2,1)S(1)} %multiply_convert_fusion.refs_0_), channel_id=1, source_target_pairs={{0,4},{4,0},{8,12},{12,8},{1,5},{5,1},{9,13},{13,9},{2,6},{6,2},{1... | collective-permute-start | bytes 393224 | tf_op jit(solution)/shard_map/ppermute | solution.py:21
  72.5 12.9 %collective-permute-start.17 = (bf16[32,2048]{1,0:T(8,128)(2,1)S(1)}, bf16[32,2048]{1,0:T(8,128)(2,1)S(1)}, u32[]{:S(2)}, u32[]{:S(2)}) collective-permute-start(bf16[32,2048]{1,0:T(8,128)(2,1)S(1)} %multiply_convert_fusion.refs_0_), channel_id=1, source_target_pairs={{0,8},{4,12},{8,0},{12,4},{1,9},{5,13},{9,1},{13,5},{2,10},{6,14},... | collective-permute-start | bytes 393224 | tf_op jit(solution)/shard_map/ppermute | solution.py:21
  73.4 12.0 %collective-permute-start.18 = (bf16[32,2048]{1,0:T(8,128)(2,1)S(1)}, bf16[32,2048]{1,0:T(8,128)(2,1)S(1)}, u32[]{:S(2)}, u32[]{:S(2)}) collective-permute-start(bf16[32,2048]{1,0:T(8,128)(2,1)S(1)} %multiply_convert_fusion.refs_0_), channel_id=1, source_target_pairs={{0,12},{4,8},{8,4},{12,0},{1,13},{5,9},{9,5},{13,1},{2,14},{6,10},... | collective-permute-start | bytes 393224 | tf_op jit(solution)/shard_map/ppermute | solution.py:21
  87.4 10.4 %collective-permute-start.27 = (bf16[256,2048]{1,0:T(8,128)(2,1)S(1)}, bf16[256,2048]{1,0:T(8,128)(2,1)S(1)}, u32[]{:S(2)}, u32[]{:S(2)}) collective-permute-start(bf16[256,2048]{1,0:T(8,128)(2,1)S(1)} %collective-permute-done.26.refs_1_.refs_9_), channel_id=1, source_target_pairs={{0,1},{1,0},{2,3},{3,2},{4,5},{5,4},{6,7},{7,6},{8,9},{9,8},{10,11... | collective-permute-start | bytes 3145736 | tf_op jit(solution)/shard_map/ppermute | solution.py:21
  87.5 6.4 %collective-permute-start.20 = (bf16[32,2048]{1,0:T(8,128)(2,1)S(1)}, bf16[32,2048]{1,0:T(8,128)(2,1)S(1)}, u32[]{:S(2)}, u32[]{:S(2)}) collective-permute-start(bf16[32,2048]{1,0:T(8,128)(2,1)S(1)} %slice.204), channel_id=1, source_target_pairs={{0,2},{1,3},{2,0},{3,1},{4,6},{5,7},{6,4},{7,5},{8,10},{9,11},{10,... | collective-permute-start | bytes 393224 | tf_op jit(solution)/shard_map/ppermute | solution.py:21
  88.8 20.4 %collective-permute-start.24 = (bf16[128,2048]{1,0:T(8,128)(2,1)S(1)}, bf16[128,2048]{1,0:T(8,128)(2,1)S(1)}, u32[]{:S(2)}, u32[]{:S(2)}) collective-permute-start(bf16[128,2048]{1,0:T(8,128)(2,1)S(1)} %shard_map.233.refs_0_), channel_id=1, source_target_pairs={{0,16},{16,0},{1,17},{17,1},{2,18},{18,2},{3,19},{19,3},{4,20},{20... | collective-permute-start | bytes 1572872 | tf_op jit(solution)/shard_map/ppermute | solution.py:26
  90.3 18.9 %collective-permute-start.25 = (bf16[128,2048]{1,0:T(8,128)(2,1)S(1)}, bf16[128,2048]{1,0:T(8,128)(2,1)S(1)}, u32[]{:S(2)}, u32[]{:S(2)}) collective-permute-start(bf16[128,2048]{1,0:T(8,128)(2,1)S(1)} %shard_map.233.refs_0_), channel_id=1, source_target_pairs={{0,2},{1,3},{2,0},{3,1},{4,6},{5,7},{6,4},{7,5},{8,10},{9,11},{10,... | collective-permute-start | bytes 1572872 | tf_op jit(solution)/shard_map/ppermute | solution.py:21
  95.2 14.1 %collective-permute-start.21 = (bf16[32,2048]{1,0:T(8,128)(2,1)S(1)}, bf16[32,2048]{1,0:T(8,128)(2,1)S(1)}, u32[]{:S(2)}, u32[]{:S(2)}) collective-permute-start(bf16[32,2048]{1,0:T(8,128)(2,1)S(1)} %get-tuple-element.128.refs_0_), channel_id=1, source_target_pairs={{0,4},{4,0},{8,12},{12,8},{1,5},{5,1},{9,13},{13,9},{2,6},{6,2},{1... | collective-permute-start | bytes 393224 | tf_op jit(solution)/shard_map/ppermute | solution.py:21
  96.9 12.4 %collective-permute-start.22 = (bf16[32,2048]{1,0:T(8,128)(2,1)S(1)}, bf16[32,2048]{1,0:T(8,128)(2,1)S(1)}, u32[]{:S(2)}, u32[]{:S(2)}) collective-permute-start(bf16[32,2048]{1,0:T(8,128)(2,1)S(1)} %get-tuple-element.128.refs_0_), channel_id=1, source_target_pairs={{0,8},{4,12},{8,0},{12,4},{1,9},{5,13},{9,1},{13,5},{2,10},{6,14},... | collective-permute-start | bytes 393224 | tf_op jit(solution)/shard_map/ppermute | solution.py:21
  97.8 11.4 %collective-permute-start.23 = (bf16[32,2048]{1,0:T(8,128)(2,1)S(1)}, bf16[32,2048]{1,0:T(8,128)(2,1)S(1)}, u32[]{:S(2)}, u32[]{:S(2)}) collective-permute-start(bf16[32,2048]{1,0:T(8,128)(2,1)S(1)} %get-tuple-element.128.refs_0_), channel_id=1, source_target_pairs={{0,12},{4,8},{8,4},{12,0},{1,13},{5,9},{9,5},{13,1},{2,14},{6,10},... | collective-permute-start | bytes 393224 | tf_op jit(solution)/shard_map/ppermute | solution.py:21
  109.3 14.0 %collective-permute-start.28 = (bf16[32,2048]{1,0:T(8,128)(2,1)S(1)}, bf16[32,2048]{1,0:T(8,128)(2,1)S(1)}, u32[]{:S(2)}, u32[]{:S(2)}) collective-permute-start(bf16[32,2048]{1,0:T(8,128)(2,1)S(1)} %get-tuple-element.128.refs_0_), channel_id=1, source_target_pairs={{0,2},{1,3},{2,0},{3,1},{4,6},{5,7},{6,4},{7,5},{8,10},{9,11},{10,... | collective-permute-start | bytes 393224 | tf_op jit(solution)/shard_map/ppermute | solution.py:21
  110.3 13.1 %collective-permute-start.29 = (bf16[32,2048]{1,0:T(8,128)(2,1)S(1)}, bf16[32,2048]{1,0:T(8,128)(2,1)S(1)}, u32[]{:S(2)}, u32[]{:S(2)}) collective-permute-start(bf16[32,2048]{1,0:T(8,128)(2,1)S(1)} %collective-permute-done.21.refs_4_), channel_id=1, source_target_pairs={{0,2},{1,3},{2,0},{3,1},{4,6},{5,7},{6,4},{7,5},{8,10},{9,11},{10,... | collective-permute-start | bytes 393224 | tf_op jit(solution)/shard_map/ppermute | solution.py:21
  111.4 12.0 %collective-permute-start.30 = (bf16[32,2048]{1,0:T(8,128)(2,1)S(1)}, bf16[32,2048]{1,0:T(8,128)(2,1)S(1)}, u32[]{:S(2)}, u32[]{:S(2)}) collective-permute-start(bf16[32,2048]{1,0:T(8,128)(2,1)S(1)} %collective-permute-done.22.refs_8_), channel_id=1, source_target_pairs={{0,2},{1,3},{2,0},{3,1},{4,6},{5,7},{6,4},{7,5},{8,10},{9,11},{10,... | collective-permute-start | bytes 393224 | tf_op jit(solution)/shard_map/ppermute | solution.py:21
  112.3 11.1 %collective-permute-start.31 = (bf16[32,2048]{1,0:T(8,128)(2,1)S(1)}, bf16[32,2048]{1,0:T(8,128)(2,1)S(1)}, u32[]{:S(2)}, u32[]{:S(2)}) collective-permute-start(bf16[32,2048]{1,0:T(8,128)(2,1)S(1)} %collective-permute-done.23.refs_12_), channel_id=1, source_target_pairs={{0,2},{1,3},{2,0},{3,1},{4,6},{5,7},{6,4},{7,5},{8,10},{9,11},{10,... | collective-permute-start | bytes 393224 | tf_op jit(solution)/shard_map/ppermute | solution.py:21
  125.6 19.4 %collective-permute-start.42 = (bf16[128,2048]{1,0:T(8,128)(2,1)S(1)}, bf16[128,2048]{1,0:T(8,128)(2,1)}, u32[]{:S(2)}, u32[]{:S(2)}) collective-permute-start(bf16[128,2048]{1,0:T(8,128)(2,1)S(1)} %collective-permute-done.24.refs_2_), channel_id=1, source_target_pairs={{0,2},{1,3},{2,0},{3,1},{4,6},{5,7},{6,4},{7,5},{8,10},{9,11},{10,... | collective-permute-start | bytes 1572872 | tf_op jit(solution)/shard_map/ppermute | solution.py:21
  144.5 4.5 %collective-permute-start.45 = (bf16[128,2048]{1,0:T(8,128)(2,1)S(1)}, bf16[128,2048]{1,0:T(8,128)(2,1)S(1)}, u32[]{:S(2)}, u32[]{:S(2)}) collective-permute-start(bf16[128,2048]{1,0:T(8,128)(2,1)S(1)} %collective-permute-done.24.refs_2_), channel_id=1, source_target_pairs={{0,1},{1,0},{2,3},{3,2},{4,5},{5,4},{6,7},{7,6},{8,9},{9,8},{10,11... | collective-permute-start | bytes 1572872 | tf_op jit(solution)/shard_map/ppermute | solution.py:21
  144.7 4.2 %collective-permute-start.44 = (bf16[128,2048]{1,0:T(8,128)(2,1)S(1)}, bf16[128,2048]{1,0:T(8,128)(2,1)S(1)}, u32[]{:S(2)}, u32[]{:S(2)}) collective-permute-start(bf16[128,2048]{1,0:T(8,128)(2,1)S(1)} %collective-permute-done.25.refs_1_), channel_id=1, source_target_pairs={{0,1},{1,0},{2,3},{3,2},{4,5},{5,4},{6,7},{7,6},{8,9},{9,8},{10,11... | collective-permute-start | bytes 1572872 | tf_op jit(solution)/shard_map/ppermute | solution.py:21
  145.0 34.8 %collective-permute-start.49 = (bf16[4,256,512]{2,1,0:T(8,128)(2,1)}, bf16[4,256,512]{2,1,0:T(8,128)(2,1)S(1)}, u32[]{:S(2)}, u32[]{:S(2)}) collective-permute-start(bf16[4,256,512]{2,1,0:T(8,128)(2,1)} %bitcast.48), channel_id=1, source_target_pairs={{0,16},{16,0},{1,17},{17,1},{2,18},{18,2},{3,19},{19,3},{4,20},{20... | collective-permute-start | bytes 3145736 | tf_op jit(solution)/shard_map/ppermute | solution.py:26
  147.8 30.4 %collective-permute-start.41 = (bf16[32,4096]{1,0:T(8,128)(2,1)S(1)}, bf16[32,4096]{1,0:T(8,128)(2,1)S(1)}, u32[]{:S(2)}, u32[]{:S(2)}) collective-permute-start(bf16[32,4096]{1,0:T(8,128)(2,1)S(1)} %slice.203), channel_id=1, source_target_pairs={{0,2},{1,3},{2,0},{3,1},{4,6},{5,7},{6,4},{7,5},{8,10},{9,11},{10,... | collective-permute-start | bytes 786440 | tf_op jit(solution)/shard_map/ppermute | solution.py:21
  178.7 8.5 %collective-permute-start.47 = (bf16[32,4096]{1,0:T(8,128)(2,1)S(1)}, bf16[32,4096]{1,0:T(8,128)(2,1)S(1)}, u32[]{:S(2)}, u32[]{:S(2)}) collective-permute-start(bf16[32,4096]{1,0:T(8,128)(2,1)S(1)} %get-tuple-element.202), channel_id=1, source_target_pairs={{0,2},{1,3},{2,0},{3,1},{4,6},{5,7},{6,4},{7,5},{8,10},{9,11},{10,... | collective-permute-start | bytes 786440 | tf_op jit(solution)/shard_map/ppermute | solution.py:21
  182.7 4.7 %collective-permute-start.50 = (f32[2,256]{1,0:T(2,128)S(1)}, f32[2,256]{1,0:T(2,128)S(1)}, u32[]{:S(2)}, u32[]{:S(2)}) collective-permute-start(f32[2,256]{1,0:T(2,128)S(1)} %pad_maximum_fusion.4), channel_id=1, source_target_pairs={{0,2},{1,3},{2,0},{3,1},{4,6},{5,7},{6,4},{7,5},{8,10},{9,11},{10,... | collective-permute-start | bytes 6152 | tf_op jit(solution)/shard_map/ppermute | solution.py:21
  (70 other events, 431.1 us)
Sparse Core Ops, SparseCore 0:
  16.6 44.0 all-gather.1

commit v6 on v5

--- a/solution.py
+++ b/solution.py
@@ -156,9 +156,11 @@
 
 def arrange_kernel(
     at_ref, rows_hbm, cot_hbm, gain_ref, normed_ref, mine_ref, cots_ref, cot_mine_ref,
-    inputs_ref, scaled_ref, root_ref, rows_in, rows_sem, cot_sem,
+    inputs_ref, scaled_ref, root_ref, rows_in, gain_in, rows_sem, cot_sem, gain_sem,
 ):
     chunk = mine_ref.shape[0]
+    gain_copy = pltpu.make_async_copy(gain_ref, gain_in, gain_sem)
+    gain_copy.start()
     spots = chunk_places(at_ref, 0, normed_ref.shape[0] // chunk, chunk)
     parts = [slice(i * chunk, (i + 1) * chunk) for i in range(len(spots))]
     copies = []
@@ -170,7 +172,8 @@
     for pair in copies:
         for copy in pair:
             copy.start()
-    gain = gain_ref[...].astype(F32).reshape(1, -1)
+    gain_copy.wait()
+    gain = gain_in[...].astype(F32).reshape(1, -1)
     for i, (part, pair) in enumerate(zip(parts, copies, strict=True)):
         pair[0].wait()
         rows = rows_in[part, :].astype(F32)
@@ -194,17 +197,18 @@
     more = [(chunk, width)] * 3
     return pl.pallas_call(
         arrange_kernel,
-        in_specs=[pl.BlockSpec(memory_space=pltpu.SMEM), HBM_WHOLE, HBM_WHOLE, VMEM_WHOLE],
+        in_specs=[pl.BlockSpec(memory_space=pltpu.SMEM), HBM_WHOLE, HBM_WHOLE, HBM_WHOLE],
         out_specs=[VMEM_WHOLE] * 7,
         out_shape=[jax.ShapeDtypeStruct(shape, BF) for shape in shapes]
         + [jax.ShapeDtypeStruct(shape, F32) for shape in more],
-        scratch_shapes=[pltpu.VMEM((count, width), BF),
-                        pltpu.SemaphoreType.DMA((slots,)), pltpu.SemaphoreType.DMA((slots,))],
+        scratch_shapes=[pltpu.VMEM((count, width), BF), pltpu.VMEM(gain.shape, BF),
+                        pltpu.SemaphoreType.DMA((slots,)), pltpu.SemaphoreType.DMA((slots,)),
+                        pltpu.SemaphoreType.DMA],
         compiler_params=pltpu.CompilerParams(vmem_limit_bytes=16 * MIB),
         cost_estimate=pl.CostEstimate(
             flops=8 * count * width, bytes_accessed=8 * count * width, transcendentals=0
         ),
-    )(places, in_hbm(rows), in_hbm(cot), gain)
+    )(places, in_hbm(rows), in_hbm(cot), in_hbm(gain))
 
 
 def column_of(row):
@@ -495,6 +499,30 @@
     return listed
 
 
+def own_hidden_back_kernel(rows_ref, wd_ref, out_ref):
+    out_ref[...] = dot_nt(rows_ref[...], wd_ref[...]).astype(BF)
+
+
+def own_hidden_back(rows, wd):
+    count, width = rows.shape
+    units = wd.shape[0]
+    block = min(512, units)
+    return pl.pallas_call(
+        own_hidden_back_kernel,
+        grid=(units // block,),
+        in_specs=[
+            pl.BlockSpec((count, width), lambda i: (0, 0), pipeline_mode=pl.Buffered(1)),
+            pl.BlockSpec((block, width), lambda i: (i, 0)),
+        ],
+        out_specs=pl.BlockSpec((count, block), lambda i: (0, i)),
+        out_shape=jax.ShapeDtypeStruct((count, units), BF),
+        compiler_params=pltpu.CompilerParams(vmem_limit_bytes=24 * MIB),
+        cost_estimate=pl.CostEstimate(
+            flops=2 * count * width * units, bytes_accessed=2 * width * units, transcendentals=0
+        ),
+    )(rows, in_hbm(wd))
+
+
 def hidden_back_kernel(tile, more, count, at_ref, *refs):
     sources, (wd_ref, hidden_ref, before) = refs[:count], refs[count : count + 3]
     out_ref, sum_ref, cot, total, sem = refs[-5:]
@@ -769,9 +797,7 @@
     cos = jnp.asarray(np.concatenate([np.cos(angles), np.cos(angles)], axis=1))
     sin = jnp.asarray(np.concatenate([-np.sin(angles), np.sin(angles)], axis=1))
     rings = [after(ring, seq_places, starts, places) for ring in rings]
-    hidden_back = lax.dot_general(
-        after(cot, rings), down_weight, (((1,), (1,)), ((), ())), preferred_element_type=F32
-    ).astype(BF)
+    hidden_back = own_hidden_back(after(cot, rings), down_weight)
     seq_pieces = spread(rings, hidden_back)
     own_pieces = [normed_first[i * chunk : (i + 1) * chunk] for i in range(n_t)]
     q, k, v, attended, mass, x_seq = attend(

time: 198 us -> 198 us (level)
  matrix products: 7.67 us -> 1.39 us
  Pallas kernels: 91.7 us -> 97.6 us
    dot_general x1 -> x0, matrix products: 6.28 us -> none  [per_device(): lax.dot_general(after(cot, rings), down_weight, (((1,), (1,)), ((), ())),...]
    pallas_call x0 -> x1, Pallas kernels: none -> 5.92 us  [own_hidden_back(): pl.pallas_call(own_hidden_back_kernel, grid=(units // block,), in_specs=[...]
    unnamed x99 -> x97, local copies, waits for them, and re-layouts: 4.18 us -> 3.49 us
  transfers between devices with their start and end apart: 53 -> 53, of which waited for: 13 -> 15; matrix products, arithmetic and copies ran while one was open for 11% -> 8% of each run, Pallas kernels for 45% -> 48%
where the time goes in v6:
time: 198 us; the launch traced here: 197 us
  Pallas kernels  97.6 us (49%)
  starting transfers between devices  42.2 us (21%)
  waiting for transfers between devices  21.4 us (11%)
  between operations  17.5 us (9%)
  local copies, waits for them, and re-layouts  10.2 us (5%)
  other arithmetic  6.9 us (3%)
    ppermute x49, starting transfers between devices, swap(): return lax.ppermute(values, axis, [(i, i ^ distance) for i in range(count)])  37.4 us
    pallas_call x1, Pallas kernels, mlp_grad(): pl.pallas_call(functools.partial(mlp_grad_kernel, len(pieces), chunk, len...  28.1 us
    pallas_call x2, Pallas kernels, hidden_back_of(): pl.pallas_call(functools.partial(hidden_back_kernel, tile, len(before) >...  19.5 us
    ppermute x49, waiting for transfers between devices, swap(): return lax.ppermute(values, axis, [(i, i ^ distance) for i in range(count)])  19.3 us
    pallas_call x1, Pallas kernels, attend_back(): pl.pallas_call(functools.partial(attend_back_kernel, chunk, slots, scale,...  16.4 us
    pallas_call x1, Pallas kernels, attend(): pl.pallas_call(functools.partial(attend_kernel, chunk, slots, scale, shif...  10.1 us
    pallas_call x1, Pallas kernels, mlp(): pl.pallas_call(functools.partial(mlp_kernel, min(512, units)), in_specs=[...  8.03 us
    pallas_call x1, Pallas kernels, own_hidden_back(): pl.pallas_call(own_hidden_back_kernel, grid=(units // block,), in_specs=[...  5.92 us
  transfers between devices with their start and end apart: 53, of which 15 were waited for; matrix products, arithmetic and copies ran while one was open for 8% of the time, Pallas kernels for 48%

profile of v6, /device:TPU:0, one launch (start us, length us, event | category | flops | bytes accessed | tf_op | source)
XLA Modules:
  0.0 197.2 jit_solution(7452520650637270072)
XLA Ops:
  7.3 2.9 %shard_map.229 = (bf16[128,2048]{1,0:T(8,128)(2,1)S(1)}, bf16[32,2048]{1,0:T(8,128)(2,1)S(1)}, bf16[128,2048]{1,0:T(8,128)(2,1)S(1)}, bf16[32,2048]{1,0:T(8,128)...) custom-call(s32[4]{0:T(128)S(1)} %get-tuple-element.191.at_ref, ...), custom_call_target="tpu_custom_call" | custom-call | flops 2097152 | bytes 2097152 | tf_op jit(solution)/shard_map/pallas_call | solution.py:198
  10.2 3.1 %collective-permute-start = (bf16[32,2048]{1,0:T(8,128)(2,1)S(1)}, bf16[32,2048]{1,0:T(8,128)(2,1)S(1)}, u32[]{:S(2)}, u32[]{:S(2)}) collective-permute-start(bf16[32,2048]{1,0:T(8,128)(2,1)S(1)} %get-tuple-element.87), channel_id=1, source_target_pairs={{0,4},{4,0},{8,12},{12,8},{1,5},{5,1},{9,13},{13,9},{2,6},{6,2},{1... | collective-permute-start | bytes 393224 | tf_op jit(solution)/shard_map/ppermute | solution.py:21
  13.3 2.6 %collective-permute-start.2 = (bf16[32,2048]{1,0:T(8,128)(2,1)S(1)}, bf16[32,2048]{1,0:T(8,128)(2,1)S(1)}, u32[]{:S(2)}, u32[]{:S(2)}) collective-permute-start(bf16[32,2048]{1,0:T(8,128)(2,1)S(1)} %get-tuple-element.87), channel_id=1, source_target_pairs={{0,8},{4,12},{8,0},{12,4},{1,9},{5,13},{9,1},{13,5},{2,10},{6,14},... | collective-permute-start | bytes 393224 | tf_op jit(solution)/shard_map/ppermute | solution.py:21
  21.0 5.2 %collective-permute-done.2.refs_8_ = bf16[32,2048]{1,0:T(8,128)(2,1)S(1)} collective-permute-done((bf16[32,2048]{1,0:T(8,128)(2,1)S(1)}, bf16[32,2048]{1,0:T(8,128)(2,1)S(1)}, u32[]{:S(2)}, u32[]{:S(2)}) %collective-permute-start.2) | collective-permute-done | bytes 131104 | tf_op jit(solution)/shard_map/ppermute | solution.py:21
  26.3 1.6 collective-permute-start.1
  28.3 1.5 collective-permute-start.5
  29.8 5.9 %shard_map.230.hb_ref = bf16[128,2048]{1,0:T(8,128)(2,1)S(1)} custom-call(bf16[128,2048]{1,0:T(8,128)(2,1)S(1)} %get-tuple-element.92.rows_ref, bf16[2048,2048]{1,0:T(8,128)(2,1)} %refs_3_.3), custom_call_target="tpu_custom_call" | custom-call | flops 1073741824 | bytes 8388608 | tf_op jit(solution)/shard_map/pallas_call | solution.py:510
  39.4 10.1 %shard_map.231 = (bf16[512,512]{1,0:T(8,128)(2,1)}, bf16[512,512]{1,0:T(8,128)(2,1)}, bf16[512,512]{1,0:T(8,128)(2,1)}, bf16[128,512]{1,0:T(8,128)(2,1)}, f32[4,...) custom-call(s32[16]{0:T(128)} %concatenate.19.at_ref, bf16[32,2048]{1,0:T(8,128)(2,1)} %get-tuple-element.201.refs_0_, ...), custom_call_target="tpu_custom_call" | custom-call | flops 3221225472 | bytes 6291456 | tf_op jit(solution)/shard_map/pallas_call | solution.py:275
  49.5 1.4 convolution_convert_fusion
  52.8 1.4 collective-permute-start.13
  55.1 3.3 %collective-permute-done.13 = bf16[32,2048]{1,0:T(8,128)(2,1)S(1)} collective-permute-done((bf16[32,2048]{1,0:T(8,128)(2,1)S(1)}, bf16[32,2048]{1,0:T(8,128)(2,1)S(1)}, u32[]{:S(2)}, u32[]{:S(2)}) %collective-permute-start.13) | collective-permute-done | bytes 131104 | tf_op jit(solution)/shard_map/ppermute | solution.py:21
  58.6 1.5 collective-permute-start.14
  60.1 1.3 constant_dynamic-slice_fusion
  61.5 1.6 collective-permute-start.26
  63.1 5.8 %shard_map.232 = (bf16[2048,2048]{1,0:T(8,128)(2,1)S(1)}, bf16[2048,2048]{1,0:T(8,128)(2,1)S(1)}) custom-call(bf16[2048,2048]{1,0:T(8,128)(2,1)} %refs_15_.1, bf16[2048,2048]{1,0:T(8,128)(2,1)} %refs_16_.5), custom_call_target="tpu_custom_call" | custom-call | tf_op jit(solution)/shard_map/pallas_call | solution.py:144
  69.0 2.7 %collective-permute-start.16 = (bf16[32,2048]{1,0:T(8,128)(2,1)S(1)}, bf16[32,2048]{1,0:T(8,128)(2,1)S(1)}, u32[]{:S(2)}, u32[]{:S(2)}) collective-permute-start(bf16[32,2048]{1,0:T(8,128)(2,1)S(1)} %multiply_convert_fusion.refs_0_), channel_id=1, source_target_pairs={{0,4},{4,0},{8,12},{12,8},{1,5},{5,1},{9,13},{13,9},{2,6},{6,2},{1... | collective-permute-start | bytes 393224 | tf_op jit(solution)/shard_map/ppermute | solution.py:21
  72.7 1.4 collective-permute-start.18
  74.2 8.0 %shard_map.233 = (bf16[128,2048]{1,0:T(8,128)(2,1)S(1)}, bf16[128,2048]{1,0:T(8,128)(2,1)S(1)}, bf16[128,2048]{1,0:T(8,128)(2,1)S(1)}, bf16[128,2048]{1,0:T(8,128)(2,1)S(1)}) custom-call(bf16[128,2048]{1,0:T(8,128)(2,1)S(1)} %pad_maximum_fusion.x_ref, bf16[128,2048]{1,0:T(8,128)(2,1)S(1)} %shard_map.230.hb_ref, ...), custom_call_target="tpu_custom_call" | custom-call | tf_op jit(solution)/shard_map/pallas_call | solution.py:478
  82.3 2.3 %collective-permute-done.17.refs_2_ = bf16[32,2048]{1,0:T(8,128)(2,1)S(1)} collective-permute-done((bf16[32,2048]{1,0:T(8,128)(2,1)S(1)}, bf16[32,2048]{1,0:T(8,128)(2,1)S(1)}, u32[]{:S(2)}, u32[]{:S(2)}) %collective-permute-start.17) | collective-permute-done | bytes 131104 | tf_op jit(solution)/shard_map/ppermute | solution.py:21
  84.7 2.1 %collective-permute-done.26.refs_1_.refs_9_ = bf16[256,2048]{1,0:T(8,128)(2,1)S(1)} collective-permute-done((bf16[256,2048]{1,0:T(8,128)(2,1)S(1)}, bf16[256,2048]{1,0:T(8,128)(2,1)S(1)}, u32[]{:S(2)}, u32[]{:S(2)}) %collective-permute-start.26) | collective-permute-done | bytes 1048608 | tf_op jit(solution)/shard_map/ppermute | solution.py:26
  88.4 1.5 collective-permute-start.24
  89.9 1.5 collective-permute-start.25
  91.4 1.7 collective-permute-done.20
  94.5 1.4 collective-permute-start.21
  97.2 1.7 collective-permute-start.23
  98.9 9.6 %shard_map.235 = (bf16[1024,2048]{1,0:T(8,128)(2,1)}, f32[128,2048]{1,0:T(8,128)}) custom-call(s32[4]{0:T(128)} %copy-done.25, bf16[512,2048]{1,0:T(8,128)(2,1)} %all-gather.2.cloned.1.call-done.refs_0_.refs_8_, bf16[256,2048]{1,0:T(8,128)(2,1)} %copy-done.6, bf16[256,2048]{1,0:T(8,128)(2,1)} %copy-done.7, bf16[2048,2048]{1,0:T(8,128)(2,1)} %refs_3_.3, ...), custom_call_target="tpu_custom_call" | custom-call | flops 4294967296 | bytes 12582912 | tf_op jit(solution)/shard_map/pallas_call | solution.py:576
  112.8 9.9 %shard_map.236 = (bf16[1024,2048]{1,0:T(8,128)(2,1)}, bf16[128,2048]{1,0:T(8,128)(2,1)}) custom-call(s32[4]{0:T(128)} %copy-done.25, bf16[512,2048]{1,0:T(8,128)(2,1)} %all-gather.2.cloned.1.call-done.refs_0_.refs_8_, bf16[256,2048]{1,0:T(8,128)(2,1)} %copy-done.6, bf16[256,2048]{1,0:T(8,128)(2,1)} %copy-done.7, ...), custom_call_target="tpu_custom_call", output_to_operand_aliasing={{0}: (7, {})} | custom-call | flops 4294967296 | bytes 12582912 | tf_op jit(solution)/shard_map/pallas_call | solution.py:576
  126.7 16.4 %shard_map.237 = (f32[4,256,512]{2,1,0:T(8,128)}, bf16[1,4,256,512]{3,2,1,0:T(8,128)(2,1)}, bf16[64,4096]{1,0:T(8,128)(2,1)}, bf16[64,4096]{1,0:T(8,128)(2,1)}) custom-call(s32[16]{0:T(128)} %concatenate.19.at_ref, s32[2]{0:T(128)} %add_multiply_fusion.starts_ref, bf16[32,2048]{1,0:T(8,128)(2,1)} %copy-done.8, bf16[32,2048]{1,0:T(8,128)(2,1)} %copy-done.13, ...), custom_call_target="tpu_custom_call" | custom-call | flops 2952790016 | bytes 9437184 | tf_op jit(solution)/shard_map/pallas_call | solution.py:417
  144.3 1.6 collective-permute-start.49
  149.4 28.1 %shard_map.238 = (f32[256,2048]{1,0:T(8,128)}, f32[256,2048]{1,0:T(8,128)}, f32[2048,256]{1,0:T(8,128)}, f32[1,256]{1,0:T(1,128)}) custom-call(s32[41]{0:T(128)} %concatenate.20.at_ref, bf16[128,2048]{1,0:T(8,128)(2,1)} %copy-done, bf16[128,2048]{1,0:T(8,128)(2,1)} %copy-done.31, bf16[128,2048]{1,0:T(8,128)(2,1)} %copy-done.30, ...), custom_call_target="tpu_custom_call" | custom-call | flops 20401094656 | bytes 25165824 | tf_op jit(solution)/shard_map/pallas_call | solution.py:707
  179.5 2.4 %add_reduce_fusion = (f32[256]{0:T(256)S(1)}, f32[256,512]{1,0:T(8,128)}, f32[256,512]{1,0:T(8,128)}, f32[256,512]{1,0:T(8,128)}) fusion(bf16[2048,512]{1,0:T(8,128)(2,1)} %refs_27_.1, s32[]{:T(128)S(6)} %select_n.82, bf16[2048,512]{1,0:T(8,128)(2,1)} %refs_26_.1, bf16[2048,512]{1,0:T(8,128)(2,1)} %refs_25_.1, f32[4,256,512]{2,1,0:T(8,128)S(1)} %convert_add_fusion), kind=kLoop, calls=%fused_computation.13 | loop fusion | flops 1179392 | bytes 3933188 | tf_op jit(solution)/shard_map/reduce_sum | solution.py:882
  184.0 2.5 %collective-permute-done.47 = bf16[32,4096]{1,0:T(8,128)(2,1)S(1)} collective-permute-done((bf16[32,4096]{1,0:T(8,128)(2,1)S(1)}, bf16[32,4096]{1,0:T(8,128)(2,1)S(1)}, u32[]{:S(2)}, u32[]{:S(2)}) %collective-permute-start.47) | collective-permute-done | bytes 262176 | tf_op jit(solution)/shard_map/ppermute | solution.py:21
  (237 shorter events, 35.4 us)
Async XLA Ops:
  7.2 53.0 %all-gather.2.cloned.1.call-start = ((), (), s32[]{:S(2)}) async-start(), calls=%async_computation | async-start | bytes 2228224 | tf_op jit(solution)/shard_map/all_gather | solution.py:767
  10.2 10.8 %collective-permute-start = (bf16[32,2048]{1,0:T(8,128)(2,1)S(1)}, bf16[32,2048]{1,0:T(8,128)(2,1)S(1)}, u32[]{:S(2)}, u32[]{:S(2)}) collective-permute-start(bf16[32,2048]{1,0:T(8,128)(2,1)S(1)} %get-tuple-element.87), channel_id=1, source_target_pairs={{0,4},{4,0},{8,12},{12,8},{1,5},{5,1},{9,13},{13,9},{2,6},{6,2},{1... | collective-permute-start | bytes 393224 | tf_op jit(solution)/shard_map/ppermute | solution.py:21
  13.3 12.9 %collective-permute-start.2 = (bf16[32,2048]{1,0:T(8,128)(2,1)S(1)}, bf16[32,2048]{1,0:T(8,128)(2,1)S(1)}, u32[]{:S(2)}, u32[]{:S(2)}) collective-permute-start(bf16[32,2048]{1,0:T(8,128)(2,1)S(1)} %get-tuple-element.87), channel_id=1, source_target_pairs={{0,8},{4,12},{8,0},{12,4},{1,9},{5,13},{9,1},{13,5},{2,10},{6,14},... | collective-permute-start | bytes 393224 | tf_op jit(solution)/shard_map/ppermute | solution.py:21
  15.9 10.3 %collective-permute-start.4 = (bf16[32,2048]{1,0:T(8,128)(2,1)S(1)}, bf16[32,2048]{1,0:T(8,128)(2,1)S(1)}, u32[]{:S(2)}, u32[]{:S(2)}) collective-permute-start(bf16[32,2048]{1,0:T(8,128)(2,1)S(1)} %get-tuple-element.87), channel_id=1, source_target_pairs={{0,12},{4,8},{8,4},{12,0},{1,13},{5,9},{9,5},{13,1},{2,14},{6,10},... | collective-permute-start | bytes 393224 | tf_op jit(solution)/shard_map/ppermute | solution.py:21
  26.3 9.5 %collective-permute-start.1 = (bf16[32,2048]{1,0:T(8,128)(2,1)S(1)}, bf16[32,2048]{1,0:T(8,128)(2,1)S(1)}, u32[]{:S(2)}, u32[]{:S(2)}) collective-permute-start(bf16[32,2048]{1,0:T(8,128)(2,1)S(1)} %collective-permute-done.refs_4_), channel_id=1, source_target_pairs={{0,2},{1,3},{2,0},{3,1},{4,6},{5,7},{6,4},{7,5},{8,10},{9,11},{10,... | collective-permute-start | bytes 393224 | tf_op jit(solution)/shard_map/ppermute | solution.py:21
  27.8 8.0 %collective-permute-start.3 = (bf16[32,2048]{1,0:T(8,128)(2,1)S(1)}, bf16[32,2048]{1,0:T(8,128)(2,1)S(1)}, u32[]{:S(2)}, u32[]{:S(2)}) collective-permute-start(bf16[32,2048]{1,0:T(8,128)(2,1)S(1)} %collective-permute-done.2.refs_8_), channel_id=1, source_target_pairs={{0,2},{1,3},{2,0},{3,1},{4,6},{5,7},{6,4},{7,5},{8,10},{9,11},{10,... | collective-permute-start | bytes 393224 | tf_op jit(solution)/shard_map/ppermute | solution.py:21
  28.3 7.7 %collective-permute-start.5 = (bf16[32,2048]{1,0:T(8,128)(2,1)S(1)}, bf16[32,2048]{1,0:T(8,128)(2,1)S(1)}, u32[]{:S(2)}, u32[]{:S(2)}) collective-permute-start(bf16[32,2048]{1,0:T(8,128)(2,1)S(1)} %collective-permute-done.4.refs_12_), channel_id=1, source_target_pairs={{0,2},{1,3},{2,0},{3,1},{4,6},{5,7},{6,4},{7,5},{8,10},{9,11},{10,... | collective-permute-start | bytes 393224 | tf_op jit(solution)/shard_map/ppermute | solution.py:21
  52.8 5.6 %collective-permute-start.13 = (bf16[32,2048]{1,0:T(8,128)(2,1)S(1)}, bf16[32,2048]{1,0:T(8,128)(2,1)S(1)}, u32[]{:S(2)}, u32[]{:S(2)}) collective-permute-start(bf16[32,2048]{1,0:T(8,128)(2,1)S(1)} %slice.205), channel_id=1, source_target_pairs={{0,2},{1,3},{2,0},{3,1},{4,6},{5,7},{6,4},{7,5},{8,10},{9,11},{10,... | collective-permute-start | bytes 393224 | tf_op jit(solution)/shard_map/ppermute | solution.py:21
  58.6 10.2 %collective-permute-start.14 = (bf16[32,2048]{1,0:T(8,128)(2,1)S(1)}, bf16[32,2048]{1,0:T(8,128)(2,1)S(1)}, u32[]{:S(2)}, u32[]{:S(2)}) collective-permute-start(bf16[32,2048]{1,0:T(8,128)(2,1)S(1)} %multiply_convert_fusion.refs_0_), channel_id=1, source_target_pairs={{0,2},{1,3},{2,0},{3,1},{4,6},{5,7},{6,4},{7,5},{8,10},{9,11},{10,... | collective-permute-start | bytes 393224 | tf_op jit(solution)/shard_map/ppermute | solution.py:21
  61.5 25.3 %collective-permute-start.26 = (bf16[256,2048]{1,0:T(8,128)(2,1)S(1)}, bf16[256,2048]{1,0:T(8,128)(2,1)S(1)}, u32[]{:S(2)}, u32[]{:S(2)}) collective-permute-start(bf16[256,2048]{1,0:T(8,128)(2,1)S(1)} %constant_dynamic-slice_fusion), channel_id=1, source_target_pairs={{0,16},{16,0},{1,17},{17,1},{2,18},{18,2},{3,19},{19,3},{4,20},{20... | collective-permute-start | bytes 3145736 | tf_op jit(solution)/shard_map/ppermute | solution.py:26
  68.9 5.2 %collective-permute-start.15 = (bf16[64,2048]{1,0:T(8,128)(2,1)S(1)}, bf16[64,2048]{1,0:T(8,128)(2,1)S(1)}, u32[]{:S(2)}, u32[]{:S(2)}) collective-permute-start(bf16[64,2048]{1,0:T(8,128)(2,1)S(1)} %pad_maximum_fusion.2), channel_id=1, source_target_pairs={{0,1},{1,0},{2,3},{3,2},{4,5},{5,4},{6,7},{7,6},{8,9},{9,8},{10,11... | collective-permute-start | bytes 786440 | tf_op jit(solution)/shard_map/ppermute | solution.py:21
  69.0 13.3 %collective-permute-start.16 = (bf16[32,2048]{1,0:T(8,128)(2,1)S(1)}, bf16[32,2048]{1,0:T(8,128)(2,1)S(1)}, u32[]{:S(2)}, u32[]{:S(2)}) collective-permute-start(bf16[32,2048]{1,0:T(8,128)(2,1)S(1)} %multiply_convert_fusion.refs_0_), channel_id=1, source_target_pairs={{0,4},{4,0},{8,12},{12,8},{1,5},{5,1},{9,13},{13,9},{2,6},{6,2},{1... | collective-permute-start | bytes 393224 | tf_op jit(solution)/shard_map/ppermute | solution.py:21
  71.7 12.9 %collective-permute-start.17 = (bf16[32,2048]{1,0:T(8,128)(2,1)S(1)}, bf16[32,2048]{1,0:T(8,128)(2,1)S(1)}, u32[]{:S(2)}, u32[]{:S(2)}) collective-permute-start(bf16[32,2048]{1,0:T(8,128)(2,1)S(1)} %multiply_convert_fusion.refs_0_), channel_id=1, source_target_pairs={{0,8},{4,12},{8,0},{12,4},{1,9},{5,13},{9,1},{13,5},{2,10},{6,14},... | collective-permute-start | bytes 393224 | tf_op jit(solution)/shard_map/ppermute | solution.py:21
  72.7 11.9 %collective-permute-start.18 = (bf16[32,2048]{1,0:T(8,128)(2,1)S(1)}, bf16[32,2048]{1,0:T(8,128)(2,1)S(1)}, u32[]{:S(2)}, u32[]{:S(2)}) collective-permute-start(bf16[32,2048]{1,0:T(8,128)(2,1)S(1)} %multiply_convert_fusion.refs_0_), channel_id=1, source_target_pairs={{0,12},{4,8},{8,4},{12,0},{1,13},{5,9},{9,5},{13,1},{2,14},{6,10},... | collective-permute-start | bytes 393224 | tf_op jit(solution)/shard_map/ppermute | solution.py:21
  86.8 10.4 %collective-permute-start.27 = (bf16[256,2048]{1,0:T(8,128)(2,1)S(1)}, bf16[256,2048]{1,0:T(8,128)(2,1)S(1)}, u32[]{:S(2)}, u32[]{:S(2)}) collective-permute-start(bf16[256,2048]{1,0:T(8,128)(2,1)S(1)} %collective-permute-done.26.refs_1_.refs_9_), channel_id=1, source_target_pairs={{0,1},{1,0},{2,3},{3,2},{4,5},{5,4},{6,7},{7,6},{8,9},{9,8},{10,11... | collective-permute-start | bytes 3145736 | tf_op jit(solution)/shard_map/ppermute | solution.py:21
  86.9 6.3 %collective-permute-start.20 = (bf16[32,2048]{1,0:T(8,128)(2,1)S(1)}, bf16[32,2048]{1,0:T(8,128)(2,1)S(1)}, u32[]{:S(2)}, u32[]{:S(2)}) collective-permute-start(bf16[32,2048]{1,0:T(8,128)(2,1)S(1)} %slice.204), channel_id=1, source_target_pairs={{0,2},{1,3},{2,0},{3,1},{4,6},{5,7},{6,4},{7,5},{8,10},{9,11},{10,... | collective-permute-start | bytes 393224 | tf_op jit(solution)/shard_map/ppermute | solution.py:21
  88.4 20.1 %collective-permute-start.24 = (bf16[128,2048]{1,0:T(8,128)(2,1)S(1)}, bf16[128,2048]{1,0:T(8,128)(2,1)S(1)}, u32[]{:S(2)}, u32[]{:S(2)}) collective-permute-start(bf16[128,2048]{1,0:T(8,128)(2,1)S(1)} %shard_map.234.refs_0_), channel_id=1, source_target_pairs={{0,16},{16,0},{1,17},{17,1},{2,18},{18,2},{3,19},{19,3},{4,20},{20... | collective-permute-start | bytes 1572872 | tf_op jit(solution)/shard_map/ppermute | solution.py:26
  89.9 18.6 %collective-permute-start.25 = (bf16[128,2048]{1,0:T(8,128)(2,1)S(1)}, bf16[128,2048]{1,0:T(8,128)(2,1)S(1)}, u32[]{:S(2)}, u32[]{:S(2)}) collective-permute-start(bf16[128,2048]{1,0:T(8,128)(2,1)S(1)} %shard_map.234.refs_0_), channel_id=1, source_target_pairs={{0,2},{1,3},{2,0},{3,1},{4,6},{5,7},{6,4},{7,5},{8,10},{9,11},{10,... | collective-permute-start | bytes 1572872 | tf_op jit(solution)/shard_map/ppermute | solution.py:21
  94.5 14.1 %collective-permute-start.21 = (bf16[32,2048]{1,0:T(8,128)(2,1)S(1)}, bf16[32,2048]{1,0:T(8,128)(2,1)S(1)}, u32[]{:S(2)}, u32[]{:S(2)}) collective-permute-start(bf16[32,2048]{1,0:T(8,128)(2,1)S(1)} %get-tuple-element.128.refs_0_), channel_id=1, source_target_pairs={{0,4},{4,0},{8,12},{12,8},{1,5},{5,1},{9,13},{13,9},{2,6},{6,2},{1... | collective-permute-start | bytes 393224 | tf_op jit(solution)/shard_map/ppermute | solution.py:21
  95.9 12.7 %collective-permute-start.22 = (bf16[32,2048]{1,0:T(8,128)(2,1)S(1)}, bf16[32,2048]{1,0:T(8,128)(2,1)S(1)}, u32[]{:S(2)}, u32[]{:S(2)}) collective-permute-start(bf16[32,2048]{1,0:T(8,128)(2,1)S(1)} %get-tuple-element.128.refs_0_), channel_id=1, source_target_pairs={{0,8},{4,12},{8,0},{12,4},{1,9},{5,13},{9,1},{13,5},{2,10},{6,14},... | collective-permute-start | bytes 393224 | tf_op jit(solution)/shard_map/ppermute | solution.py:21
  97.2 11.4 %collective-permute-start.23 = (bf16[32,2048]{1,0:T(8,128)(2,1)S(1)}, bf16[32,2048]{1,0:T(8,128)(2,1)S(1)}, u32[]{:S(2)}, u32[]{:S(2)}) collective-permute-start(bf16[32,2048]{1,0:T(8,128)(2,1)S(1)} %get-tuple-element.128.refs_0_), channel_id=1, source_target_pairs={{0,12},{4,8},{8,4},{12,0},{1,13},{5,9},{9,5},{13,1},{2,14},{6,10},... | collective-permute-start | bytes 393224 | tf_op jit(solution)/shard_map/ppermute | solution.py:21
  108.6 14.0 %collective-permute-start.28 = (bf16[32,2048]{1,0:T(8,128)(2,1)S(1)}, bf16[32,2048]{1,0:T(8,128)(2,1)S(1)}, u32[]{:S(2)}, u32[]{:S(2)}) collective-permute-start(bf16[32,2048]{1,0:T(8,128)(2,1)S(1)} %get-tuple-element.128.refs_0_), channel_id=1, source_target_pairs={{0,2},{1,3},{2,0},{3,1},{4,6},{5,7},{6,4},{7,5},{8,10},{9,11},{10,... | collective-permute-start | bytes 393224 | tf_op jit(solution)/shard_map/ppermute | solution.py:21
  109.4 13.2 %collective-permute-start.29 = (bf16[32,2048]{1,0:T(8,128)(2,1)S(1)}, bf16[32,2048]{1,0:T(8,128)(2,1)S(1)}, u32[]{:S(2)}, u32[]{:S(2)}) collective-permute-start(bf16[32,2048]{1,0:T(8,128)(2,1)S(1)} %collective-permute-done.21.refs_4_), channel_id=1, source_target_pairs={{0,2},{1,3},{2,0},{3,1},{4,6},{5,7},{6,4},{7,5},{8,10},{9,11},{10,... | collective-permute-start | bytes 393224 | tf_op jit(solution)/shard_map/ppermute | solution.py:21
  110.7 12.0 %collective-permute-start.30 = (bf16[32,2048]{1,0:T(8,128)(2,1)S(1)}, bf16[32,2048]{1,0:T(8,128)(2,1)S(1)}, u32[]{:S(2)}, u32[]{:S(2)}) collective-permute-start(bf16[32,2048]{1,0:T(8,128)(2,1)S(1)} %collective-permute-done.22.refs_8_), channel_id=1, source_target_pairs={{0,2},{1,3},{2,0},{3,1},{4,6},{5,7},{6,4},{7,5},{8,10},{9,11},{10,... | collective-permute-start | bytes 393224 | tf_op jit(solution)/shard_map/ppermute | solution.py:21
  111.5 11.3 %collective-permute-start.31 = (bf16[32,2048]{1,0:T(8,128)(2,1)S(1)}, bf16[32,2048]{1,0:T(8,128)(2,1)S(1)}, u32[]{:S(2)}, u32[]{:S(2)}) collective-permute-start(bf16[32,2048]{1,0:T(8,128)(2,1)S(1)} %collective-permute-done.23.refs_12_), channel_id=1, source_target_pairs={{0,2},{1,3},{2,0},{3,1},{4,6},{5,7},{6,4},{7,5},{8,10},{9,11},{10,... | collective-permute-start | bytes 393224 | tf_op jit(solution)/shard_map/ppermute | solution.py:21
  125.0 19.4 %collective-permute-start.42 = (bf16[128,2048]{1,0:T(8,128)(2,1)S(1)}, bf16[128,2048]{1,0:T(8,128)(2,1)}, u32[]{:S(2)}, u32[]{:S(2)}) collective-permute-start(bf16[128,2048]{1,0:T(8,128)(2,1)S(1)} %collective-permute-done.24.refs_2_), channel_id=1, source_target_pairs={{0,2},{1,3},{2,0},{3,1},{4,6},{5,7},{6,4},{7,5},{8,10},{9,11},{10,... | collective-permute-start | bytes 1572872 | tf_op jit(solution)/shard_map/ppermute | solution.py:21
  143.8 4.4 %collective-permute-start.45 = (bf16[128,2048]{1,0:T(8,128)(2,1)S(1)}, bf16[128,2048]{1,0:T(8,128)(2,1)S(1)}, u32[]{:S(2)}, u32[]{:S(2)}) collective-permute-start(bf16[128,2048]{1,0:T(8,128)(2,1)S(1)} %collective-permute-done.24.refs_2_), channel_id=1, source_target_pairs={{0,1},{1,0},{2,3},{3,2},{4,5},{5,4},{6,7},{7,6},{8,9},{9,8},{10,11... | collective-permute-start | bytes 1572872 | tf_op jit(solution)/shard_map/ppermute | solution.py:21
  144.0 4.2 %collective-permute-start.44 = (bf16[128,2048]{1,0:T(8,128)(2,1)S(1)}, bf16[128,2048]{1,0:T(8,128)(2,1)S(1)}, u32[]{:S(2)}, u32[]{:S(2)}) collective-permute-start(bf16[128,2048]{1,0:T(8,128)(2,1)S(1)} %collective-permute-done.25.refs_1_), channel_id=1, source_target_pairs={{0,1},{1,0},{2,3},{3,2},{4,5},{5,4},{6,7},{7,6},{8,9},{9,8},{10,11... | collective-permute-start | bytes 1572872 | tf_op jit(solution)/shard_map/ppermute | solution.py:21
  144.3 34.8 %collective-permute-start.49 = (bf16[4,256,512]{2,1,0:T(8,128)(2,1)}, bf16[4,256,512]{2,1,0:T(8,128)(2,1)S(1)}, u32[]{:S(2)}, u32[]{:S(2)}) collective-permute-start(bf16[4,256,512]{2,1,0:T(8,128)(2,1)} %bitcast.46), channel_id=1, source_target_pairs={{0,16},{16,0},{1,17},{17,1},{2,18},{18,2},{3,19},{19,3},{4,20},{20... | collective-permute-start | bytes 3145736 | tf_op jit(solution)/shard_map/ppermute | solution.py:26
  147.1 30.4 %collective-permute-start.41 = (bf16[32,4096]{1,0:T(8,128)(2,1)S(1)}, bf16[32,4096]{1,0:T(8,128)(2,1)S(1)}, u32[]{:S(2)}, u32[]{:S(2)}) collective-permute-start(bf16[32,4096]{1,0:T(8,128)(2,1)S(1)} %slice.203), channel_id=1, source_target_pairs={{0,2},{1,3},{2,0},{3,1},{4,6},{5,7},{6,4},{7,5},{8,10},{9,11},{10,... | collective-permute-start | bytes 786440 | tf_op jit(solution)/shard_map/ppermute | solution.py:21
  178.0 8.5 %collective-permute-start.47 = (bf16[32,4096]{1,0:T(8,128)(2,1)S(1)}, bf16[32,4096]{1,0:T(8,128)(2,1)S(1)}, u32[]{:S(2)}, u32[]{:S(2)}) collective-permute-start(bf16[32,4096]{1,0:T(8,128)(2,1)S(1)} %get-tuple-element.202), channel_id=1, source_target_pairs={{0,2},{1,3},{2,0},{3,1},{4,6},{5,7},{6,4},{7,5},{8,10},{9,11},{10,... | collective-permute-start | bytes 786440 | tf_op jit(solution)/shard_map/ppermute | solution.py:21
  181.9 4.7 %collective-permute-start.50 = (f32[2,256]{1,0:T(2,128)S(1)}, f32[2,256]{1,0:T(2,128)S(1)}, u32[]{:S(2)}, u32[]{:S(2)}) collective-permute-start(f32[2,256]{1,0:T(2,128)S(1)} %pad_maximum_fusion.4), channel_id=1, source_target_pairs={{0,2},{1,3},{2,0},{3,1},{4,6},{5,7},{6,4},{7,5},{8,10},{9,11},{10,... | collective-permute-start | bytes 6152 | tf_op jit(solution)/shard_map/ppermute | solution.py:21
  (69 other events, 429.4 us)
Sparse Core Ops, SparseCore 0:
  16.1 43.9 all-gather.1

commit v7 on v6

--- a/solution.py
+++ b/solution.py
@@ -456,14 +456,23 @@
 
 
 def mlp_kernel(
-    block, x_ref, hb_ref, wg_ref, wu_ref, hidden_ref, gate_ref, up_ref, back_ref
+    block, x_ref, hb_ref, wg_ref, up_hbm, hidden_ref, gate_ref, up_ref, back_ref, wu_ref, sem
 ):
+    tiles = [slice(i * block, (i + 1) * block) for i in range(wg_ref.shape[1] // block)]
+    copies = [
+        pltpu.make_async_copy(up_hbm.at[:, at], wu_ref.at[:, at], sem.at[i])
+        for i, at in enumerate(tiles)
+    ]
+    for copy in copies:
+        copy.start()
     x, total = x_ref[...], None
-    for i in range(wg_ref.shape[1] // block):
-        at = slice(i * block, (i + 1) * block)
-        wg, wu = wg_ref[:, at], wu_ref[:, at]
+    for copy, at in zip(copies, tiles, strict=True):
+        wg = wg_ref[:, at]
+        gate = dot(x, wg)
+        copy.wait()
+        wu = wu_ref[:, at]
         hidden_ref[:, at], gate_back, up_back = gate_math(
-            dot(x, wg), dot(x, wu), hb_ref[:, at].astype(F32)
+            gate, dot(x, wu), hb_ref[:, at].astype(F32)
         )
         gate_ref[:, at] = gate_back
         up_ref[:, at] = up_back
@@ -475,18 +484,20 @@
 def mlp(x, hidden_back, wg, wu):
     rows, width = x.shape
     units = wg.shape[1]
+    block = min(512, units)
     return pl.pallas_call(
-        functools.partial(mlp_kernel, min(512, units)),
-        in_specs=[VMEM_WHOLE] * 4,
+        functools.partial(mlp_kernel, block),
+        in_specs=[VMEM_WHOLE] * 3 + [HBM_WHOLE],
         out_specs=[VMEM_WHOLE] * 4,
         out_shape=[
             *[jax.ShapeDtypeStruct((rows, units), BF)] * 3, jax.ShapeDtypeStruct((rows, width), BF)
         ],
-        compiler_params=pltpu.CompilerParams(vmem_limit_bytes=20 * MIB),
-        cost_estimate=pl.CostEstimate(
-            flops=0, bytes_accessed=0, transcendentals=0
-        ),
-    )(x, hidden_back, in_vmem(wg), in_vmem(wu))
+        scratch_shapes=[
+            pltpu.VMEM(wu.shape, wu.dtype), pltpu.SemaphoreType.DMA((units // block,))
+        ],
+        compiler_params=pltpu.CompilerParams(vmem_limit_bytes=28 * MIB),
+        cost_estimate=pl.CostEstimate(flops=0, bytes_accessed=0, transcendentals=0),
+    )(x, hidden_back, in_vmem(wg), in_hbm(wu))
 
 
 def tiles_of(sources, at_ref, first, tile):
@@ -824,10 +835,10 @@
     size = length // 2
     cot_half = lax.dynamic_slice_in_dim(cot_own, half * size, size, 0)
     cot_far = [turn(cot_half, "dp", step) for step in range(1, n_dp)]
-    gate, up = fetch(after(gate_weight, normed_chunk), up_weight)
-    normed_second = gather_tensor(normed_chunk, (gate, up))
+    (gate,) = fetch(after(gate_weight, normed_chunk))
+    normed_second = gather_tensor(normed_chunk, gate)
     chunk_rings = ring_of(normed_chunk)
-    hidden, gate_back, up_back, second_part = mlp(normed_second, hidden_back, gate, up)
+    hidden, gate_back, up_back, second_part = mlp(normed_second, hidden_back, gate, up_weight)
     second_part, chunk_rings = lax.optimization_barrier((second_part, chunk_rings))
     x_near = [join(chunk_rings)]
     x_far = over_dp(x_near)

time: 198 us -> 198 us (level)
    ppermute x3, waiting for transfers between devices: 2.08 us -> 4.51 us  [turn(): lax.ppermute(values, axis, [(i, (i + shift) % count) for i in range(count)])]
    pallas_call x1, Pallas kernels: 5.78 us -> 3.39 us  [fetch(): pl.pallas_call(functools.partial(fetch_kernel, len(weights)), in_specs=[H...]
    ppermute x49, waiting for transfers between devices: 19.3 us -> 17.1 us  [swap(): return lax.ppermute(values, axis, [(i, i ^ distance) for i in range(count)])]
    pallas_call x1, Pallas kernels: 8.03 us -> 10.1 us  [mlp(): pl.pallas_call(functools.partial(mlp_kernel, block), in_specs=[VMEM_WHOLE...]
  transfers between devices with their start and end apart: 53 -> 53, of which waited for: 15 -> 14; matrix products, arithmetic and copies ran while one was open for 8% -> 8% of each run, Pallas kernels for 48% -> 48%
where the time goes in v7:
time: 198 us; the launch traced here: 197 us
  Pallas kernels  97.2 us (49%)
  starting transfers between devices  42.3 us (21%)
  waiting for transfers between devices  21.6 us (11%)
  between operations  17.5 us (9%)
  local copies, waits for them, and re-layouts  10.1 us (5%)
  other arithmetic  6.96 us (4%)
    ppermute x49, starting transfers between devices, swap(): return lax.ppermute(values, axis, [(i, i ^ distance) for i in range(count)])  37.7 us
    pallas_call x1, Pallas kernels, mlp_grad(): pl.pallas_call(functools.partial(mlp_grad_kernel, len(pieces), chunk, len...  28.1 us
    pallas_call x2, Pallas kernels, hidden_back_of(): pl.pallas_call(functools.partial(hidden_back_kernel, tile, len(before) >...  19.5 us
    ppermute x49, waiting for transfers between devices, swap(): return lax.ppermute(values, axis, [(i, i ^ distance) for i in range(count)])  17.1 us
    pallas_call x1, Pallas kernels, attend_back(): pl.pallas_call(functools.partial(attend_back_kernel, chunk, slots, scale,...  16.4 us
    pallas_call x1, Pallas kernels, attend(): pl.pallas_call(functools.partial(attend_kernel, chunk, slots, scale, shif...  10.1 us
    pallas_call x1, Pallas kernels, mlp(): pl.pallas_call(functools.partial(mlp_kernel, block), in_specs=[VMEM_WHOLE...  10.1 us
    pallas_call x1, Pallas kernels, own_hidden_back(): pl.pallas_call(own_hidden_back_kernel, grid=(units // block,), in_specs=[...  5.92 us
  transfers between devices with their start and end apart: 53, of which 14 were waited for; matrix products, arithmetic and copies ran while one was open for 8% of the time, Pallas kernels for 48%

profile of v7, /device:TPU:0, one launch (start us, length us, event | category | flops | bytes accessed | tf_op | source)
XLA Modules:
  0.0 197.1 jit_solution(17838710978980073634)
XLA Ops:
  7.3 2.9 %shard_map.229 = (bf16[128,2048]{1,0:T(8,128)(2,1)S(1)}, bf16[32,2048]{1,0:T(8,128)(2,1)S(1)}, bf16[128,2048]{1,0:T(8,128)(2,1)S(1)}, bf16[32,2048]{1,0:T(8,128)...) custom-call(s32[4]{0:T(128)S(1)} %get-tuple-element.187.at_ref, ...), custom_call_target="tpu_custom_call" | custom-call | flops 2097152 | bytes 2097152 | tf_op jit(solution)/shard_map/pallas_call | solution.py:198
  10.2 3.1 %collective-permute-start = (bf16[32,2048]{1,0:T(8,128)(2,1)S(1)}, bf16[32,2048]{1,0:T(8,128)(2,1)S(1)}, u32[]{:S(2)}, u32[]{:S(2)}) collective-permute-start(bf16[32,2048]{1,0:T(8,128)(2,1)S(1)} %get-tuple-element.85), channel_id=1, source_target_pairs={{0,4},{4,0},{8,12},{12,8},{1,5},{5,1},{9,13},{13,9},{2,6},{6,2},{1... | collective-permute-start | bytes 393224 | tf_op jit(solution)/shard_map/ppermute | solution.py:21
  13.3 2.6 %collective-permute-start.2 = (bf16[32,2048]{1,0:T(8,128)(2,1)S(1)}, bf16[32,2048]{1,0:T(8,128)(2,1)S(1)}, u32[]{:S(2)}, u32[]{:S(2)}) collective-permute-start(bf16[32,2048]{1,0:T(8,128)(2,1)S(1)} %get-tuple-element.85), channel_id=1, source_target_pairs={{0,8},{4,12},{8,0},{12,4},{1,9},{5,13},{9,1},{13,5},{2,10},{6,14},... | collective-permute-start | bytes 393224 | tf_op jit(solution)/shard_map/ppermute | solution.py:21
  21.2 5.1 %collective-permute-done.2.refs_8_ = bf16[32,2048]{1,0:T(8,128)(2,1)S(1)} collective-permute-done((bf16[32,2048]{1,0:T(8,128)(2,1)S(1)}, bf16[32,2048]{1,0:T(8,128)(2,1)S(1)}, u32[]{:S(2)}, u32[]{:S(2)}) %collective-permute-start.2) | collective-permute-done | bytes 131104 | tf_op jit(solution)/shard_map/ppermute | solution.py:21
  26.3 1.6 collective-permute-start.1
  28.3 1.5 collective-permute-start.5
  29.8 5.9 %shard_map.230.hb_ref = bf16[128,2048]{1,0:T(8,128)(2,1)S(1)} custom-call(bf16[128,2048]{1,0:T(8,128)(2,1)S(1)} %get-tuple-element.90.rows_ref, bf16[2048,2048]{1,0:T(8,128)(2,1)} %refs_3_.3), custom_call_target="tpu_custom_call" | custom-call | flops 1073741824 | bytes 8388608 | tf_op jit(solution)/shard_map/pallas_call | solution.py:521
  39.4 10.1 %shard_map.231 = (bf16[512,512]{1,0:T(8,128)(2,1)}, bf16[512,512]{1,0:T(8,128)(2,1)}, bf16[512,512]{1,0:T(8,128)(2,1)}, bf16[128,512]{1,0:T(8,128)(2,1)}, f32[4,...) custom-call(s32[16]{0:T(128)} %concatenate.19.at_ref, bf16[32,2048]{1,0:T(8,128)(2,1)} %get-tuple-element.197.refs_0_, ...), custom_call_target="tpu_custom_call" | custom-call | flops 3221225472 | bytes 6291456 | tf_op jit(solution)/shard_map/pallas_call | solution.py:275
  49.5 1.4 convolution_convert_fusion
  52.7 1.5 collective-permute-start.13
  55.1 3.3 %collective-permute-done.13 = bf16[32,2048]{1,0:T(8,128)(2,1)S(1)} collective-permute-done((bf16[32,2048]{1,0:T(8,128)(2,1)S(1)}, bf16[32,2048]{1,0:T(8,128)(2,1)S(1)}, u32[]{:S(2)}, u32[]{:S(2)}) %collective-permute-start.13) | collective-permute-done | bytes 131104 | tf_op jit(solution)/shard_map/ppermute | solution.py:21
  58.6 1.5 collective-permute-start.14
  60.1 1.3 constant_dynamic-slice_fusion
  61.5 1.6 collective-permute-start.26
  63.1 3.4 %shard_map.232.wg_ref = bf16[2048,2048]{1,0:T(8,128)(2,1)S(1)} custom-call(bf16[2048,2048]{1,0:T(8,128)(2,1)} %refs_15_.1), custom_call_target="tpu_custom_call" | custom-call | tf_op jit(solution)/shard_map/pallas_call | solution.py:144
  66.6 2.7 %collective-permute-start.16 = (bf16[32,2048]{1,0:T(8,128)(2,1)S(1)}, bf16[32,2048]{1,0:T(8,128)(2,1)S(1)}, u32[]{:S(2)}, u32[]{:S(2)}) collective-permute-start(bf16[32,2048]{1,0:T(8,128)(2,1)S(1)} %multiply_convert_fusion.refs_0_), channel_id=1, source_target_pairs={{0,4},{4,0},{8,12},{12,8},{1,5},{5,1},{9,13},{13,9},{2,6},{6,2},{1... | collective-permute-start | bytes 393224 | tf_op jit(solution)/shard_map/ppermute | solution.py:21
  70.3 1.4 collective-permute-start.18
  71.8 10.1 %shard_map.233 = (bf16[128,2048]{1,0:T(8,128)(2,1)S(1)}, bf16[128,2048]{1,0:T(8,128)(2,1)S(1)}, bf16[128,2048]{1,0:T(8,128)(2,1)S(1)}, bf16[128,2048]{1,0:T(8,128)(2,1)S(1)}) custom-call(bf16[128,2048]{1,0:T(8,128)(2,1)S(1)} %pad_maximum_fusion.x_ref, bf16[128,2048]{1,0:T(8,128)(2,1)S(1)} %shard_map.230.hb_ref, bf16[2048,2048]{1,0:T(8,128)(2,1)S(1)} %shard_map.232.wg_ref, ...), custom_call_target="tpu_custom_call" | custom-call | tf_op jit(solution)/shard_map/pallas_call | solution.py:488
  82.3 4.5 %collective-permute-done.26.refs_1_.refs_9_ = bf16[256,2048]{1,0:T(8,128)(2,1)S(1)} collective-permute-done((bf16[256,2048]{1,0:T(8,128)(2,1)S(1)}, bf16[256,2048]{1,0:T(8,128)(2,1)S(1)}, u32[]{:S(2)}, u32[]{:S(2)}) %collective-permute-start.26) | collective-permute-done | bytes 1048608 | tf_op jit(solution)/shard_map/ppermute | solution.py:26
  88.4 1.5 collective-permute-start.24
  89.9 1.5 collective-permute-start.25
  91.4 1.9 collective-permute-done.20
  95.8 1.4 collective-permute-start.22
  97.2 1.8 collective-permute-start.23
  99.0 9.6 %shard_map.235 = (bf16[1024,2048]{1,0:T(8,128)(2,1)}, f32[128,2048]{1,0:T(8,128)}) custom-call(s32[4]{0:T(128)} %copy-done.25, bf16[512,2048]{1,0:T(8,128)(2,1)} %all-gather.2.cloned.1.call-done.refs_0_.refs_8_, bf16[256,2048]{1,0:T(8,128)(2,1)} %copy-done.6, bf16[256,2048]{1,0:T(8,128)(2,1)} %copy-done.7, bf16[2048,2048]{1,0:T(8,128)(2,1)} %refs_3_.3, ...), custom_call_target="tpu_custom_call" | custom-call | flops 4294967296 | bytes 12582912 | tf_op jit(solution)/shard_map/pallas_call | solution.py:587
  112.9 9.9 %shard_map.236 = (bf16[1024,2048]{1,0:T(8,128)(2,1)}, bf16[128,2048]{1,0:T(8,128)(2,1)}) custom-call(s32[4]{0:T(128)} %copy-done.25, bf16[512,2048]{1,0:T(8,128)(2,1)} %all-gather.2.cloned.1.call-done.refs_0_.refs_8_, bf16[256,2048]{1,0:T(8,128)(2,1)} %copy-done.6, bf16[256,2048]{1,0:T(8,128)(2,1)} %copy-done.7, ...), custom_call_target="tpu_custom_call", output_to_operand_aliasing={{0}: (7, {})} | custom-call | flops 4294967296 | bytes 12582912 | tf_op jit(solution)/shard_map/pallas_call | solution.py:587
  126.9 16.4 %shard_map.237 = (f32[4,256,512]{2,1,0:T(8,128)}, bf16[1,4,256,512]{3,2,1,0:T(8,128)(2,1)}, bf16[64,4096]{1,0:T(8,128)(2,1)}, bf16[64,4096]{1,0:T(8,128)(2,1)}) custom-call(s32[16]{0:T(128)} %concatenate.19.at_ref, s32[2]{0:T(128)} %add_multiply_fusion.starts_ref, bf16[32,2048]{1,0:T(8,128)(2,1)} %copy-done.8, bf16[32,2048]{1,0:T(8,128)(2,1)} %copy-done.13, ...), custom_call_target="tpu_custom_call" | custom-call | flops 2952790016 | bytes 9437184 | tf_op jit(solution)/shard_map/pallas_call | solution.py:417
  144.4 1.5 collective-permute-start.49
  149.3 28.1 %shard_map.238 = (f32[256,2048]{1,0:T(8,128)}, f32[256,2048]{1,0:T(8,128)}, f32[2048,256]{1,0:T(8,128)}, f32[1,256]{1,0:T(1,128)}) custom-call(s32[41]{0:T(128)} %concatenate.20.at_ref, bf16[128,2048]{1,0:T(8,128)(2,1)} %copy-done, bf16[128,2048]{1,0:T(8,128)(2,1)} %copy-done.31, bf16[128,2048]{1,0:T(8,128)(2,1)} %copy-done.30, ...), custom_call_target="tpu_custom_call" | custom-call | flops 20401094656 | bytes 25165824 | tf_op jit(solution)/shard_map/pallas_call | solution.py:718
  179.4 2.4 %add_reduce_fusion = (f32[256]{0:T(256)S(1)}, f32[256,512]{1,0:T(8,128)}, f32[256,512]{1,0:T(8,128)}, f32[256,512]{1,0:T(8,128)}) fusion(bf16[2048,512]{1,0:T(8,128)(2,1)} %refs_27_.1, s32[]{:T(128)S(6)} %select_n.82, bf16[2048,512]{1,0:T(8,128)(2,1)} %refs_26_.1, bf16[2048,512]{1,0:T(8,128)(2,1)} %refs_25_.1, f32[4,256,512]{2,1,0:T(8,128)S(1)} %convert_add_fusion), kind=kLoop, calls=%fused_computation.13 | loop fusion | flops 1179392 | bytes 3933188 | tf_op jit(solution)/shard_map/reduce_sum | solution.py:893
  184.0 2.5 %collective-permute-done.47 = bf16[32,4096]{1,0:T(8,128)(2,1)S(1)} collective-permute-done((bf16[32,4096]{1,0:T(8,128)(2,1)S(1)}, bf16[32,4096]{1,0:T(8,128)(2,1)S(1)}, u32[]{:S(2)}, u32[]{:S(2)}) %collective-permute-start.47) | collective-permute-done | bytes 262176 | tf_op jit(solution)/shard_map/ppermute | solution.py:21
  187.2 1.3 collective-permute-done.51
  (237 shorter events, 34.4 us)
Async XLA Ops:
  7.2 53.0 %all-gather.2.cloned.1.call-start = ((), (), s32[]{:S(2)}) async-start(), calls=%async_computation | async-start | bytes 2228224 | tf_op jit(solution)/shard_map/all_gather | solution.py:778
  10.2 10.9 %collective-permute-start = (bf16[32,2048]{1,0:T(8,128)(2,1)S(1)}, bf16[32,2048]{1,0:T(8,128)(2,1)S(1)}, u32[]{:S(2)}, u32[]{:S(2)}) collective-permute-start(bf16[32,2048]{1,0:T(8,128)(2,1)S(1)} %get-tuple-element.85), channel_id=1, source_target_pairs={{0,4},{4,0},{8,12},{12,8},{1,5},{5,1},{9,13},{13,9},{2,6},{6,2},{1... | collective-permute-start | bytes 393224 | tf_op jit(solution)/shard_map/ppermute | solution.py:21
  13.3 12.9 %collective-permute-start.2 = (bf16[32,2048]{1,0:T(8,128)(2,1)S(1)}, bf16[32,2048]{1,0:T(8,128)(2,1)S(1)}, u32[]{:S(2)}, u32[]{:S(2)}) collective-permute-start(bf16[32,2048]{1,0:T(8,128)(2,1)S(1)} %get-tuple-element.85), channel_id=1, source_target_pairs={{0,8},{4,12},{8,0},{12,4},{1,9},{5,13},{9,1},{13,5},{2,10},{6,14},... | collective-permute-start | bytes 393224 | tf_op jit(solution)/shard_map/ppermute | solution.py:21
  15.9 10.3 %collective-permute-start.4 = (bf16[32,2048]{1,0:T(8,128)(2,1)S(1)}, bf16[32,2048]{1,0:T(8,128)(2,1)S(1)}, u32[]{:S(2)}, u32[]{:S(2)}) collective-permute-start(bf16[32,2048]{1,0:T(8,128)(2,1)S(1)} %get-tuple-element.85), channel_id=1, source_target_pairs={{0,12},{4,8},{8,4},{12,0},{1,13},{5,9},{9,5},{13,1},{2,14},{6,10},... | collective-permute-start | bytes 393224 | tf_op jit(solution)/shard_map/ppermute | solution.py:21
  26.3 9.5 %collective-permute-start.1 = (bf16[32,2048]{1,0:T(8,128)(2,1)S(1)}, bf16[32,2048]{1,0:T(8,128)(2,1)S(1)}, u32[]{:S(2)}, u32[]{:S(2)}) collective-permute-start(bf16[32,2048]{1,0:T(8,128)(2,1)S(1)} %collective-permute-done.refs_4_), channel_id=1, source_target_pairs={{0,2},{1,3},{2,0},{3,1},{4,6},{5,7},{6,4},{7,5},{8,10},{9,11},{10,... | collective-permute-start | bytes 393224 | tf_op jit(solution)/shard_map/ppermute | solution.py:21
  27.8 8.0 %collective-permute-start.3 = (bf16[32,2048]{1,0:T(8,128)(2,1)S(1)}, bf16[32,2048]{1,0:T(8,128)(2,1)S(1)}, u32[]{:S(2)}, u32[]{:S(2)}) collective-permute-start(bf16[32,2048]{1,0:T(8,128)(2,1)S(1)} %collective-permute-done.2.refs_8_), channel_id=1, source_target_pairs={{0,2},{1,3},{2,0},{3,1},{4,6},{5,7},{6,4},{7,5},{8,10},{9,11},{10,... | collective-permute-start | bytes 393224 | tf_op jit(solution)/shard_map/ppermute | solution.py:21
  28.3 7.7 %collective-permute-start.5 = (bf16[32,2048]{1,0:T(8,128)(2,1)S(1)}, bf16[32,2048]{1,0:T(8,128)(2,1)S(1)}, u32[]{:S(2)}, u32[]{:S(2)}) collective-permute-start(bf16[32,2048]{1,0:T(8,128)(2,1)S(1)} %collective-permute-done.4.refs_12_), channel_id=1, source_target_pairs={{0,2},{1,3},{2,0},{3,1},{4,6},{5,7},{6,4},{7,5},{8,10},{9,11},{10,... | collective-permute-start | bytes 393224 | tf_op jit(solution)/shard_map/ppermute | solution.py:21
  52.7 5.6 %collective-permute-start.13 = (bf16[32,2048]{1,0:T(8,128)(2,1)S(1)}, bf16[32,2048]{1,0:T(8,128)(2,1)S(1)}, u32[]{:S(2)}, u32[]{:S(2)}) collective-permute-start(bf16[32,2048]{1,0:T(8,128)(2,1)S(1)} %slice.205), channel_id=1, source_target_pairs={{0,2},{1,3},{2,0},{3,1},{4,6},{5,7},{6,4},{7,5},{8,10},{9,11},{10,... | collective-permute-start | bytes 393224 | tf_op jit(solution)/shard_map/ppermute | solution.py:21
  58.6 7.8 %collective-permute-start.14 = (bf16[32,2048]{1,0:T(8,128)(2,1)S(1)}, bf16[32,2048]{1,0:T(8,128)(2,1)S(1)}, u32[]{:S(2)}, u32[]{:S(2)}) collective-permute-start(bf16[32,2048]{1,0:T(8,128)(2,1)S(1)} %multiply_convert_fusion.refs_0_), channel_id=1, source_target_pairs={{0,2},{1,3},{2,0},{3,1},{4,6},{5,7},{6,4},{7,5},{8,10},{9,11},{10,... | collective-permute-start | bytes 393224 | tf_op jit(solution)/shard_map/ppermute | solution.py:21
  61.5 25.3 %collective-permute-start.26 = (bf16[256,2048]{1,0:T(8,128)(2,1)S(1)}, bf16[256,2048]{1,0:T(8,128)(2,1)S(1)}, u32[]{:S(2)}, u32[]{:S(2)}) collective-permute-start(bf16[256,2048]{1,0:T(8,128)(2,1)S(1)} %constant_dynamic-slice_fusion), channel_id=1, source_target_pairs={{0,16},{16,0},{1,17},{17,1},{2,18},{18,2},{3,19},{19,3},{4,20},{20... | collective-permute-start | bytes 3145736 | tf_op jit(solution)/shard_map/ppermute | solution.py:26
  66.5 5.2 %collective-permute-start.15 = (bf16[64,2048]{1,0:T(8,128)(2,1)S(1)}, bf16[64,2048]{1,0:T(8,128)(2,1)S(1)}, u32[]{:S(2)}, u32[]{:S(2)}) collective-permute-start(bf16[64,2048]{1,0:T(8,128)(2,1)S(1)} %pad_maximum_fusion.2), channel_id=1, source_target_pairs={{0,1},{1,0},{2,3},{3,2},{4,5},{5,4},{6,7},{7,6},{8,9},{9,8},{10,11... | collective-permute-start | bytes 786440 | tf_op jit(solution)/shard_map/ppermute | solution.py:21
  66.6 15.3 %collective-permute-start.16 = (bf16[32,2048]{1,0:T(8,128)(2,1)S(1)}, bf16[32,2048]{1,0:T(8,128)(2,1)S(1)}, u32[]{:S(2)}, u32[]{:S(2)}) collective-permute-start(bf16[32,2048]{1,0:T(8,128)(2,1)S(1)} %multiply_convert_fusion.refs_0_), channel_id=1, source_target_pairs={{0,4},{4,0},{8,12},{12,8},{1,5},{5,1},{9,13},{13,9},{2,6},{6,2},{1... | collective-permute-start | bytes 393224 | tf_op jit(solution)/shard_map/ppermute | solution.py:21
  69.3 12.9 %collective-permute-start.17 = (bf16[32,2048]{1,0:T(8,128)(2,1)S(1)}, bf16[32,2048]{1,0:T(8,128)(2,1)S(1)}, u32[]{:S(2)}, u32[]{:S(2)}) collective-permute-start(bf16[32,2048]{1,0:T(8,128)(2,1)S(1)} %multiply_convert_fusion.refs_0_), channel_id=1, source_target_pairs={{0,8},{4,12},{8,0},{12,4},{1,9},{5,13},{9,1},{13,5},{2,10},{6,14},... | collective-permute-start | bytes 393224 | tf_op jit(solution)/shard_map/ppermute | solution.py:21
  70.3 11.9 %collective-permute-start.18 = (bf16[32,2048]{1,0:T(8,128)(2,1)S(1)}, bf16[32,2048]{1,0:T(8,128)(2,1)S(1)}, u32[]{:S(2)}, u32[]{:S(2)}) collective-permute-start(bf16[32,2048]{1,0:T(8,128)(2,1)S(1)} %multiply_convert_fusion.refs_0_), channel_id=1, source_target_pairs={{0,12},{4,8},{8,4},{12,0},{1,13},{5,9},{9,5},{13,1},{2,14},{6,10},... | collective-permute-start | bytes 393224 | tf_op jit(solution)/shard_map/ppermute | solution.py:21
  82.2 4.6 %collective-permute-start.19 = (bf16[64,2048]{1,0:T(8,128)(2,1)S(1)}, bf16[64,2048]{1,0:T(8,128)(2,1)S(1)}, u32[]{:S(2)}, u32[]{:S(2)}) collective-permute-start(bf16[64,2048]{1,0:T(8,128)(2,1)S(1)} %slice.134), channel_id=1, source_target_pairs={{0,1},{1,0},{2,3},{3,2},{4,5},{5,4},{6,7},{7,6},{8,9},{9,8},{10,11... | collective-permute-start | bytes 786440 | tf_op jit(solution)/shard_map/ppermute | solution.py:21
  86.8 10.4 %collective-permute-start.27 = (bf16[256,2048]{1,0:T(8,128)(2,1)S(1)}, bf16[256,2048]{1,0:T(8,128)(2,1)S(1)}, u32[]{:S(2)}, u32[]{:S(2)}) collective-permute-start(bf16[256,2048]{1,0:T(8,128)(2,1)S(1)} %collective-permute-done.26.refs_1_.refs_9_), channel_id=1, source_target_pairs={{0,1},{1,0},{2,3},{3,2},{4,5},{5,4},{6,7},{7,6},{8,9},{9,8},{10,11... | collective-permute-start | bytes 3145736 | tf_op jit(solution)/shard_map/ppermute | solution.py:21
  86.9 6.4 %collective-permute-start.20 = (bf16[32,2048]{1,0:T(8,128)(2,1)S(1)}, bf16[32,2048]{1,0:T(8,128)(2,1)S(1)}, u32[]{:S(2)}, u32[]{:S(2)}) collective-permute-start(bf16[32,2048]{1,0:T(8,128)(2,1)S(1)} %slice.204), channel_id=1, source_target_pairs={{0,2},{1,3},{2,0},{3,1},{4,6},{5,7},{6,4},{7,5},{8,10},{9,11},{10,... | collective-permute-start | bytes 393224 | tf_op jit(solution)/shard_map/ppermute | solution.py:21
  88.4 20.2 %collective-permute-start.24 = (bf16[128,2048]{1,0:T(8,128)(2,1)S(1)}, bf16[128,2048]{1,0:T(8,128)(2,1)S(1)}, u32[]{:S(2)}, u32[]{:S(2)}) collective-permute-start(bf16[128,2048]{1,0:T(8,128)(2,1)S(1)} %shard_map.234.refs_0_), channel_id=1, source_target_pairs={{0,16},{16,0},{1,17},{17,1},{2,18},{18,2},{3,19},{19,3},{4,20},{20... | collective-permute-start | bytes 1572872 | tf_op jit(solution)/shard_map/ppermute | solution.py:26
  89.9 18.7 %collective-permute-start.25 = (bf16[128,2048]{1,0:T(8,128)(2,1)S(1)}, bf16[128,2048]{1,0:T(8,128)(2,1)S(1)}, u32[]{:S(2)}, u32[]{:S(2)}) collective-permute-start(bf16[128,2048]{1,0:T(8,128)(2,1)S(1)} %shard_map.234.refs_0_), channel_id=1, source_target_pairs={{0,2},{1,3},{2,0},{3,1},{4,6},{5,7},{6,4},{7,5},{8,10},{9,11},{10,... | collective-permute-start | bytes 1572872 | tf_op jit(solution)/shard_map/ppermute | solution.py:21
  94.6 14.1 %collective-permute-start.21 = (bf16[32,2048]{1,0:T(8,128)(2,1)S(1)}, bf16[32,2048]{1,0:T(8,128)(2,1)S(1)}, u32[]{:S(2)}, u32[]{:S(2)}) collective-permute-start(bf16[32,2048]{1,0:T(8,128)(2,1)S(1)} %get-tuple-element.124.refs_0_), channel_id=1, source_target_pairs={{0,4},{4,0},{8,12},{12,8},{1,5},{5,1},{9,13},{13,9},{2,6},{6,2},{1... | collective-permute-start | bytes 393224 | tf_op jit(solution)/shard_map/ppermute | solution.py:21
  95.8 12.9 %collective-permute-start.22 = (bf16[32,2048]{1,0:T(8,128)(2,1)S(1)}, bf16[32,2048]{1,0:T(8,128)(2,1)S(1)}, u32[]{:S(2)}, u32[]{:S(2)}) collective-permute-start(bf16[32,2048]{1,0:T(8,128)(2,1)S(1)} %get-tuple-element.124.refs_0_), channel_id=1, source_target_pairs={{0,8},{4,12},{8,0},{12,4},{1,9},{5,13},{9,1},{13,5},{2,10},{6,14},... | collective-permute-start | bytes 393224 | tf_op jit(solution)/shard_map/ppermute | solution.py:21
  97.2 11.5 %collective-permute-start.23 = (bf16[32,2048]{1,0:T(8,128)(2,1)S(1)}, bf16[32,2048]{1,0:T(8,128)(2,1)S(1)}, u32[]{:S(2)}, u32[]{:S(2)}) collective-permute-start(bf16[32,2048]{1,0:T(8,128)(2,1)S(1)} %get-tuple-element.124.refs_0_), channel_id=1, source_target_pairs={{0,12},{4,8},{8,4},{12,0},{1,13},{5,9},{9,5},{13,1},{2,14},{6,10},... | collective-permute-start | bytes 393224 | tf_op jit(solution)/shard_map/ppermute | solution.py:21
  108.7 14.0 %collective-permute-start.28 = (bf16[32,2048]{1,0:T(8,128)(2,1)S(1)}, bf16[32,2048]{1,0:T(8,128)(2,1)S(1)}, u32[]{:S(2)}, u32[]{:S(2)}) collective-permute-start(bf16[32,2048]{1,0:T(8,128)(2,1)S(1)} %get-tuple-element.124.refs_0_), channel_id=1, source_target_pairs={{0,2},{1,3},{2,0},{3,1},{4,6},{5,7},{6,4},{7,5},{8,10},{9,11},{10,... | collective-permute-start | bytes 393224 | tf_op jit(solution)/shard_map/ppermute | solution.py:21
  109.8 13.0 %collective-permute-start.29 = (bf16[32,2048]{1,0:T(8,128)(2,1)S(1)}, bf16[32,2048]{1,0:T(8,128)(2,1)S(1)}, u32[]{:S(2)}, u32[]{:S(2)}) collective-permute-start(bf16[32,2048]{1,0:T(8,128)(2,1)S(1)} %collective-permute-done.21.refs_4_), channel_id=1, source_target_pairs={{0,2},{1,3},{2,0},{3,1},{4,6},{5,7},{6,4},{7,5},{8,10},{9,11},{10,... | collective-permute-start | bytes 393224 | tf_op jit(solution)/shard_map/ppermute | solution.py:21
  110.8 12.0 %collective-permute-start.30 = (bf16[32,2048]{1,0:T(8,128)(2,1)S(1)}, bf16[32,2048]{1,0:T(8,128)(2,1)S(1)}, u32[]{:S(2)}, u32[]{:S(2)}) collective-permute-start(bf16[32,2048]{1,0:T(8,128)(2,1)S(1)} %collective-permute-done.22.refs_8_), channel_id=1, source_target_pairs={{0,2},{1,3},{2,0},{3,1},{4,6},{5,7},{6,4},{7,5},{8,10},{9,11},{10,... | collective-permute-start | bytes 393224 | tf_op jit(solution)/shard_map/ppermute | solution.py:21
  111.8 11.0 %collective-permute-start.31 = (bf16[32,2048]{1,0:T(8,128)(2,1)S(1)}, bf16[32,2048]{1,0:T(8,128)(2,1)S(1)}, u32[]{:S(2)}, u32[]{:S(2)}) collective-permute-start(bf16[32,2048]{1,0:T(8,128)(2,1)S(1)} %collective-permute-done.23.refs_12_), channel_id=1, source_target_pairs={{0,2},{1,3},{2,0},{3,1},{4,6},{5,7},{6,4},{7,5},{8,10},{9,11},{10,... | collective-permute-start | bytes 393224 | tf_op jit(solution)/shard_map/ppermute | solution.py:21
  125.1 19.4 %collective-permute-start.42 = (bf16[128,2048]{1,0:T(8,128)(2,1)S(1)}, bf16[128,2048]{1,0:T(8,128)(2,1)}, u32[]{:S(2)}, u32[]{:S(2)}) collective-permute-start(bf16[128,2048]{1,0:T(8,128)(2,1)S(1)} %collective-permute-done.24.refs_2_), channel_id=1, source_target_pairs={{0,2},{1,3},{2,0},{3,1},{4,6},{5,7},{6,4},{7,5},{8,10},{9,11},{10,... | collective-permute-start | bytes 1572872 | tf_op jit(solution)/shard_map/ppermute | solution.py:21
  143.9 4.3 %collective-permute-start.45 = (bf16[128,2048]{1,0:T(8,128)(2,1)S(1)}, bf16[128,2048]{1,0:T(8,128)(2,1)S(1)}, u32[]{:S(2)}, u32[]{:S(2)}) collective-permute-start(bf16[128,2048]{1,0:T(8,128)(2,1)S(1)} %collective-permute-done.24.refs_2_), channel_id=1, source_target_pairs={{0,1},{1,0},{2,3},{3,2},{4,5},{5,4},{6,7},{7,6},{8,9},{9,8},{10,11... | collective-permute-start | bytes 1572872 | tf_op jit(solution)/shard_map/ppermute | solution.py:21
  144.4 34.6 %collective-permute-start.49 = (bf16[4,256,512]{2,1,0:T(8,128)(2,1)}, bf16[4,256,512]{2,1,0:T(8,128)(2,1)S(1)}, u32[]{:S(2)}, u32[]{:S(2)}) collective-permute-start(bf16[4,256,512]{2,1,0:T(8,128)(2,1)} %bitcast.46), channel_id=1, source_target_pairs={{0,16},{16,0},{1,17},{17,1},{2,18},{18,2},{3,19},{19,3},{4,20},{20... | collective-permute-start | bytes 3145736 | tf_op jit(solution)/shard_map/ppermute | solution.py:26
  147.1 30.3 %collective-permute-start.41 = (bf16[32,4096]{1,0:T(8,128)(2,1)S(1)}, bf16[32,4096]{1,0:T(8,128)(2,1)S(1)}, u32[]{:S(2)}, u32[]{:S(2)}) collective-permute-start(bf16[32,4096]{1,0:T(8,128)(2,1)S(1)} %slice.203), channel_id=1, source_target_pairs={{0,2},{1,3},{2,0},{3,1},{4,6},{5,7},{6,4},{7,5},{8,10},{9,11},{10,... | collective-permute-start | bytes 786440 | tf_op jit(solution)/shard_map/ppermute | solution.py:21
  178.0 8.5 %collective-permute-start.47 = (bf16[32,4096]{1,0:T(8,128)(2,1)S(1)}, bf16[32,4096]{1,0:T(8,128)(2,1)S(1)}, u32[]{:S(2)}, u32[]{:S(2)}) collective-permute-start(bf16[32,4096]{1,0:T(8,128)(2,1)S(1)} %get-tuple-element.198), channel_id=1, source_target_pairs={{0,2},{1,3},{2,0},{3,1},{4,6},{5,7},{6,4},{7,5},{8,10},{9,11},{10,... | collective-permute-start | bytes 786440 | tf_op jit(solution)/shard_map/ppermute | solution.py:21
  181.9 4.7 %collective-permute-start.50 = (f32[2,256]{1,0:T(2,128)S(1)}, f32[2,256]{1,0:T(2,128)S(1)}, u32[]{:S(2)}, u32[]{:S(2)}) collective-permute-start(f32[2,256]{1,0:T(2,128)S(1)} %pad_maximum_fusion.4), channel_id=1, source_target_pairs={{0,2},{1,3},{2,0},{3,1},{4,6},{5,7},{6,4},{7,5},{8,10},{9,11},{10,... | collective-permute-start | bytes 6152 | tf_op jit(solution)/shard_map/ppermute | solution.py:21
  (69 other events, 431.0 us)
Sparse Core Ops, SparseCore 0:
  16.1 43.9 all-gather.1
